TPU v7x, 256 devices: a whole 4x4x8 slice. The times are simulated.
256 devices in a mesh: gx: 16 (over y, x), gy: 8 (over z), gz: 2 (over core).
Axes of the slice: x: 4, y: 4, z: 8, core: 2. Of those that a mesh axis runs over, the one named last changes fastest.
Arguments:
- era5_columns: float32 [128, 1024, 256], P(('gx', 'gy'), None, 'gz'), may hold values from -6 to 6
- column_owner: int32 [128, 1024], P(('gx', 'gy')), may hold values from 0 to 127, as said below
- live_counts: int32 [128], P(('gx', 'gy')), may hold values from 135 to 1024, as said below
- vertical_weights: float32 [32, 32], P('gz'), may hold values from -1 to 1
- stencil_index: int32 [4, 512, 2048], P(None, 'gx', 'gy'), may hold values from 0 to 1023, as said below
- stencil_weight: float32 [4, 512, 2048], P(None, 'gx', 'gy'), may hold values from 0.1 to 1
- terrain_mask: int32 [32, 512, 2048], P('gz', 'gx', 'gy'), may hold values from 0 to 1, as said below
- fuel_start: float32 [3, 512, 2048], P(None, 'gx', 'gy'), may hold values from 0.5 to 3
Outputs:
- potential: float32 [32, 512, 2048], P('gz', 'gx', 'gy')
- wind_field: float32 [3, 32, 512, 2048], P(None, 'gz', 'gx', 'gy')
- fuel_moisture: float32 [3, 512, 2048], P(None, 'gx', 'gy')
Inputs may be any that keep to these rules, and one draw needn't show every extreme that they name: `column_owner`: among the first live_counts entries of a device's row, each tile appears at least once and at most 8 times, and one tile, the same for every device, appears exactly 8 times in every row; entries after the live ones carry no meaning. A device's live ERA5 column rows are its first live_counts rows. `stencil_index`: each entry names a row s * 8 + k of the block that its grid column's tile receives, with k below the number of live rows that device s holds for that tile. `terrain_mask`: in each grid column the terrain cells are the lowest ones, at most 16 of them.
All inputs are finite; a program needn't handle non-finite values.
Results may differ from a plain program's by a relative error of at most 0.0003.
Values sent between devices are 32-bit elements; how exact they have to be, the bound alone decides.
No kernel may reach another device: no remote copies, remote signals or barrier semaphores. Data moves between devices by JAX's collectives and lax.ppermute only.
A program may use at most 64 MiB of HBM per device.

v0:
```python
import math

import jax
import jax.numpy as jnp
from jax import lax
from jax.sharding import PartitionSpec as P

ITERS = 3
PASSES = 4


drying_lags = (1.0, 10.0, 100.0)


def padded_2(block, sides, width):
    for axis, dim in sides:
        count = lax.axis_size(axis)
        forward = [(i, i + 1) for i in range(count - 1)]
        backward = [(target, source) for source, target in forward]
        low = lax.ppermute(
            lax.slice_in_dim(block, block.shape[dim] - width, None, axis=dim), axis, forward
        )
        high = lax.ppermute(lax.slice_in_dim(block, 0, width, axis=dim), axis, backward)
        block = jnp.concatenate([low, block, high], axis=dim)
    return block


def smooth_box(padded):
    along_z = 0.5 * padded[:-2] + padded[1:-1] + 0.5 * padded[2:]
    along_x = 0.5 * along_z[:, :-2] + along_z[:, 1:-1] + 0.5 * along_z[:, 2:]
    return 0.5 * along_x[:, :, :-2] + along_x[:, :, 1:-1] + 0.5 * along_x[:, :, 2:]


def extend(field_in):
    return padded_2(field_in, (("gx", 1), ("gy", 2), ("gz", 0)), 1)


def operate(field_in, air_mask):
    masked = air_mask * field_in
    nearby = smooth_box(extend(masked))
    return air_mask * (16.0 * masked - 2.0 * nearby) + (1.0 - air_mask) * field_in


def residual_dot(residual, precond):
    return lax.psum(jnp.sum(residual * precond), ("gx", "gy", "gz"))


def shards(
    era5_columns,
    column_owner,
    live_counts,
    vertical_weights,
    stencil_index,
    stencil_weight,
    terrain_mask,
    fuel_start,
):
    tile_count = lax.axis_size(("gx", "gy"))
    column_count = column_owner.shape[1]
    capacity = column_count // tile_count
    feature_count = era5_columns.shape[2]
    level_count = vertical_weights.shape[1]
    field_count = feature_count // level_count
    layer_count = vertical_weights.shape[0]
    slot_total = tile_count * capacity
    owners = column_owner[0]
    is_live = jnp.arange(column_count, dtype=jnp.int32) < live_counts[0]
    onehot = (
        (owners[:, None] == jnp.arange(tile_count, dtype=jnp.int32)[None, :]) & is_live[:, None]
    ).astype(jnp.int32)
    before = jnp.cumsum(onehot, axis=0) - onehot
    slot_rank = jnp.sum(before * onehot, axis=1)
    target = jnp.where(is_live, owners * capacity + slot_rank, slot_total)
    outgoing = (
        jnp.zeros((slot_total, feature_count), jnp.float32)
        .at[target]
        .set(era5_columns[0], mode="drop")
    )
    payload_width = outgoing.shape[1]
    incoming = lax.all_to_all(
        outgoing.reshape(tile_count, capacity, payload_width),
        ("gx", "gy"),
        split_axis=0,
        concat_axis=0,
        tiled=True,
    )
    incoming = incoming.reshape(slot_total, field_count, level_count)
    profile = jnp.einsum("sce,ze->czs", incoming, vertical_weights, precision=lax.Precision.HIGHEST)
    profile = profile.reshape(field_count * layer_count, slot_total)
    points, rows_x, rows_y = stencil_index.shape
    indices = stencil_index.reshape(points, rows_x * rows_y)
    weights = stencil_weight.reshape(points, rows_x * rows_y)
    weights = weights / jnp.sum(weights, axis=0)
    picked = jnp.take(profile, indices, axis=1)
    gridded_quantities = jnp.sum(picked * weights[None], axis=1).reshape(
        field_count, layer_count, rows_x, rows_y
    )
    zonal_velocity, meridional_velocity, kelvin_reading, saturation_percent = (
        gridded_quantities[0],
        gridded_quantities[1],
        gridded_quantities[2],
        gridded_quantities[3],
    )
    air_mask = terrain_mask.astype(jnp.float32)
    framed = padded_2(jnp.stack([zonal_velocity, meridional_velocity]), (("gx", 2), ("gy", 3)), 1)
    divergence = 0.5 * (framed[0, :, 2:, 1:-1] - framed[0, :, :-2, 1:-1]) + 0.5 * (
        framed[1, :, 1:-1, 2:] - framed[1, :, 1:-1, :-2]
    )
    source = air_mask * divergence
    scaling = 14.0 * air_mask + (1.0 - air_mask)
    potential = jnp.zeros_like(source)
    residual = source
    precond = residual / scaling
    direction = precond
    current = residual_dot(residual, precond)
    for iteration in range(ITERS):
        applied = operate(direction, air_mask)
        alpha_step = current / lax.psum(jnp.sum(direction * applied), ("gx", "gy", "gz"))
        potential = potential + alpha_step * direction
        residual = residual - alpha_step * applied
        if iteration + 1 < ITERS:
            precond = residual / scaling
            updated = residual_dot(residual, precond)
            direction = precond + updated / current * direction
            current = updated
    padded = extend(air_mask * potential)
    slope_east = 0.5 * (padded[1:-1, 2:, 1:-1] - padded[1:-1, :-2, 1:-1])
    slope_north = 0.5 * (padded[1:-1, 1:-1, 2:] - padded[1:-1, 1:-1, :-2])
    slope_up = 0.5 * (padded[2:, 1:-1, 1:-1] - padded[:-2, 1:-1, 1:-1])
    wind_field = jnp.stack(
        [
            air_mask * (zonal_velocity + slope_east),
            air_mask * (meridional_velocity + slope_north),
            air_mask * slope_up,
        ]
    )
    flow_speed_norm = jnp.sqrt(jnp.sum(wind_field * wind_field, axis=0))
    layer_sums = jnp.stack(
        [
            jnp.sum(flow_speed_norm, axis=0),
            jnp.sum(kelvin_reading, axis=0),
            jnp.sum(saturation_percent, axis=0),
        ]
    )
    column_totals = lax.psum(layer_sums, "gz")
    profile_means = column_totals / (layer_count * lax.axis_size("gz"))
    speed_mean, temp_mean, humid_mean = (profile_means[0], profile_means[1], profile_means[2])
    balance = 1.2 + 0.5 * jnp.tanh(humid_mean) - 0.3 * jnp.tanh(temp_mean)
    lag_table = jnp.asarray(drying_lags, jnp.float32)[:, None, None]
    decay_rate = jnp.exp(-(1.0 + 0.5 * speed_mean)[None] / lag_table)
    fuel_moisture = fuel_start
    for sweep_no in range(PASSES):
        goal_now = balance + 0.3 * math.cos(2.0 * math.pi * sweep_no / 24.0)
        fuel_moisture = goal_now + (fuel_moisture - goal_now) * decay_rate
    return (potential, wind_field, fuel_moisture)


def solution(mesh):
    placed = (
        P(("gx", "gy"), None, "gz"),
        P(("gx", "gy"), None),
        P(("gx", "gy")),
        P("gz", None),
        P(None, "gx", "gy"),
        P(None, "gx", "gy"),
        P("gz", "gx", "gy"),
        P(None, "gx", "gy"),
    )
    return jax.shard_map(
        shards,
        mesh=mesh,
        in_specs=placed,
        out_specs=(P("gz", "gx", "gy"), P(None, "gz", "gx", "gy"), P(None, "gx", "gy")),
        check_vma=False,
    )
```

profile of v0, /device:TPU:1, one launch (start us, length us, event | category | flops | bytes accessed | tf_op | source)
XLA Modules:
  0.0 751.9 jit_solution(10836665932382594732)
XLA Ops:
  9.9 3.9 scatter_custom_fusion
  13.8 16.3 %all-to-all-start = ((f32[128,8,128]{2,1,0:T(8,128)}), f32[128,8,128]{2,1,0:T(8,128)S(1)}, u32[]{:S(2)}, u32[]{:S(2)}) async-start(f32[128,8,128]{2,1,0:T(8,128)} %bitcast.10), calls=%async_computation | async-start | bytes 1048576 | tf_op jit(solution)/shard_map/all_to_all | solution.py:80
  30.7 18.5 %all-to-all-done = f32[128,8,128]{2,1,0:T(8,128)S(1)} async-done(((f32[128,8,128]{2,1,0:T(8,128)}), f32[128,8,128]{2,1,0:T(8,128)S(1)}, u32[]{:S(2)}, u32[]{:S(2)}) %all-to-all-start) | async-done | bytes 524320 | tf_op jit(solution)/shard_map/all_to_all | solution.py:80
  52.3 108.5 %gather_fusion = f32[32768,64]{1,0:T(8,128)} fusion(f32[64,1024]{0,1:T(8,128)S(1)} %copy.234, s32[32768]{0:T(1024)S(1)} %broadcast_clamp_fusion), kind=kCustom, calls=%fused_computation | custom fusion | bytes 16908288 | tf_op jit(solution)/shard_map/jit(_take)/gather | solution.py:94
  160.8 12.8 %multiply_reduce_fusion = f32[8192,64]{1,0:T(8,128)S(1)} fusion(f32[4,8192,64]{2,1,0:T(8,128)} %bitcast.72, f32[4,8192]{1,0:T(4,128)S(1)} %broadcast_divide_fusion, pred[4,8192]{1,0:T(4,128)(4,1)S(1)} %compare_and_fusion), kind=kLoop, calls=%fused_computation.2 | loop fusion | flops 5767168 | bytes 10649600 | tf_op jit(solution)/shard_map/reduce_sum | solution.py:95
  173.6 7.7 %slice_reduce_fusion.1 = (f32[8192]{0:T(1024)S(1)}, f32[8192]{0:T(1024)S(1)}, f32[16,8192]{0,1:T(8,128)}, f32[16,8192]{0,1:T(8,128)}) fusion(f32[64,8192]{0,1:T(8,128)S(1)} %bitcast.71), kind=kLoop, calls=%fused_computation.4 | loop fusion | flops 245760 | bytes 3211264 | tf_op jit(solution)/shard_map/reduce_sum | solution.py:141
  184.1 2.8 copy.236
  189.7 3.2 collective-permute-done
  195.2 4.0 collective-permute-start.3
  204.1 3.2 collective-permute-done.5
  207.4 3.6 collective-permute-start.6
  214.5 3.8 collective-permute-done.7
  220.1 10.3 %collective-permute-start.9 = (f32[1,34,258]{2,0,1:T(1,128)S(1)}, f32[1,34,258]{2,0,1:T(1,128)S(1)}, u32[]{:S(2)}, u32[]{:S(2)}) collective-permute-start(f32[1,34,258]{2,0,1:T(1,128)S(1)} %get-tuple-element.57), channel_id=1, source_target_pairs={{1,0},{3,2},{5,4},{7,6},{9,8},{11,10},{13,12},{15,14},{17,16},{19,... | collective-permute-start | bytes 105272 | tf_op jit(solution)/shard_map/ppermute | solution.py:23
  233.5 80.3 %all-reduce = (f32[]{:T(128)}, f32[]{:T(128)}) all-reduce(f32[]{:T(128)} %get-tuple-element.24, f32[]{:T(128)} %get-tuple-element.23), channel_id=1, replica_groups=mesh['gx'=16,'gy'=8,'gz'=2] {'gx','gy','gz'}, use_global_device_ids=true, to_apply=%region_7.8 | all-reduce | flops 2 | bytes 16 | tf_op jit(solution)/shard_map/psum | solution.py:45
  316.2 72.8 %psum.51 = f32[]{:T(128)} all-reduce(f32[]{:T(128)} %get-tuple-element.37), channel_id=1, replica_groups=mesh['gx'=16,'gy'=8,'gz'=2] {'gx','gy','gz'}, use_global_device_ids=true, to_apply=%region_11.12 | all-reduce | flops 1 | bytes 8 | tf_op jit(solution)/shard_map/psum | solution.py:45
  390.7 2.8 collective-permute-start.10
  394.8 3.2 collective-permute-done.11
  398.2 3.7 collective-permute-start.12
  405.7 3.8 collective-permute-done.13
  411.3 5.2 collective-permute-start.15
  419.6 76.7 %psum.52 = f32[]{:T(128)} all-reduce(f32[]{:T(128)} %get-tuple-element.33), channel_id=1, replica_groups=mesh['gx'=16,'gy'=8,'gz'=2] {'gx','gy','gz'}, use_global_device_ids=true, to_apply=%region_13.14 | all-reduce | flops 1 | bytes 8 | tf_op jit(solution)/shard_map/psum | solution.py:118
  498.6 73.6 %psum.53 = f32[]{:T(128)} all-reduce(f32[]{:T(128)} %get-tuple-element.31), channel_id=1, replica_groups=mesh['gx'=16,'gy'=8,'gz'=2] {'gx','gy','gz'}, use_global_device_ids=true, to_apply=%region_15.16 | all-reduce | flops 1 | bytes 8 | tf_op jit(solution)/shard_map/psum | solution.py:45
  573.9 3.0 collective-permute-start.16
  578.3 3.2 collective-permute-done.17
  581.6 3.7 collective-permute-start.18
  589.1 3.8 collective-permute-done.19
  594.7 5.2 collective-permute-start.21
  603.0 76.7 %psum.54 = f32[]{:T(128)} all-reduce(f32[]{:T(128)} %fusion.37), channel_id=1, replica_groups=mesh['gx'=16,'gy'=8,'gz'=2] {'gx','gy','gz'}, use_global_device_ids=true, to_apply=%region_17.18 | all-reduce | flops 1 | bytes 8 | tf_op jit(solution)/shard_map/psum | solution.py:118
  683.6 4.0 collective-permute-start.23
  689.9 4.0 collective-permute-start.25
  699.9 4.3 collective-permute-start.26
  714.3 29.1 %all-reduce.3.cloned.1.call-done = f32[3,32,256]{2,1,0:T(8,128)} async-done(((f32[3,32,256]{2,1,0:T(8,128)}), f32[3,32,256]{2,1,0:T(8,128)}) %all-reduce.3.cloned.1.call-update) | async-done | bytes 98320 | tf_op jit(solution)/shard_map/psum | solution.py:145
  (146 shorter events, 71.9 us)
Async XLA Ops:
  13.8 35.5 %all-to-all-start = ((f32[128,8,128]{2,1,0:T(8,128)}), f32[128,8,128]{2,1,0:T(8,128)S(1)}, u32[]{:S(2)}, u32[]{:S(2)}) async-start(f32[128,8,128]{2,1,0:T(8,128)} %bitcast.10), calls=%async_computation | async-start | bytes 1048576 | tf_op jit(solution)/shard_map/all_to_all | solution.py:80
  30.1 713.3 %all-reduce.3.cloned.1.call-start = ((), (), s32[]{:S(2)}) async-start(), calls=%async_computation.1 | async-start | bytes 196608 | tf_op jit(solution)/shard_map/psum | solution.py:145
  186.9 2.8 collective-permute-start.1
  188.2 4.7 collective-permute-start
  193.5 5.6 collective-permute-start.2
  195.2 4.8 collective-permute-start.3
  200.9 3.2 collective-permute-start.4
  202.8 4.5 collective-permute-start.5
  207.4 7.1 collective-permute-start.6
  211.1 7.3 collective-permute-start.7
  218.8 11.6 %collective-permute-start.8 = (f32[1,34,258]{2,0,1:T(1,128)S(1)}, f32[1,34,258]{2,0,1:T(1,128)S(1)}, u32[]{:S(2)}, u32[]{:S(2)}) collective-permute-start(f32[1,34,258]{2,0,1:T(1,128)S(1)} %get-tuple-element.56), channel_id=1, source_target_pairs={{0,1},{2,3},{4,5},{6,7},{8,9},{10,11},{12,13},{14,15},{16,17},{18,... | collective-permute-start | bytes 105272 | tf_op jit(solution)/shard_map/ppermute | solution.py:20
  220.1 11.1 %collective-permute-start.9 = (f32[1,34,258]{2,0,1:T(1,128)S(1)}, f32[1,34,258]{2,0,1:T(1,128)S(1)}, u32[]{:S(2)}, u32[]{:S(2)}) collective-permute-start(f32[1,34,258]{2,0,1:T(1,128)S(1)} %get-tuple-element.57), channel_id=1, source_target_pairs={{1,0},{3,2},{5,4},{7,6},{9,8},{11,10},{13,12},{15,14},{17,16},{19,... | collective-permute-start | bytes 105272 | tf_op jit(solution)/shard_map/ppermute | solution.py:23
  390.7 4.1 collective-permute-start.10
  393.5 4.5 collective-permute-start.11
  398.2 7.5 %collective-permute-start.12 = (f32[16,34,1]{2,0,1:T(8,128)S(1)}, f32[16,34,1]{2,0,1:T(8,128)S(1)}, u32[]{:S(2)}, u32[]{:S(2)}) collective-permute-start(f32[16,34,1]{2,0,1:T(8,128)S(1)} %get-tuple-element.62), channel_id=1, source_target_pairs={{0,2},{2,4},{4,6},{6,8},{8,10},{10,12},{12,14},{1,3},{3,5},{5,7},{... | collective-permute-start | bytes 6536 | tf_op jit(solution)/shard_map/ppermute | solution.py:20
  401.9 7.7 %collective-permute-start.13 = (f32[16,34,1]{2,0,1:T(8,128)S(1)}, f32[16,34,1]{2,0,1:T(8,128)S(1)}, u32[]{:S(2)}, u32[]{:S(2)}) collective-permute-start(f32[16,34,1]{2,0,1:T(8,128)S(1)} %get-tuple-element.63), channel_id=1, source_target_pairs={{2,0},{4,2},{6,4},{8,6},{10,8},{12,10},{14,12},{3,1},{5,3},{7,5},{... | collective-permute-start | bytes 6536 | tf_op jit(solution)/shard_map/ppermute | solution.py:23
  410.0 6.5 collective-permute-start.14
  411.3 6.1 collective-permute-start.15
  573.9 4.3 collective-permute-start.16
  576.9 4.5 collective-permute-start.17
  581.6 7.5 %collective-permute-start.18 = (f32[16,34,1]{2,0,1:T(8,128)S(1)}, f32[16,34,1]{2,0,1:T(8,128)S(1)}, u32[]{:S(2)}, u32[]{:S(2)}) collective-permute-start(f32[16,34,1]{2,0,1:T(8,128)S(1)} %get-tuple-element.60), channel_id=1, source_target_pairs={{0,2},{2,4},{4,6},{6,8},{8,10},{10,12},{12,14},{1,3},{3,5},{5,7},{... | collective-permute-start | bytes 6536 | tf_op jit(solution)/shard_map/ppermute | solution.py:20
  585.3 7.7 %collective-permute-start.19 = (f32[16,34,1]{2,0,1:T(8,128)S(1)}, f32[16,34,1]{2,0,1:T(8,128)S(1)}, u32[]{:S(2)}, u32[]{:S(2)}) collective-permute-start(f32[16,34,1]{2,0,1:T(8,128)S(1)} %get-tuple-element.61), channel_id=1, source_target_pairs={{2,0},{4,2},{6,4},{8,6},{10,8},{12,10},{14,12},{3,1},{5,3},{7,5},{... | collective-permute-start | bytes 6536 | tf_op jit(solution)/shard_map/ppermute | solution.py:23
  593.4 6.5 collective-permute-start.20
  594.7 6.1 collective-permute-start.21
  682.3 5.3 collective-permute-start.22
  683.6 4.8 collective-permute-start.23
  688.6 10.9 %collective-permute-start.24 = (f32[16,34,1]{2,0,1:T(8,128)S(1)}, f32[16,34,1]{2,0,1:T(8,128)S(1)}, u32[]{:S(2)}, u32[]{:S(2)}) collective-permute-start(f32[16,34,1]{2,0,1:T(8,128)S(1)} %get-tuple-element.58), channel_id=1, source_target_pairs={{2,0},{4,2},{6,4},{8,6},{10,8},{12,10},{14,12},{3,1},{5,3},{7,5},{... | collective-permute-start | bytes 6536 | tf_op jit(solution)/shard_map/ppermute | solution.py:23
  689.9 9.7 %collective-permute-start.25 = (f32[16,34,1]{2,0,1:T(8,128)S(1)}, f32[16,34,1]{2,0,1:T(8,128)S(1)}, u32[]{:S(2)}, u32[]{:S(2)}) collective-permute-start(f32[16,34,1]{2,0,1:T(8,128)S(1)} %get-tuple-element.59), channel_id=1, source_target_pairs={{0,2},{2,4},{4,6},{6,8},{8,10},{10,12},{12,14},{1,3},{3,5},{5,7},{... | collective-permute-start | bytes 6536 | tf_op jit(solution)/shard_map/ppermute | solution.py:20
  699.9 6.0 collective-permute-start.26
  704.2 3.1 collective-permute-start.27
  710.2 34.9 %copy-start.1 = (f32[1,1024,128]{2,1,0:T(8,128)S(1)}, f32[1,1024,128]{2,1,0:T(8,128)}, u32[]{:S(2)}) copy-start(f32[1,1024,128]{2,1,0:T(8,128)} %param.9) | copy-start | bytes 1572868
  711.6 32.8 %copy-start.7 = (f32[3,32,256]{2,1,0:T(8,128)S(1)}, f32[3,32,256]{2,1,0:T(8,128)}, u32[]{:S(2)}) copy-start(f32[3,32,256]{2,1,0:T(8,128)} %param.16) | copy-start | bytes 294916
  (9 other events, 109.6 us)
Sparse Core Ops, SparseCore 0:
  713.3 30.0 all-reduce.2
where the time goes:
time: 754 us; the launch traced here: 752 us
  blocking collectives  380 us (50%)
  local copies, waits for them, and re-layouts  133 us (18%)
  starting transfers between devices  91.5 us (12%)
  waiting for transfers between devices  84.3 us (11%)
  other arithmetic  38.9 us (5%)
  between operations  22.3 us (3%)
    psum x3, blocking collectives, residual_dot(): return lax.psum(jnp.sum(residual * precond), ('gx', 'gy', 'gz'))  227 us
    psum x2, blocking collectives, shards(): lax.psum(jnp.sum(direction * applied), ('gx', 'gy', 'gz'))  153 us
    gather x1, local copies, waits for them, and re-layouts, shards(): picked = jnp.take(profile, indices, axis=1)  108 us
    ppermute x14, starting transfers between devices, padded_2(): lax.ppermute(lax.slice_in_dim(block, 0, width, axis=dim), axis, backward)  38 us
    ppermute x14, starting transfers between devices, padded_2(): lax.ppermute(lax.slice_in_dim(block, block.shape[dim] - width, None, axis...  37.2 us
    psum x1, waiting for transfers between devices, shards(): column_totals = lax.psum(layer_sums, 'gz')  29.1 us
    ppermute x14, waiting for transfers between devices, padded_2(): lax.ppermute(lax.slice_in_dim(block, 0, width, axis=dim), axis, backward)  26.8 us
    all_to_all x1, waiting for transfers between devices, shards(): lax.all_to_all(outgoing.reshape(tile_count, capacity, payload_width), ('g...  18.5 us
  transfers between devices with their start and end apart: 30, of which 18 were waited for; matrix products, arithmetic and copies ran while one was open for 1% of the time, Pallas kernels for 0%

commit v1 on v0

v1 whole, which is shorter than its diff:
```python
import functools
import math

import jax
import jax.numpy as jnp
from jax import lax
from jax.experimental import pallas as pl
from jax.experimental.pallas import tpu as pltpu
from jax.sharding import PartitionSpec as P

F32 = jnp.float32
BF16 = jnp.bfloat16
PASSES = 4
LAGS = (1.0, 10.0, 100.0)

LZ = 16
DEEP = 3
NF = 40
NS = NF + LZ
XR = 40
YR = 384
VMEM = 56 * 1024 * 1024


def params():
    return pltpu.CompilerParams(vmem_limit_bytes=VMEM)


def split(value):
    high = value.astype(BF16)
    return high, (value - high.astype(F32)).astype(BF16)


def dot_nt(a, b):
    return lax.dot_general(a, b, (((1,), (1,)), ((), ())), preferred_element_type=F32)


def profile_kernel(weights_ref, columns_ref, own_ref, send_ref):
    w_high, w_low = split(weights_ref[...])
    c_high, c_low = split(columns_ref[...])
    result = dot_nt(w_high, c_high) + dot_nt(w_high, c_low) + dot_nt(w_low, c_high)
    own_ref[...] = result[:NF]
    send_ref[...] = result[NF:]


def route_kernel(live_ref, owner_ref, own_ref, other_ref, out_ref, *, tiles, capacity):
    rows = owner_ref.shape[1]
    slots = out_ref.shape[0]
    position = lax.broadcasted_iota(jnp.int32, (1, rows), 1)
    owner = jnp.where(position < live_ref[0], owner_ref[...], -1)
    matches = lax.broadcasted_iota(jnp.int32, (tiles, rows), 0) == owner
    hits = jnp.where(matches, 1.0, 0.0)
    earlier = lax.broadcasted_iota(jnp.int32, (rows, rows), 0) < lax.broadcasted_iota(
        jnp.int32, (rows, rows), 1
    )
    before = jnp.dot(
        hits.astype(BF16), jnp.where(earlier, 1.0, 0.0).astype(BF16), preferred_element_type=F32
    )
    rank = jnp.sum(hits * before, axis=0, keepdims=True).astype(jnp.int32)
    target = jnp.where(owner >= 0, owner * capacity + rank, -1)
    place = lax.broadcasted_iota(jnp.int32, (slots, rows), 0) == target
    profile = jnp.concatenate([own_ref[: NF - 8], own_ref[NF - 8 :] + other_ref[...]], axis=0)
    high, low = split(profile)
    pad = jnp.zeros((64 - NF, rows), BF16)
    both = jnp.concatenate([high, pad, low, pad], axis=0)
    out_ref[...] = dot_nt(jnp.where(place, 1.0, 0.0).astype(BF16), both)


def lane_pick(table, lanes):
    return jnp.take_along_axis(table, lanes, axis=1)


def pick_columns(table_ref, index, weight, blocks):
    total = weight[0] + weight[1] + weight[2] + weight[3]
    acc = [None] * (NF // 8)
    for point in range(len(index)):
        lanes = jnp.broadcast_to(index[point] & 127, (8, 128))
        part = jnp.broadcast_to(index[point] >> 7, (8, 128))
        share = jnp.broadcast_to(weight[point] / total, (8, 128))
        masks = [part == b for b in range(1, blocks)]
        for g in range(NF // 8):
            value = lane_pick(table_ref[0, 8 * g : 8 * g + 8], lanes)
            for b in range(1, blocks):
                other = lane_pick(table_ref[b, 8 * g : 8 * g + 8], lanes)
                value = jnp.where(masks[b - 1], other, value)
            term = value * share
            acc[g] = term if acc[g] is None else acc[g] + term
    return acc


def gather_kernel(
    block_ref, received_ref, index_ref, weight_ref, mask_ref, far_mask_ref,
    grid_ref, low_y_ref, high_y_ref, low_x_ref, high_x_ref,
    table_ref, index_y_ref, weight_y_ref, mask_f_ref, *, blocks
):
    lower = block_ref[2] == 0
    points, rows, cols = index_ref.shape
    for b in range(blocks):
        turned = jnp.transpose(received_ref[128 * b : 128 * b + 128, :])
        table_ref[b] = turned[:NF] + turned[64 : 64 + NF]

    for h in range(cols // 128):
        at = slice(128 * h, 128 * h + 128)
        near = mask_ref[0 : 8 * rows, at]
        mask_f_ref[h, 0 : 8 * rows] = jnp.where(lower, near, far_mask_ref[:, at]).astype(F32)
        mask_f_ref[h, 8 * rows :] = mask_ref[8 * rows :, at].astype(F32)

    lane = lax.broadcasted_iota(jnp.int32, (1, 128), 1)

    for x in range(rows):
        mine = (lane >> 2) == x
        for side in range(2):
            start = 0 if side == 0 else cols - 128
            turn = (4 * x if side == 0 else 4 * x + 4) % 128
            for k in range(points):
                row = index_ref[k, x : x + 1, start : start + 128]
                row = pltpu.roll(row, turn, 1)
                index_y_ref[side, k] = jnp.where(mine, row, index_y_ref[side, k])
                row = weight_ref[k, x : x + 1, start : start + 128]
                row = pltpu.roll(row, turn, 1)
                weight_y_ref[side, k] = jnp.where(mine, row, weight_y_ref[side, k])
            out = low_y_ref if side == 0 else high_y_ref
            for g in range(LZ // 8):
                value = mask_f_ref[start // 128, pl.ds(x + g * 8 * rows, 8, stride=rows), :]
                at = slice(NF + 8 * g, NF + 8 * g + 8)
                out[at] = jnp.where(mine, pltpu.roll(value, turn, 1), out[at])

    for side, out in ((0, low_y_ref), (1, high_y_ref)):
        got = pick_columns(
            table_ref,
            [index_y_ref[side, k] for k in range(points)],
            [weight_y_ref[side, k] for k in range(points)],
            blocks,
        )
        for g in range(NF // 8):
            out[8 * g : 8 * g + 8] = got[g]

    def group_body(group, carry):
        first = pl.multiple_of(8 * group, 8)
        for h in range(cols // 128):
            at = slice(128 * h, 128 * h + 128)
            index = [index_ref[k, pl.ds(first, 8), at] for k in range(points)]
            weight = [weight_ref[k, pl.ds(first, 8), at] for k in range(points)]
            for j in range(8):
                got = pick_columns(
                    table_ref,
                    [value[j : j + 1] for value in index],
                    [value[j : j + 1] for value in weight],
                    blocks,
                )
                for g in range(NF // 8):
                    grid_ref[h, first + j, 8 * g : 8 * g + 8, :] = got[g]
        return carry

    lax.fori_loop(0, rows // 8, group_body, 0)
    for d in range(4):
        for out, x in ((low_x_ref, d), (high_x_ref, rows - 1 - d)):
            if d < 3:
                for h in range(cols // 128):
                    out[NS * d : NS * d + NF, 128 * h : 128 * h + 128] = grid_ref[h, x]
                for g in range(LZ // 8):
                    at = NS * d + NF + 8 * g
                    for h in range(cols // 128):
                        out[at : at + 8, 128 * h : 128 * h + 128] = mask_f_ref[
                            h, pl.ds(x + g * 8 * rows, 8, stride=rows), :
                        ]
            else:
                for h in range(cols // 128):
                    at = slice(128 * h, 128 * h + 128)
                    out[NS * 3 : NS * 3 + 16, at] = grid_ref[h, x, 0:16]
                    out[NS * 3 + 16 : NS * 3 + 24, at] = grid_ref[h, x, 32:40]


def ring_smooth(plane):
    plane = plane + 0.5 * (pltpu.roll(plane, 1, 0) + pltpu.roll(plane, XR - 1, 0))
    return plane + 0.5 * (pltpu.roll(plane, 1, 1) + pltpu.roll(plane, YR - 1, 1))


def basis_kernel(
    block_ref, grid_ref, mask_ref, far_mask_ref,
    right_ref, left_ref, above_ref, above_corner_ref, below_ref, below_corner_ref,
    basis_ref, moments_ref,
    ext_ref, source_ref, air_ref, last_ref, *, last_gx, last_gy
):
    gx, gy, gz = block_ref[0], block_ref[1], block_ref[2]
    lower = gz == 0
    halves, rows = grid_ref.shape[:2]
    cols = 128 * halves
    lane = lax.broadcasted_iota(jnp.int32, (8, 128), 1)

    def own_row(x, carry):
        for h in range(halves):
            ext_ref[h, pl.ds(pl.multiple_of(x * NS, 8), NF), :] = grid_ref[h, x]
        for g in range(NS // 8):
            at = slice(8 * g, 8 * g + 8)
            right = pltpu.roll(right_ref[at], (128 - 4 * x) & 127, 1)
            left = pltpu.roll(left_ref[at], (124 - 4 * x) & 127, 1)
            side = jnp.where(lane < 4, right, jnp.where(lane >= 124, left, 0.0))
            ext_ref[halves, pl.ds(pl.multiple_of(x * NS + 8 * g, 8), 8), :] = side
        return carry

    lax.fori_loop(0, rows, own_row, 0)
    for d in range(4):
        for near_ref, corner_ref, ring, origin in (
            (above_ref, above_corner_ref, rows + d, d),
            (below_ref, below_corner_ref, XR - 1 - d, rows - 1 - d),
        ):
            base = ring * NS
            for h in range(halves):
                at = slice(128 * h, 128 * h + 128)
                if d < 3:
                    ext_ref[h, base : base + NS] = near_ref[NS * d : NS * d + NS, at]
                else:
                    ext_ref[h, base : base + 16] = near_ref[NS * 3 : NS * 3 + 16, at]
                    ext_ref[h, base + 16 : base + 32] = jnp.zeros((16, 128), F32)
                    ext_ref[h, base + 32 : base + 40] = near_ref[NS * 3 + 16 : NS * 3 + 24, at]
                    ext_ref[h, base + 40 : base + NS] = jnp.zeros((LZ, 128), F32)
            for g in range(NS // 8):
                at = slice(8 * g, 8 * g + 8)
                right = pltpu.roll(corner_ref[at, 0:128], (128 - 4 * origin) % 128, 1)
                left = pltpu.roll(corner_ref[at, 128:256], (124 - 4 * origin) % 128, 1)
                side = jnp.where(lane < 4, right, jnp.where(lane >= 124, left, 0.0))
                ext_ref[halves, base + 8 * g : base + 8 * g + 8] = side

    def source_row(x, carry):
        here = pl.multiple_of(x * NS, 8)
        after = pl.multiple_of(jnp.where(x == XR - 1, 0, x + 1) * NS, 8)
        prior = pl.multiple_of(jnp.where(x == 0, XR - 1, x - 1) * NS, 8)

        def row_of(start, f):
            return jnp.concatenate(
                [ext_ref[h, pl.ds(start + f, 8), :] for h in range(halves + 1)], axis=1
            )

        def east(f):
            return row_of(after, f) - row_of(prior, f)

        def north(f):
            value = row_of(here, f)
            return pltpu.roll(value, YR - 1, 1) - pltpu.roll(value, 1, 1)

        out = pl.multiple_of(x * 24, 8)
        values = (
            0.5 * east(0) + 0.5 * north(16),
            0.5 * east(8) + 0.5 * north(24),
            0.5 * east(32) + 0.5 * pltpu.roll(north(32), 5, 0),
        )
        for g, value in enumerate(values):
            for h in range(halves + 1):
                source_ref[h, pl.ds(out + 8 * g, 8), :] = value[:, 128 * h : 128 * h + 128]
        return carry

    lax.fori_loop(0, XR, source_row, 0)

    row_id = lax.broadcasted_iota(jnp.int32, (XR, YR), 0)
    col_id = lax.broadcasted_iota(jnp.int32, (XR, YR), 1)
    row_in = (row_id < 32) | ((row_id < 36) & (gx < last_gx)) | ((row_id >= 36) & (gx > 0))
    col_in = (
        (col_id < 256) | ((col_id < 260) & (gy < last_gy)) | ((col_id >= 380) & (gy > 0))
    )
    inside = jnp.where(row_in & col_in, 1.0, 0.0)
    for layer in range(LZ + DEEP):
        picked = layer if layer < LZ else 23 - layer
        for group in range(XR // 8):
            for h in range(YR // 128):
                at = slice(128 * h, 128 * h + 128)
                x = slice(8 * group, 8 * group + 8)
                if group < 4 and h < 2:
                    if layer < LZ:
                        known = mask_ref[rows * picked + 8 * group : rows * picked + 8 * group + 8, at]
                    else:
                        known = far_mask_ref[rows * picked + 8 * group : rows * picked + 8 * group + 8, at]
                    known = known.astype(F32)
                else:
                    known = ext_ref[h, pl.ds(8 * group * NS + NF + picked, 8, stride=NS), :]
                full = inside[x, at]
                air = jnp.where(lower, known, full) if layer < LZ else jnp.where(lower, full, known)
                air_ref[layer, x, at] = air
                source = air * source_ref[h, pl.ds(8 * group * 24 + layer, 8, stride=24), :]
                value = source / (14.0 * air + (1.0 - air))
                if layer < LZ + 1:
                    basis_ref[0, layer, x, at] = value
                else:
                    last_ref[0, layer - LZ - 1, x, at] = value

    def read(k, layer):
        if layer < LZ + 1:
            return basis_ref[k, layer]
        return last_ref[k, layer - LZ - 1]

    def advance(k, layer):
        here = read(k, layer)
        beside = read(k, layer + 1)
        if layer > 0:
            beside = beside + read(k, layer - 1)
        return air_ref[layer] * (ring_smooth(here + 0.5 * beside) - here) * (1.0 / 7.0)

    sums = [None] * 6

    def add(at, value):
        value = value[:, 0:128] + value[:, 128:256]
        sums[at] = value if sums[at] is None else sums[at] + value

    for layer in range(LZ + 2):
        value = advance(0, layer)
        if layer < LZ + 1:
            basis_ref[1, layer] = value
        else:
            last_ref[1, layer - LZ - 1] = value
    for layer in range(LZ + 1):
        basis_ref[2, layer] = advance(1, layer)
    for layer in range(LZ):
        third = advance(2, layer)[0:rows, 0:cols]
        first, second, zero = (basis_ref[k, layer, 0:rows, 0:cols] for k in (1, 2, 0))
        air = air_ref[layer, 0:rows, 0:cols]
        scaling = 14.0 * air + (1.0 - air)
        zero_s, first_s, second_s = zero * scaling, first * scaling, second * scaling
        add(0, zero_s * zero)
        add(1, zero_s * first)
        add(2, first_s * first)
        add(3, first_s * second)
        add(4, second_s * second)
        add(5, second_s * third)
    rows_out = [jnp.sum(value, axis=0, keepdims=True) for value in sums]
    moments_ref[...] = jnp.concatenate(rows_out + [jnp.zeros((2, 128), F32)], axis=0)


def iterate(nu):
    def inner(a, b):
        total = None
        for i, left in enumerate(a):
            for j, right in enumerate(b):
                term = left * right * nu[i + j]
                total = term if total is None else total + term
        return total

    one = jnp.ones_like(nu[0])
    precond = [one]
    direction = [one]
    potential = []
    current = nu[0]
    for step in range(3):
        applied = (
            [direction[0]]
            + [direction[i] - direction[i - 1] for i in range(1, len(direction))]
            + [-direction[-1]]
        )
        alpha = current / inner(direction, applied)
        potential = [
            (potential[i] + alpha * d) if i < len(potential) else alpha * d
            for i, d in enumerate(direction)
        ]
        if step < 2:
            precond = [
                (precond[i] - alpha * a) if i < len(precond) else -(alpha * a)
                for i, a in enumerate(applied)
            ]
            updated = inner(precond, precond)
            ratio = updated / current
            direction = [
                (p + ratio * direction[i]) if i < len(direction) else p
                for i, p in enumerate(precond)
            ]
            current = updated
    return potential


def wind_kernel(
    block_ref, moments_ref, basis_ref, grid_ref, mask_ref,
    potential_ref, wind_ref, speed_ref, balance_ref, p_ref
):
    gz = block_ref[2]
    rows, cols = speed_ref.shape
    totals = jnp.sum(moments_ref[...], axis=1, keepdims=True)
    factors = iterate([totals[k : k + 1] for k in range(6)])
    factors = [jnp.broadcast_to(c, (8, 128)) for c in factors]
    factors = [jnp.tile(c, (XR // 8, YR // 128)) for c in factors]

    def combine(layer):
        return (
            factors[0] * basis_ref[0, layer]
            + factors[1] * basis_ref[1, layer]
            + factors[2] * basis_ref[2, layer]
        )

    for layer in range(LZ + 1):
        p_ref[layer] = combine(layer)
    upward = jnp.where(gz == 0, 0.5, -0.5)

    def wind_of(layer, below):
        here = p_ref[layer]
        slope_up = p_ref[layer + 1][0:rows, 0:cols]
        if below:
            slope_up = slope_up - p_ref[layer - 1][0:rows, 0:cols]
        slope_up = upward * slope_up
        slope_east = 0.5 * (pltpu.roll(here, XR - 1, 0) - pltpu.roll(here, 1, 0))[0:rows, 0:cols]
        slope_north = 0.5 * (pltpu.roll(here, YR - 1, 1) - pltpu.roll(here, 1, 1))[0:rows, 0:cols]
        out = jnp.where(gz == 0, layer, LZ - 1 - layer)
        potential_ref[out] = here[0:rows, 0:cols]
        for group in range(rows // 8):
            x = slice(8 * group, 8 * group + 8)
            for h in range(cols // 128):
                at = slice(128 * h, 128 * h + 128)
                east = grid_ref[h, pl.ds(8 * group * NF + layer, 8, stride=NF), :]
                north = grid_ref[h, pl.ds(8 * group * NF + LZ + layer, 8, stride=NF), :]
                air = mask_ref[out, x, at].astype(F32)
                a = air * (east + slope_east[x, at])
                b = air * (north + slope_north[x, at])
                c = air * slope_up[x, at]
                wind_ref[0, out, x, at] = a
                wind_ref[1, out, x, at] = b
                wind_ref[2, out, x, at] = c
                speed = jnp.sqrt(a * a + b * b + c * c)
                if below:
                    speed = speed_ref[x, at] + speed
                speed_ref[x, at] = speed

    for layer in range(LZ):
        wind_of(layer, layer > 0)
    for group in range(rows // 8):
        x = slice(8 * group, 8 * group + 8)
        for h in range(cols // 128):
            at = slice(128 * h, 128 * h + 128)
            temp = grid_ref[h, pl.ds(8 * group * NF + NF - 2, 8, stride=NF), :] / 32.0
            humid = grid_ref[h, pl.ds(8 * group * NF + NF - 1, 8, stride=NF), :] / 32.0
            balance_ref[x, at] = 1.2 + 0.5 * jnp.tanh(humid) - 0.3 * jnp.tanh(temp)


def shifted(block, axis, by):
    count = lax.axis_size(axis)
    pairs = [(i, i + by) for i in range(count) if 0 <= i + by < count]
    return lax.ppermute(block, axis, pairs)


def swapped(block, axis, bit):
    count = lax.axis_size(axis)
    return lax.ppermute(block, axis, [(i, i ^ bit) for i in range(count)])


def shards(
    era5_columns,
    column_owner,
    live_counts,
    vertical_weights,
    stencil_index,
    stencil_weight,
    terrain_mask,
    fuel_start,
):
    gx, gy, gz = (lax.axis_index(a).astype(jnp.int32) for a in ("gx", "gy", "gz"))
    block = jnp.stack([gx, gy, gz])
    tiles = lax.axis_size(("gx", "gy"))
    rows_in = column_owner.shape[1]
    capacity = rows_in // tiles
    slots = tiles * capacity
    blocks = slots // 128
    layers, rows, cols = terrain_mask.shape
    points = stencil_index.shape[0]
    levels = vertical_weights.shape[1]
    vmem = pl.BlockSpec(memory_space=pltpu.VMEM)
    smem = pl.BlockSpec(memory_space=pltpu.SMEM)

    weights = jnp.where(gz == 0, vertical_weights, vertical_weights[::-1])
    total = jnp.sum(vertical_weights, axis=0, keepdims=True)
    edge = weights[: -DEEP - 1 : -1]

    def at_field(value, field):
        return jnp.pad(value, ((0, 0), (field * levels, (3 - field) * levels)))

    rows_of_weights = jnp.concatenate(
        [
            at_field(weights, 0),
            at_field(weights, 1),
            jnp.zeros((2 * DEEP, 4 * levels), F32),
            at_field(total, 2),
            at_field(total, 3),
            at_field(edge, 0),
            at_field(edge, 1),
            at_field(total, 2),
            at_field(total, 3),
        ],
        axis=0,
    )
    own, leaving = pl.pallas_call(
        profile_kernel,
        out_shape=(
            jax.ShapeDtypeStruct((NF, rows_in), F32),
            jax.ShapeDtypeStruct((8, rows_in), F32),
        ),
        in_specs=[vmem] * 2,
        out_specs=(vmem, vmem),
        compiler_params=params(),
        name="profile",
    )(rows_of_weights, era5_columns[0])
    other = swapped(leaving, "gz", 1)
    far_mask = swapped(terrain_mask[8:], "gz", 1).reshape(8 * rows, cols)
    near_mask = terrain_mask.reshape(layers * rows, cols)

    outgoing = pl.pallas_call(
        functools.partial(route_kernel, tiles=tiles, capacity=capacity),
        out_shape=jax.ShapeDtypeStruct((slots, 128), F32),
        in_specs=[smem, vmem, vmem, vmem],
        out_specs=vmem,
        compiler_params=params(),
        name="route",
    )(live_counts, column_owner, own, other)
    received = lax.all_to_all(
        outgoing.reshape(tiles, capacity, 128), ("gx", "gy"), split_axis=0, concat_axis=0, tiled=True
    ).reshape(slots, 128)

    strip_rows = NS * 3 + 24
    grid, low_y, high_y, low_x, high_x = pl.pallas_call(
        functools.partial(gather_kernel, blocks=blocks),
        out_shape=(
            jax.ShapeDtypeStruct((cols // 128, rows, NF, 128), F32),
            jax.ShapeDtypeStruct((NS, 128), F32),
            jax.ShapeDtypeStruct((NS, 128), F32),
            jax.ShapeDtypeStruct((strip_rows, cols), F32),
            jax.ShapeDtypeStruct((strip_rows, cols), F32),
        ),
        in_specs=[smem] + [vmem] * 5,
        out_specs=(vmem,) * 5,
        scratch_shapes=[
            pltpu.VMEM((blocks, NF, 128), F32),
            pltpu.VMEM((2, points, 1, 128), jnp.int32),
            pltpu.VMEM((2, points, 1, 128), F32),
            pltpu.VMEM((cols // 128, layers * rows, 128), F32),
        ],
        compiler_params=params(),
        name="gather",
    )(block, received, stencil_index, stencil_weight, near_mask, far_mask)

    right = shifted(low_y, "gy", -1)
    left = shifted(high_y, "gy", 1)
    above = shifted(low_x, "gx", -1)
    below = shifted(high_x, "gx", 1)
    corners = jnp.concatenate([right, left], axis=1)
    above_corner = shifted(corners, "gx", -1)
    below_corner = shifted(corners, "gx", 1)

    basis, moments = pl.pallas_call(
        functools.partial(
            basis_kernel, last_gx=lax.axis_size("gx") - 1, last_gy=lax.axis_size("gy") - 1
        ),
        out_shape=(
            jax.ShapeDtypeStruct((3, LZ + 1, XR, YR), F32),
            jax.ShapeDtypeStruct((8, 128), F32),
        ),
        in_specs=[smem] + [vmem] * 9,
        out_specs=(vmem, vmem),
        scratch_shapes=[
            pltpu.VMEM((YR // 128, XR * NS, 128), F32),
            pltpu.VMEM((YR // 128, XR * 24, 128), F32),
            pltpu.VMEM((LZ + DEEP, XR, YR), F32),
            pltpu.VMEM((2, DEEP - 1, XR, YR), F32),
        ],
        compiler_params=params(),
        name="basis",
    )(
        block, grid, near_mask, far_mask,
        right, left, above, above_corner, below, below_corner,
    )

    moments = moments + swapped(moments, "gz", 1)
    for axis in ("gy", "gx"):
        bit = 1
        while bit < lax.axis_size(axis):
            moments = moments + swapped(moments, axis, bit)
            bit *= 2

    potential, wind_field, speed, balance = pl.pallas_call(
        wind_kernel,
        out_shape=(
            jax.ShapeDtypeStruct((layers, rows, cols), F32),
            jax.ShapeDtypeStruct((3, layers, rows, cols), F32),
            jax.ShapeDtypeStruct((rows, cols), F32),
            jax.ShapeDtypeStruct((rows, cols), F32),
        ),
        in_specs=[smem] + [vmem] * 4,
        out_specs=(vmem,) * 4,
        scratch_shapes=[pltpu.VMEM((LZ + 1, XR, YR), F32)],
        compiler_params=params(),
        name="wind",
    )(block, moments, basis, grid.reshape(cols // 128, rows * NF, 128), terrain_mask)

    speed_mean = (speed + swapped(speed, "gz", 1)) / 32.0
    lags = jnp.asarray(LAGS, F32)[:, None, None]
    decay_rate = jnp.exp(-(1.0 + 0.5 * speed_mean)[None] / lags)
    fuel_moisture = fuel_start
    for hour in range(PASSES):
        goal = balance + 0.3 * math.cos(2.0 * math.pi * hour / 24.0)
        fuel_moisture = goal + (fuel_moisture - goal) * decay_rate
    return (potential, wind_field, fuel_moisture)


def solution(mesh):
    placed = (
        P(("gx", "gy"), None, "gz"),
        P(("gx", "gy"), None),
        P(("gx", "gy")),
        P("gz", None),
        P(None, "gx", "gy"),
        P(None, "gx", "gy"),
        P("gz", "gx", "gy"),
        P(None, "gx", "gy"),
    )
    return jax.shard_map(
        shards,
        mesh=mesh,
        in_specs=placed,
        out_specs=(P("gz", "gx", "gy"), P(None, "gz", "gx", "gy"), P(None, "gx", "gy")),
        check_vma=False,
    )
```

time: 754 us -> 143 us (0.19)
  blocking collectives: 380 us -> 0 us
  local copies, waits for them, and re-layouts: 133 us -> 5.59 us
  waiting for transfers between devices: 84.3 us -> 39.9 us
  starting transfers between devices: 91.5 us -> 52.9 us
  Pallas kernels: 0 us -> 36.8 us
  other arithmetic: 38.9 us -> 4.96 us
  between operations: 22.3 us -> 1.5 us
    psum x5 -> x0, blocking collectives: 380 us -> none  [the longest x3 227 us: residual_dot(): return lax.psum(jnp.sum(residual * precond), ('gx', 'gy', 'gz'))]
    gather x1 -> x0, local copies, waits for them, and re-layouts: 108 us -> none  [shards(): picked = jnp.take(profile, indices, axis=1)]
    pallas_call x0 -> x5, Pallas kernels: none -> 36.8 us  [the longest x1 15.8 us: shards(): pl.pallas_call(functools.partial(gather_kernel, blocks=blocks), out_shape...]
    ppermute x28 -> x17, starting transfers between devices: 75.2 us -> 39.2 us  [the longest x11 25.4 us: swapped(): return lax.ppermute(block, axis, [(i, i ^ bit) for i in range(count)])]
    psum x1 -> x0, waiting for transfers between devices: 29.1 us -> none  [shards(): column_totals = lax.psum(layer_sums, 'gz')]
    reduce_sum x11 -> x1, other arithmetic: 27.6 us -> 0.72 us  [shards(): total = jnp.sum(vertical_weights, axis=0, keepdims=True)]
    ppermute x28 -> x17, waiting for transfers between devices: 36.7 us -> 22.4 us  [the longest x11 18.8 us: swapped(): return lax.ppermute(block, axis, [(i, i ^ bit) for i in range(count)])]
  transfers between devices with their start and end apart: 30 -> 18, of which waited for: 18 -> 14; matrix products, arithmetic and copies ran while one was open for 1% -> 1% of each run, Pallas kernels for 0% -> 0%
where the time goes in v1:
time: 143 us; the launch traced here: 142 us
  starting transfers between devices  52.9 us (37%)
  waiting for transfers between devices  39.9 us (28%)
  Pallas kernels  36.8 us (26%)
  local copies, waits for them, and re-layouts  5.59 us (4%)
  other arithmetic  4.96 us (3%)
  between operations  1.5 us (1%)
    ppermute x11, starting transfers between devices, swapped(): return lax.ppermute(block, axis, [(i, i ^ bit) for i in range(count)])  25.4 us
    ppermute x11, waiting for transfers between devices, swapped(): return lax.ppermute(block, axis, [(i, i ^ bit) for i in range(count)])  18.8 us
    all_to_all x1, waiting for transfers between devices, shards(): lax.all_to_all(outgoing.reshape(tiles, capacity, 128), ('gx', 'gy'), spli...  17.4 us
    pallas_call x1, Pallas kernels, shards(): pl.pallas_call(functools.partial(gather_kernel, blocks=blocks), out_shape...  15.8 us
    all_to_all x1, starting transfers between devices, shards(): lax.all_to_all(outgoing.reshape(tiles, capacity, 128), ('gx', 'gy'), spli...  13.8 us
    ppermute x6, starting transfers between devices, shifted(): return lax.ppermute(block, axis, pairs)  13.8 us
    pallas_call x1, Pallas kernels, shards(): pl.pallas_call(functools.partial(basis_kernel, last_gx=lax.axis_size('gx'...  11.5 us
    pallas_call x1, Pallas kernels, shards(): pl.pallas_call(wind_kernel, out_shape=(jax.ShapeDtypeStruct((layers, rows...  4.6 us
  transfers between devices with their start and end apart: 18, of which 14 were waited for; matrix products, arithmetic and copies ran while one was open for 1% of the time, Pallas kernels for 0%

profile of v1, /device:TPU:1, one launch (start us, length us, event | category | flops | bytes accessed | tf_op | source)
XLA Modules:
  0.0 141.7 jit_solution(5144249543589208396)
XLA Ops:
  2.4 2.4 %concatenate.6.weights_ref = f32[48,128]{1,0:T(8,128)} concatenate(f32[16,128]{1,0:T(8,128)S(1)} %get-tuple-element.36, f32[16,128]{1,0:T(8,128)S(1)} %get-tuple-element.35, f32[6,128]{1,0:T(8,128)S(1)} %broadcast_in_dim.4, f32[1,128]{1,0:T(1,128)S(1)} %get-tuple-element.40, f32[1,128]{1,0:T(1,128)S(1)} %get-tuple-element.39, f32[3,128]{1,0:T(4,128)S(1)} %get-tuple-element.38, ...), dimensions={0} | concatenate | bytes 49152 | tf_op jit(solution)/shard_map/concatenate | solution.py:470
  4.8 2.1 %profile.1 = (f32[40,1024]{1,0:T(8,128)}, f32[8,1024]{1,0:T(8,128)}) custom-call(f32[48,128]{1,0:T(8,128)} %concatenate.6.weights_ref, f32[1024,128]{1,0:T(8,128)} %bitcast.17), custom_call_target="tpu_custom_call" | custom-call | tf_op jit(solution)/shard_map/profile/pallas_call | solution.py:484
  6.9 3.2 %collective-permute-start = (f32[8,1024]{1,0:T(8,128)}, f32[8,1024]{1,0:T(8,128)S(1)}, u32[]{:S(2)}, u32[]{:S(2)}) collective-permute-start(f32[8,1024]{1,0:T(8,128)} %get-tuple-element.17), channel_id=1, source_target_pairs={{0,1},{1,0},{2,3},{3,2},{4,5},{5,4},{6,7},{7,6},{8,9},{9,8},{10,11... | collective-permute-start | bytes 98312 | tf_op jit(solution)/shard_map/ppermute | solution.py:437
  11.8 2.8 %route.1 = f32[1024,128]{1,0:T(8,128)} custom-call(s32[1]{0:T(128)S(6)} %copy.13.live_ref, s32[1,1024]{1,0:T(1,128)} %owner_ref.1, f32[40,1024]{1,0:T(8,128)} %get-tuple-element.16.own_ref, f32[8,1024]{1,0:T(8,128)} %copy-done.10), custom_call_target="tpu_custom_call" | custom-call | tf_op jit(solution)/shard_map/route/pallas_call | solution.py:499
  14.7 13.8 %all-to-all-start = ((f32[128,8,128]{2,1,0:T(8,128)}), f32[128,8,128]{2,1,0:T(8,128)S(1)}, u32[]{:S(2)}, u32[]{:S(2)}) async-start(f32[128,8,128]{2,1,0:T(8,128)} %bitcast.14), calls=%async_computation | async-start | bytes 1048576 | tf_op jit(solution)/shard_map/all_to_all | solution.py:507
  30.4 17.4 %all-to-all-done = f32[128,8,128]{2,1,0:T(8,128)S(1)} async-done(((f32[128,8,128]{2,1,0:T(8,128)}), f32[128,8,128]{2,1,0:T(8,128)S(1)}, u32[]{:S(2)}, u32[]{:S(2)}) %all-to-all-start) | async-done | bytes 524320 | tf_op jit(solution)/shard_map/all_to_all | solution.py:507
  47.8 0.8 copy-done.1
  48.6 15.8 %gather.1 = (f32[2,32,40,128]{3,2,1,0:T(8,128)}, f32[56,128]{1,0:T(8,128)}, f32[56,128]{1,0:T(8,128)}, f32[192,256]{1,0:T(8,128)}, f32[192,256]{1,0:T(8,128)}) custom-call(s32[3]{0:T(128)} %pad_add_fusion.block_ref, f32[1024,128]{1,0:T(8,128)} %bitcast.13, s32[4,32,256]{2,1,0:T(8,128)} %index_ref.1, f32[4,32,256]{2,1,0:T(8,128)} %weight_ref.1, ...), custom_call_target="tpu_custom_call" | custom-call | tf_op jit(solution)/shard_map/gather/pallas_call | solution.py:512
  64.4 1.3 collective-permute-start.2
  65.7 4.0 %collective-permute-start.3 = (f32[56,128]{1,0:T(8,128)}, f32[56,128]{1,0:T(8,128)S(1)}, u32[]{:S(2)}, u32[]{:S(2)}) collective-permute-start(f32[56,128]{1,0:T(8,128)} %get-tuple-element.20), channel_id=1, source_target_pairs={{0,2},{2,4},{4,6},{6,8},{8,10},{10,12},{12,14},{1,3},{3,5},{5,7},{... | collective-permute-start | bytes 86024 | tf_op jit(solution)/shard_map/ppermute | solution.py:432
  69.7 1.3 collective-permute-start.4
  71.0 4.0 %collective-permute-start.6 = (f32[192,256]{1,0:T(8,128)}, f32[192,256]{1,0:T(8,128)S(1)}, u32[]{:S(2)}, u32[]{:S(2)}) collective-permute-start(f32[192,256]{1,0:T(8,128)} %get-tuple-element.22), channel_id=1, source_target_pairs={{0,16},{16,32},{32,48},{48,64},{64,80},{80,96},{96,112},{112,128},... | collective-permute-start | bytes 589832 | tf_op jit(solution)/shard_map/ppermute | solution.py:432
  75.1 1.9 %collective-permute-start.7 = (f32[56,256]{1,0:T(8,128)S(1)}, f32[56,256]{1,0:T(8,128)S(1)}, u32[]{:S(2)}, u32[]{:S(2)}) collective-permute-start(f32[56,256]{1,0:T(8,128)S(1)} %constant_dynamic-update-slice_fusion), channel_id=1, source_target_pairs={{0,16},{16,32},{32,48},{48,64},{64,80},{80,96},{96,112},{112,128},... | collective-permute-start | bytes 172040 | tf_op jit(solution)/shard_map/ppermute | solution.py:432
  77.0 1.3 collective-permute-start.5
  78.4 3.5 %collective-permute-done.5.above_corner_ref = f32[56,256]{1,0:T(8,128)S(1)} collective-permute-done((f32[56,256]{1,0:T(8,128)S(1)}, f32[56,256]{1,0:T(8,128)S(1)}, u32[]{:S(2)}, u32[]{:S(2)}) %collective-permute-start.5) | collective-permute-done | bytes 57376 | tf_op jit(solution)/shard_map/ppermute | solution.py:432
  82.7 11.5 %basis.1 = (f32[3,17,40,384]{3,2,1,0:T(8,128)}, f32[8,128]{1,0:T(8,128)}) custom-call(s32[3]{0:T(128)} %pad_add_fusion.block_ref, f32[2,32,40,128]{3,2,1,0:T(8,128)} %get-tuple-element.18.grid_ref, s32[512,256]{1,0:T(8,128)} %bitcast.11, s32[256,256]{1,0:T(8,128)} %bitcast.16, f32[56,128]{1,0:T(8,128)} %copy-done.5, f32[56,128]{1,0:T(8,128)} %copy-done.6, ...), custom_call_target="tpu_custom_call" | custom-call | tf_op jit(solution)/shard_map/basis/pallas_call | solution.py:541
  94.1 4.5 %collective-permute-start.8 = (f32[8,128]{1,0:T(8,128)}, f32[8,128]{1,0:T(8,128)S(1)}, u32[]{:S(2)}, u32[]{:S(2)}) collective-permute-start(f32[8,128]{1,0:T(8,128)} %get-tuple-element.23), channel_id=1, source_target_pairs={{0,1},{1,0},{2,3},{3,2},{4,5},{5,4},{6,7},{7,6},{8,9},{9,8},{10,11... | collective-permute-start | bytes 12296 | tf_op jit(solution)/shard_map/ppermute | solution.py:437
  98.7 1.0 collective-permute-done.8
  100.7 2.2 %collective-permute-done.9 = f32[8,128]{1,0:T(8,128)S(1)} collective-permute-done((f32[8,128]{1,0:T(8,128)S(1)}, f32[8,128]{1,0:T(8,128)S(1)}, u32[]{:S(2)}, u32[]{:S(2)}) %collective-permute-start.9) | collective-permute-done | bytes 4128 | tf_op jit(solution)/shard_map/ppermute | solution.py:437
  103.3 2.9 %collective-permute-done.10 = f32[8,128]{1,0:T(8,128)S(1)} collective-permute-done((f32[8,128]{1,0:T(8,128)S(1)}, f32[8,128]{1,0:T(8,128)S(1)}, u32[]{:S(2)}, u32[]{:S(2)}) %collective-permute-start.10) | collective-permute-done | bytes 4128 | tf_op jit(solution)/shard_map/ppermute | solution.py:437
  106.2 1.1 collective-permute-start.11
  107.3 5.3 %collective-permute-done.11 = f32[8,128]{1,0:T(8,128)S(1)} collective-permute-done((f32[8,128]{1,0:T(8,128)S(1)}, f32[8,128]{1,0:T(8,128)S(1)}, u32[]{:S(2)}, u32[]{:S(2)}) %collective-permute-start.11) | collective-permute-done | bytes 4128 | tf_op jit(solution)/shard_map/ppermute | solution.py:437
  112.6 0.9 collective-permute-start.12
  113.5 1.9 %collective-permute-done.12 = f32[8,128]{1,0:T(8,128)S(1)} collective-permute-done((f32[8,128]{1,0:T(8,128)S(1)}, f32[8,128]{1,0:T(8,128)S(1)}, u32[]{:S(2)}, u32[]{:S(2)}) %collective-permute-start.12) | collective-permute-done | bytes 4128 | tf_op jit(solution)/shard_map/ppermute | solution.py:437
  115.4 3.3 %collective-permute-start.13 = (f32[8,128]{1,0:T(8,128)S(1)}, f32[8,128]{1,0:T(8,128)S(1)}, u32[]{:S(2)}, u32[]{:S(2)}) collective-permute-start(f32[8,128]{1,0:T(8,128)S(1)} %add.105), channel_id=1, source_target_pairs={{0,32},{16,48},{32,0},{48,16},{64,96},{80,112},{96,64},{112,80},{1... | collective-permute-start | bytes 12296 | tf_op jit(solution)/shard_map/ppermute | solution.py:437
  118.7 1.0 collective-permute-done.13
  120.4 1.8 %collective-permute-done.14 = f32[8,128]{1,0:T(8,128)S(1)} collective-permute-done((f32[8,128]{1,0:T(8,128)S(1)}, f32[8,128]{1,0:T(8,128)S(1)}, u32[]{:S(2)}, u32[]{:S(2)}) %collective-permute-start.14) | collective-permute-done | bytes 4128 | tf_op jit(solution)/shard_map/ppermute | solution.py:437
  122.2 2.4 %collective-permute-start.15 = (f32[8,128]{1,0:T(8,128)S(1)}, f32[8,128]{1,0:T(8,128)S(1)}, u32[]{:S(2)}, u32[]{:S(2)}) collective-permute-start(f32[8,128]{1,0:T(8,128)S(1)} %add.107), channel_id=1, source_target_pairs={{0,128},{16,144},{32,160},{48,176},{64,192},{80,208},{96,224},{112... | collective-permute-start | bytes 12296 | tf_op jit(solution)/shard_map/ppermute | solution.py:437
  124.6 1.6 %collective-permute-done.15 = f32[8,128]{1,0:T(8,128)S(1)} collective-permute-done((f32[8,128]{1,0:T(8,128)S(1)}, f32[8,128]{1,0:T(8,128)S(1)}, u32[]{:S(2)}, u32[]{:S(2)}) %collective-permute-start.15) | collective-permute-done | bytes 4128 | tf_op jit(solution)/shard_map/ppermute | solution.py:437
  126.7 4.6 %wind.1 = (f32[16,32,256]{2,1,0:T(8,128)}, f32[3,16,32,256]{3,2,1,0:T(8,128)}, f32[32,256]{1,0:T(8,128)}, f32[32,256]{1,0:T(8,128)}) custom-call(s32[3]{0:T(128)} %pad_add_fusion.block_ref, f32[8,128]{1,0:T(8,128)} %add.108.moments_ref, f32[3,17,40,384]{3,2,1,0:T(8,128)} %get-tuple-element.24.basis_ref, f32[2,1280,128]{2,1,0:T(8,128)} %bitcast.12, ...), custom_call_target="tpu_custom_call" | custom-call | tf_op jit(solution)/shard_map/wind/pallas_call | solution.py:571
  131.3 7.7 %collective-permute-start.16 = (f32[32,256]{1,0:T(8,128)}, f32[32,256]{1,0:T(8,128)S(1)}, u32[]{:S(2)}, u32[]{:S(2)}) collective-permute-start(f32[32,256]{1,0:T(8,128)} %get-tuple-element.28), channel_id=1, source_target_pairs={{0,1},{1,0},{2,3},{3,2},{4,5},{5,4},{6,7},{7,6},{8,9},{9,8},{10,11... | collective-permute-start | bytes 98312 | tf_op jit(solution)/shard_map/ppermute | solution.py:437
  139.1 0.8 broadcast_add_fusion.3
  (57 shorter events, 10.1 us)
Async XLA Ops:
  0.6 27.8 %copy-start = (s32[16,32,256]{2,1,0:T(8,128)S(1)}, s32[16,32,256]{2,1,0:T(8,128)}, u32[]{:S(2)}) copy-start(s32[16,32,256]{2,1,0:T(8,128)} %mask_ref.1) | copy-start | bytes 1572868
  6.9 4.3 %collective-permute-start = (f32[8,1024]{1,0:T(8,128)}, f32[8,1024]{1,0:T(8,128)S(1)}, u32[]{:S(2)}, u32[]{:S(2)}) collective-permute-start(f32[8,1024]{1,0:T(8,128)} %get-tuple-element.17), channel_id=1, source_target_pairs={{0,1},{1,0},{2,3},{3,2},{4,5},{5,4},{6,7},{7,6},{8,9},{9,8},{10,11... | collective-permute-start | bytes 98312 | tf_op jit(solution)/shard_map/ppermute | solution.py:437
  11.2 0.6 copy-start.10
  14.7 33.1 %all-to-all-start = ((f32[128,8,128]{2,1,0:T(8,128)}), f32[128,8,128]{2,1,0:T(8,128)S(1)}, u32[]{:S(2)}, u32[]{:S(2)}) async-start(f32[128,8,128]{2,1,0:T(8,128)} %bitcast.14), calls=%async_computation | async-start | bytes 1048576 | tf_op jit(solution)/shard_map/all_to_all | solution.py:507
  28.5 1.9 %collective-permute-start.1 = (s32[8,32,256]{2,1,0:T(8,128)S(1)}, s32[8,32,256]{2,1,0:T(8,128)S(1)}, u32[]{:S(2)}, u32[]{:S(2)}) collective-permute-start(s32[8,32,256]{2,1,0:T(8,128)S(1)} %slice.7), channel_id=1, source_target_pairs={{0,1},{1,0},{2,3},{3,2},{4,5},{5,4},{6,7},{7,6},{8,9},{9,8},{10,11... | collective-permute-start | bytes 786440 | tf_op jit(solution)/shard_map/ppermute | solution.py:437
  30.4 17.5 %copy-start.2 = (s32[8,32,256]{2,1,0:T(8,128)}, s32[8,32,256]{2,1,0:T(8,128)S(1)}, u32[]{:S(2)}) copy-start(s32[8,32,256]{2,1,0:T(8,128)S(1)} %collective-permute-done.1) | copy-start | bytes 786436
  47.8 0.8 copy-start.1
  64.4 10.6 %collective-permute-start.2 = (f32[56,128]{1,0:T(8,128)}, f32[56,128]{1,0:T(8,128)S(1)}, u32[]{:S(2)}, u32[]{:S(2)}) collective-permute-start(f32[56,128]{1,0:T(8,128)} %get-tuple-element.19), channel_id=1, source_target_pairs={{2,0},{4,2},{6,4},{8,6},{10,8},{12,10},{14,12},{3,1},{5,3},{7,5},{... | collective-permute-start | bytes 86024 | tf_op jit(solution)/shard_map/ppermute | solution.py:432
  65.7 9.3 %collective-permute-start.3 = (f32[56,128]{1,0:T(8,128)}, f32[56,128]{1,0:T(8,128)S(1)}, u32[]{:S(2)}, u32[]{:S(2)}) collective-permute-start(f32[56,128]{1,0:T(8,128)} %get-tuple-element.20), channel_id=1, source_target_pairs={{0,2},{2,4},{4,6},{6,8},{8,10},{10,12},{12,14},{1,3},{3,5},{5,7},{... | collective-permute-start | bytes 86024 | tf_op jit(solution)/shard_map/ppermute | solution.py:432
  69.7 12.2 %collective-permute-start.4 = (f32[192,256]{1,0:T(8,128)}, f32[192,256]{1,0:T(8,128)S(1)}, u32[]{:S(2)}, u32[]{:S(2)}) collective-permute-start(f32[192,256]{1,0:T(8,128)} %get-tuple-element.21), channel_id=1, source_target_pairs={{16,0},{32,16},{48,32},{64,48},{80,64},{96,80},{112,96},{128,112},... | collective-permute-start | bytes 589832 | tf_op jit(solution)/shard_map/ppermute | solution.py:432
  71.0 10.9 %collective-permute-start.6 = (f32[192,256]{1,0:T(8,128)}, f32[192,256]{1,0:T(8,128)S(1)}, u32[]{:S(2)}, u32[]{:S(2)}) collective-permute-start(f32[192,256]{1,0:T(8,128)} %get-tuple-element.22), channel_id=1, source_target_pairs={{0,16},{16,32},{32,48},{48,64},{64,80},{80,96},{96,112},{112,128},... | collective-permute-start | bytes 589832 | tf_op jit(solution)/shard_map/ppermute | solution.py:432
  75.0 6.9 %copy-start.5 = (f32[56,128]{1,0:T(8,128)}, f32[56,128]{1,0:T(8,128)S(1)}, u32[]{:S(2)}) copy-start(f32[56,128]{1,0:T(8,128)S(1)} %collective-permute-done.2.right_ref) | copy-start | bytes 86020
  75.0 6.9 %copy-start.6 = (f32[56,128]{1,0:T(8,128)}, f32[56,128]{1,0:T(8,128)S(1)}, u32[]{:S(2)}) copy-start(f32[56,128]{1,0:T(8,128)S(1)} %collective-permute-done.3.left_ref) | copy-start | bytes 86020
  75.1 3.3 %collective-permute-start.7 = (f32[56,256]{1,0:T(8,128)S(1)}, f32[56,256]{1,0:T(8,128)S(1)}, u32[]{:S(2)}, u32[]{:S(2)}) collective-permute-start(f32[56,256]{1,0:T(8,128)S(1)} %constant_dynamic-update-slice_fusion), channel_id=1, source_target_pairs={{0,16},{16,32},{32,48},{48,64},{64,80},{80,96},{96,112},{112,128},... | collective-permute-start | bytes 172040 | tf_op jit(solution)/shard_map/ppermute | solution.py:432
  77.0 4.9 %collective-permute-start.5 = (f32[56,256]{1,0:T(8,128)S(1)}, f32[56,256]{1,0:T(8,128)S(1)}, u32[]{:S(2)}, u32[]{:S(2)}) collective-permute-start(f32[56,256]{1,0:T(8,128)S(1)} %constant_dynamic-update-slice_fusion), channel_id=1, source_target_pairs={{16,0},{32,16},{48,32},{64,48},{80,64},{96,80},{112,96},{128,112},... | collective-permute-start | bytes 172040 | tf_op jit(solution)/shard_map/ppermute | solution.py:432
  78.4 3.5 %copy-start.8 = (f32[56,256]{1,0:T(8,128)}, f32[56,256]{1,0:T(8,128)S(1)}, u32[]{:S(2)}) copy-start(f32[56,256]{1,0:T(8,128)S(1)} %collective-permute-done.7.below_corner_ref) | copy-start | bytes 172036
  81.9 0.6 copy-start.9
  81.9 0.7 copy-start.3
  81.9 0.7 copy-start.4
  94.1 5.6 %collective-permute-start.8 = (f32[8,128]{1,0:T(8,128)}, f32[8,128]{1,0:T(8,128)S(1)}, u32[]{:S(2)}, u32[]{:S(2)}) collective-permute-start(f32[8,128]{1,0:T(8,128)} %get-tuple-element.23), channel_id=1, source_target_pairs={{0,1},{1,0},{2,3},{3,2},{4,5},{5,4},{6,7},{7,6},{8,9},{9,8},{10,11... | collective-permute-start | bytes 12296 | tf_op jit(solution)/shard_map/ppermute | solution.py:437
  100.4 2.5 %collective-permute-start.9 = (f32[8,128]{1,0:T(8,128)S(1)}, f32[8,128]{1,0:T(8,128)S(1)}, u32[]{:S(2)}, u32[]{:S(2)}) collective-permute-start(f32[8,128]{1,0:T(8,128)S(1)} %add.101), channel_id=1, source_target_pairs={{0,2},{2,0},{4,6},{6,4},{8,10},{10,8},{12,14},{14,12},{1,3},{3,1},... | collective-permute-start | bytes 12296 | tf_op jit(solution)/shard_map/ppermute | solution.py:437
  102.9 3.4 %collective-permute-start.10 = (f32[8,128]{1,0:T(8,128)S(1)}, f32[8,128]{1,0:T(8,128)S(1)}, u32[]{:S(2)}, u32[]{:S(2)}) collective-permute-start(f32[8,128]{1,0:T(8,128)S(1)} %add.102), channel_id=1, source_target_pairs={{0,4},{2,6},{4,0},{6,2},{8,12},{10,14},{12,8},{14,10},{1,5},{3,7},... | collective-permute-start | bytes 12296 | tf_op jit(solution)/shard_map/ppermute | solution.py:437
  106.2 6.4 %collective-permute-start.11 = (f32[8,128]{1,0:T(8,128)S(1)}, f32[8,128]{1,0:T(8,128)S(1)}, u32[]{:S(2)}, u32[]{:S(2)}) collective-permute-start(f32[8,128]{1,0:T(8,128)S(1)} %add.103), channel_id=1, source_target_pairs={{0,8},{2,10},{4,12},{6,14},{8,0},{10,2},{12,4},{14,6},{1,9},{3,11}... | collective-permute-start | bytes 12296 | tf_op jit(solution)/shard_map/ppermute | solution.py:437
  112.6 2.8 %collective-permute-start.12 = (f32[8,128]{1,0:T(8,128)S(1)}, f32[8,128]{1,0:T(8,128)S(1)}, u32[]{:S(2)}, u32[]{:S(2)}) collective-permute-start(f32[8,128]{1,0:T(8,128)S(1)} %add.104), channel_id=1, source_target_pairs={{0,16},{16,0},{32,48},{48,32},{64,80},{80,64},{96,112},{112,96},{1... | collective-permute-start | bytes 12296 | tf_op jit(solution)/shard_map/ppermute | solution.py:437
  115.4 4.3 %collective-permute-start.13 = (f32[8,128]{1,0:T(8,128)S(1)}, f32[8,128]{1,0:T(8,128)S(1)}, u32[]{:S(2)}, u32[]{:S(2)}) collective-permute-start(f32[8,128]{1,0:T(8,128)S(1)} %add.105), channel_id=1, source_target_pairs={{0,32},{16,48},{32,0},{48,16},{64,96},{80,112},{96,64},{112,80},{1... | collective-permute-start | bytes 12296 | tf_op jit(solution)/shard_map/ppermute | solution.py:437
  119.7 2.5 %collective-permute-start.14 = (f32[8,128]{1,0:T(8,128)S(1)}, f32[8,128]{1,0:T(8,128)S(1)}, u32[]{:S(2)}, u32[]{:S(2)}) collective-permute-start(f32[8,128]{1,0:T(8,128)S(1)} %add.106), channel_id=1, source_target_pairs={{0,64},{16,80},{32,96},{48,112},{64,0},{80,16},{96,32},{112,48},{1... | collective-permute-start | bytes 12296 | tf_op jit(solution)/shard_map/ppermute | solution.py:437
  122.2 4.0 %collective-permute-start.15 = (f32[8,128]{1,0:T(8,128)S(1)}, f32[8,128]{1,0:T(8,128)S(1)}, u32[]{:S(2)}, u32[]{:S(2)}) collective-permute-start(f32[8,128]{1,0:T(8,128)S(1)} %add.107), channel_id=1, source_target_pairs={{0,128},{16,144},{32,160},{48,176},{64,192},{80,208},{96,224},{112... | collective-permute-start | bytes 12296 | tf_op jit(solution)/shard_map/ppermute | solution.py:437
  126.7 14.2 %copy-start.7 = (f32[3,32,256]{2,1,0:T(8,128)S(1)}, f32[3,32,256]{2,1,0:T(8,128)}, u32[]{:S(2)}) copy-start(f32[3,32,256]{2,1,0:T(8,128)} %param.16) | copy-start | bytes 294916
  126.7 14.2 %copy-start.11 = (f32[3]{0:T(128)S(1)}, f32[3]{0:T(128)}, u32[]{:S(2)}) copy-start(f32[3]{0:T(128)} %constant.52) | copy-start | bytes 40
  131.3 8.8 %collective-permute-start.16 = (f32[32,256]{1,0:T(8,128)}, f32[32,256]{1,0:T(8,128)S(1)}, u32[]{:S(2)}, u32[]{:S(2)}) collective-permute-start(f32[32,256]{1,0:T(8,128)} %get-tuple-element.28), channel_id=1, source_target_pairs={{0,1},{1,0},{2,3},{3,2},{4,5},{5,4},{6,7},{7,6},{8,9},{9,8},{10,11... | collective-permute-start | bytes 98312 | tf_op jit(solution)/shard_map/ppermute | solution.py:437

commit v2 on v1

--- a/solution.py
+++ b/solution.py
@@ -17,6 +17,7 @@
 DEEP = 3
 NF = 40
 NS = NF + LZ
+STRIP = NS * 3 + 24
 XR = 40
 YR = 384
 VMEM = 56 * 1024 * 1024
@@ -35,8 +36,26 @@
     return lax.dot_general(a, b, (((1,), (1,)), ((), ())), preferred_element_type=F32)
 
 
-def profile_kernel(weights_ref, columns_ref, own_ref, send_ref):
-    w_high, w_low = split(weights_ref[...])
+def profile_kernel(block_ref, weights_ref, columns_ref, own_ref, send_ref):
+    plain = weights_ref[...]
+    turned = jnp.concatenate([plain[LZ - 1 - i : LZ - i] for i in range(LZ)], axis=0)
+    weights = jnp.where(block_ref[2] == 0, plain, turned)
+    total = jnp.sum(plain, axis=0, keepdims=True)
+    edge = jnp.concatenate([weights[LZ - 1 - i : LZ - i] for i in range(DEEP)], axis=0)
+
+    def at_field(value, field):
+        blank = jnp.zeros_like(value)
+        return jnp.concatenate([value if f == field else blank for f in range(4)], axis=1)
+
+    sums = [at_field(total, 2), at_field(total, 3)]
+    stack = jnp.concatenate(
+        [at_field(weights, 0), at_field(weights, 1), jnp.zeros((2 * DEEP, columns_ref.shape[1]), F32)]
+        + sums
+        + [at_field(edge, 0), at_field(edge, 1)]
+        + sums,
+        axis=0,
+    )
+    w_high, w_low = split(stack)
     c_high, c_low = split(columns_ref[...])
     result = dot_nt(w_high, c_high) + dot_nt(w_high, c_low) + dot_nt(w_low, c_high)
     own_ref[...] = result[:NF]
@@ -66,109 +85,134 @@
     out_ref[...] = dot_nt(jnp.where(place, 1.0, 0.0).astype(BF16), both)
 
 
-def lane_pick(table, lanes):
-    return jnp.take_along_axis(table, lanes, axis=1)
-
-
-def pick_columns(table_ref, index, weight, blocks):
+def fill_table(received_ref, table_ref):
+    parts = received_ref.shape[0] // 256
+    turned = [jnp.transpose(received_ref[256 * p : 256 * p + 256, :]) for p in range(parts)]
+    for g in range(NF // 8):
+        for half, start in ((0, 0), (1, 64)):
+            rows = slice(start + 8 * g, start + 8 * g + 8)
+            value = jnp.concatenate([turned[p][rows] for p in range(parts)], axis=0)
+            table_ref[8 * parts * g : 8 * parts * (g + 1), 256 * half : 256 * half + 256] = (
+                value.astype(BF16)
+            )
+
+
+def pick_columns(table_ref, index, weight):
+    parts = table_ref.shape[0] // NF
     total = weight[0] + weight[1] + weight[2] + weight[3]
+    slot = lax.broadcasted_iota(jnp.int32, (256, 256), 0).astype(F32).astype(BF16)
     acc = [None] * (NF // 8)
     for point in range(len(index)):
-        lanes = jnp.broadcast_to(index[point] & 127, (8, 128))
-        part = jnp.broadcast_to(index[point] >> 7, (8, 128))
-        share = jnp.broadcast_to(weight[point] / total, (8, 128))
-        masks = [part == b for b in range(1, blocks)]
+        low = jnp.broadcast_to((index[point] & 255).astype(F32), (16, 256)).astype(BF16)
+        low = jnp.concatenate([low] * 16, axis=0)
+        chosen = jnp.where(slot == low, jnp.ones((256, 256), BF16), jnp.zeros((256, 256), BF16))
+        chosen = jnp.concatenate([chosen, chosen], axis=0)
+        found = jnp.dot(table_ref[...], chosen, preferred_element_type=F32)
+        part = jnp.broadcast_to(index[point] >> 8, (8, 256))
+        share = jnp.broadcast_to(weight[point] / total, (8, 256))
         for g in range(NF // 8):
-            value = lane_pick(table_ref[0, 8 * g : 8 * g + 8], lanes)
-            for b in range(1, blocks):
-                other = lane_pick(table_ref[b, 8 * g : 8 * g + 8], lanes)
-                value = jnp.where(masks[b - 1], other, value)
-            term = value * share
+            values = [
+                found[8 * (parts * g + p) : 8 * (parts * g + p) + 8] for p in range(parts)
+            ]
+            bit = 1
+            while len(values) > 1:
+                odd = (part & bit) != 0
+                values = [
+                    jnp.where(odd, values[i + 1], values[i]) for i in range(0, len(values), 2)
+                ]
+                bit *= 2
+            term = values[0] * share
             acc[g] = term if acc[g] is None else acc[g] + term
     return acc
 
 
-def gather_kernel(
+def pick_rows(table_ref, index_ref, weight_ref, first, steps, out_ref, base):
+    points, _, cols = index_ref.shape
+    index = [index_ref[k, pl.ds(first, 8), :] for k in range(points)]
+    weight = [weight_ref[k, pl.ds(first, 8), :] for k in range(points)]
+    for j in steps:
+        got = pick_columns(
+            table_ref, [value[j : j + 1] for value in index], [value[j : j + 1] for value in weight]
+        )
+        for g in range(NF // 8):
+            for h in range(cols // 128):
+                out_ref[h, base + j, 8 * g : 8 * g + 8, :] = got[g][:, 128 * h : 128 * h + 128]
+
+
+def edge_kernel(
     block_ref, received_ref, index_ref, weight_ref, mask_ref, far_mask_ref,
-    grid_ref, low_y_ref, high_y_ref, low_x_ref, high_x_ref,
-    table_ref, index_y_ref, weight_y_ref, mask_f_ref, *, blocks
+    table_ref, edge_ref, low_y_ref, high_y_ref, low_x_ref, high_x_ref, mask_f_ref
 ):
     lower = block_ref[2] == 0
     points, rows, cols = index_ref.shape
-    for b in range(blocks):
-        turned = jnp.transpose(received_ref[128 * b : 128 * b + 128, :])
-        table_ref[b] = turned[:NF] + turned[64 : 64 + NF]
-
+    fill_table(received_ref, table_ref)
     for h in range(cols // 128):
         at = slice(128 * h, 128 * h + 128)
         near = mask_ref[0 : 8 * rows, at]
         mask_f_ref[h, 0 : 8 * rows] = jnp.where(lower, near, far_mask_ref[:, at]).astype(F32)
         mask_f_ref[h, 8 * rows :] = mask_ref[8 * rows :, at].astype(F32)
 
-    lane = lax.broadcasted_iota(jnp.int32, (1, 128), 1)
-
-    for x in range(rows):
-        mine = (lane >> 2) == x
-        for side in range(2):
-            start = 0 if side == 0 else cols - 128
-            turn = (4 * x if side == 0 else 4 * x + 4) % 128
-            for k in range(points):
-                row = index_ref[k, x : x + 1, start : start + 128]
-                row = pltpu.roll(row, turn, 1)
-                index_y_ref[side, k] = jnp.where(mine, row, index_y_ref[side, k])
-                row = weight_ref[k, x : x + 1, start : start + 128]
-                row = pltpu.roll(row, turn, 1)
-                weight_y_ref[side, k] = jnp.where(mine, row, weight_y_ref[side, k])
-            out = low_y_ref if side == 0 else high_y_ref
-            for g in range(LZ // 8):
+    lane = lax.broadcasted_iota(jnp.int32, (8, 128), 1)
+    row = lax.broadcasted_iota(jnp.int32, (8, 128), 0)
+
+    def packed(value_ref, k):
+        sides = []
+        for start, turn in ((0, 0), (cols - 128, 4)):
+            total = None
+            for group in range(rows // 8):
+                value = value_ref[k, 8 * group : 8 * group + 8, start : start + 128]
+                value = pltpu.roll(value, 32 * group + turn, 1, stride=4, stride_axis=0)
+                value = jnp.where((lane >> 2) == row + 8 * group, value, jnp.zeros_like(value))
+                total = value if total is None else total + value
+            sides.append(jnp.sum(total, axis=0, keepdims=True))
+        return jnp.concatenate(sides, axis=1)
+
+    got = pick_columns(
+        table_ref,
+        [packed(index_ref, k) for k in range(points)],
+        [packed(weight_ref, k) for k in range(points)],
+    )
+    for out, start, turn in ((low_y_ref, 0, 0), (high_y_ref, cols - 128, 4)):
+        half = 0 if start == 0 else 1
+        for g in range(NF // 8):
+            out[8 * g : 8 * g + 8] = got[g][:, 128 * half : 128 * half + 128]
+        for g in range(LZ // 8):
+            total = None
+            for x in range(rows):
                 value = mask_f_ref[start // 128, pl.ds(x + g * 8 * rows, 8, stride=rows), :]
-                at = slice(NF + 8 * g, NF + 8 * g + 8)
-                out[at] = jnp.where(mine, pltpu.roll(value, turn, 1), out[at])
-
-    for side, out in ((0, low_y_ref), (1, high_y_ref)):
-        got = pick_columns(
-            table_ref,
-            [index_y_ref[side, k] for k in range(points)],
-            [weight_y_ref[side, k] for k in range(points)],
-            blocks,
-        )
-        for g in range(NF // 8):
-            out[8 * g : 8 * g + 8] = got[g]
-
-    def group_body(group, carry):
-        first = pl.multiple_of(8 * group, 8)
-        for h in range(cols // 128):
-            at = slice(128 * h, 128 * h + 128)
-            index = [index_ref[k, pl.ds(first, 8), at] for k in range(points)]
-            weight = [weight_ref[k, pl.ds(first, 8), at] for k in range(points)]
-            for j in range(8):
-                got = pick_columns(
-                    table_ref,
-                    [value[j : j + 1] for value in index],
-                    [value[j : j + 1] for value in weight],
-                    blocks,
-                )
-                for g in range(NF // 8):
-                    grid_ref[h, first + j, 8 * g : 8 * g + 8, :] = got[g]
-        return carry
-
-    lax.fori_loop(0, rows // 8, group_body, 0)
+                value = pltpu.roll(value, (4 * x + turn) % 128, 1)
+                total = value if total is None else jnp.where((lane >> 2) == x, value, total)
+            out[NF + 8 * g : NF + 8 * g + 8] = total
+
+    pick_rows(table_ref, index_ref, weight_ref, 0, range(4), edge_ref, 0)
+    pick_rows(table_ref, index_ref, weight_ref, rows - 8, range(4, 8), edge_ref, 0)
     for d in range(4):
-        for out, x in ((low_x_ref, d), (high_x_ref, rows - 1 - d)):
-            if d < 3:
-                for h in range(cols // 128):
-                    out[NS * d : NS * d + NF, 128 * h : 128 * h + 128] = grid_ref[h, x]
-                for g in range(LZ // 8):
-                    at = NS * d + NF + 8 * g
-                    for h in range(cols // 128):
-                        out[at : at + 8, 128 * h : 128 * h + 128] = mask_f_ref[
+        for out, x, kept in ((low_x_ref, d, d), (high_x_ref, rows - 1 - d, 7 - d)):
+            for h in range(cols // 128):
+                at = slice(128 * h, 128 * h + 128)
+                if d < 3:
+                    out[NS * d : NS * d + NF, at] = edge_ref[h, kept]
+                    for g in range(LZ // 8):
+                        first = NS * d + NF + 8 * g
+                        out[first : first + 8, at] = mask_f_ref[
                             h, pl.ds(x + g * 8 * rows, 8, stride=rows), :
                         ]
-            else:
-                for h in range(cols // 128):
-                    at = slice(128 * h, 128 * h + 128)
-                    out[NS * 3 : NS * 3 + 16, at] = grid_ref[h, x, 0:16]
-                    out[NS * 3 + 16 : NS * 3 + 24, at] = grid_ref[h, x, 32:40]
+                else:
+                    out[NS * 3 : NS * 3 + 16, at] = edge_ref[h, kept, 0:16]
+                    out[NS * 3 + 16 : NS * 3 + 24, at] = edge_ref[h, kept, 32:40]
+
+
+def middle_kernel(table_ref, index_ref, weight_ref, middle_ref):
+    rows = index_ref.shape[1]
+    pick_rows(table_ref, index_ref, weight_ref, 0, range(4, 8), middle_ref, -4)
+
+    def body(group, carry):
+        first = pl.multiple_of(8 * group, 8)
+        pick_rows(table_ref, index_ref, weight_ref, first, range(8), middle_ref, first - 4)
+        return carry
+
+    lax.fori_loop(1, rows // 8 - 1, body, 0)
+    pick_rows(table_ref, index_ref, weight_ref, rows - 8, range(4), middle_ref, rows - 12)
 
 
 def ring_smooth(plane):
@@ -177,20 +221,30 @@
 
 
 def basis_kernel(
-    block_ref, grid_ref, mask_ref, far_mask_ref,
-    right_ref, left_ref, above_ref, above_corner_ref, below_ref, below_corner_ref,
+    block_ref, edge_ref, middle_ref, mask_ref, far_mask_ref,
+    right_ref, left_ref, above_ref, below_ref,
     basis_ref, moments_ref,
     ext_ref, source_ref, air_ref, last_ref, *, last_gx, last_gy
 ):
     gx, gy, gz = block_ref[0], block_ref[1], block_ref[2]
     lower = gz == 0
-    halves, rows = grid_ref.shape[:2]
+    halves, rows = middle_ref.shape[0], middle_ref.shape[1] + 8
     cols = 128 * halves
     lane = lax.broadcasted_iota(jnp.int32, (8, 128), 1)
 
+    for h in range(halves):
+        for j in range(8):
+            x = j if j < 4 else rows - 8 + j
+            ext_ref[h, NS * x : NS * x + NF] = edge_ref[h, j]
+
+    def middle_row(x, carry):
+        for h in range(halves):
+            ext_ref[h, pl.ds(pl.multiple_of(x * NS, 8), NF), :] = middle_ref[h, x - 4]
+        return carry
+
+    lax.fori_loop(4, rows - 4, middle_row, 0)
+
     def own_row(x, carry):
-        for h in range(halves):
-            ext_ref[h, pl.ds(pl.multiple_of(x * NS, 8), NF), :] = grid_ref[h, x]
         for g in range(NS // 8):
             at = slice(8 * g, 8 * g + 8)
             right = pltpu.roll(right_ref[at], (128 - 4 * x) & 127, 1)
@@ -201,9 +255,9 @@
 
     lax.fori_loop(0, rows, own_row, 0)
     for d in range(4):
-        for near_ref, corner_ref, ring, origin in (
-            (above_ref, above_corner_ref, rows + d, d),
-            (below_ref, below_corner_ref, XR - 1 - d, rows - 1 - d),
+        for near_ref, ring, origin in (
+            (above_ref, rows + d, d),
+            (below_ref, XR - 1 - d, rows - 1 - d),
         ):
             base = ring * NS
             for h in range(halves):
@@ -216,9 +270,9 @@
                     ext_ref[h, base + 32 : base + 40] = near_ref[NS * 3 + 16 : NS * 3 + 24, at]
                     ext_ref[h, base + 40 : base + NS] = jnp.zeros((LZ, 128), F32)
             for g in range(NS // 8):
-                at = slice(8 * g, 8 * g + 8)
-                right = pltpu.roll(corner_ref[at, 0:128], (128 - 4 * origin) % 128, 1)
-                left = pltpu.roll(corner_ref[at, 128:256], (124 - 4 * origin) % 128, 1)
+                at = slice(STRIP + 8 * g, STRIP + 8 * g + 8)
+                right = pltpu.roll(near_ref[at, 0:128], (128 - 4 * origin) % 128, 1)
+                left = pltpu.roll(near_ref[at, 128:256], (124 - 4 * origin) % 128, 1)
                 side = jnp.where(lane < 4, right, jnp.where(lane >= 124, left, 0.0))
                 ext_ref[halves, base + 8 * g : base + 8 * g + 8] = side
 
@@ -321,8 +375,12 @@
         add(3, first_s * second)
         add(4, second_s * second)
         add(5, second_s * third)
-    rows_out = [jnp.sum(value, axis=0, keepdims=True) for value in sums]
-    moments_ref[...] = jnp.concatenate(rows_out + [jnp.zeros((2, 128), F32)], axis=0)
+    lane_id = lax.broadcasted_iota(jnp.int32, (1, 128), 1)
+    packed = jnp.zeros((1, 128), F32)
+    for k, value in enumerate(sums):
+        value = jnp.sum(jnp.sum(value, axis=0, keepdims=True), axis=1, keepdims=True)
+        packed = jnp.where(lane_id == k, value, packed)
+    moments_ref[...] = jnp.broadcast_to(packed, moments_ref.shape)
 
 
 def iterate(nu):
@@ -366,13 +424,18 @@
 
 
 def wind_kernel(
-    block_ref, moments_ref, basis_ref, grid_ref, mask_ref,
-    potential_ref, wind_ref, speed_ref, balance_ref, p_ref
+    block_ref, moments_ref, basis_ref, edge_ref, middle_ref, mask_ref,
+    potential_ref, wind_ref, speed_ref, balance_ref, p_ref, grid_ref
 ):
     gz = block_ref[2]
     rows, cols = speed_ref.shape
-    totals = jnp.sum(moments_ref[...], axis=1, keepdims=True)
-    factors = iterate([totals[k : k + 1] for k in range(6)])
+    near = 4 * NF
+    for h in range(cols // 128):
+        grid_ref[h, 0:near] = edge_ref[h, 0:near]
+        grid_ref[h, near : (rows - 4) * NF] = middle_ref[h]
+        grid_ref[h, (rows - 4) * NF :] = edge_ref[h, near:]
+    totals = jnp.sum(moments_ref[...], axis=0, keepdims=True)
+    factors = iterate([totals[:, k : k + 1] for k in range(6)])
     factors = [jnp.broadcast_to(c, (8, 128)) for c in factors]
     factors = [jnp.tile(c, (XR // 8, YR // 128)) for c in factors]
 
@@ -426,6 +489,18 @@
             balance_ref[x, at] = 1.2 + 0.5 * jnp.tanh(humid) - 0.3 * jnp.tanh(temp)
 
 
+def fuel_kernel(speed_ref, other_ref, balance_ref, start_ref, out_ref):
+    speed_mean = (speed_ref[...] + other_ref[...]) / 32.0
+    balance = balance_ref[...]
+    for kind, lag in enumerate(LAGS):
+        decay_rate = jnp.exp(-(1.0 + 0.5 * speed_mean) / lag)
+        moisture = start_ref[kind]
+        for hour in range(PASSES):
+            goal = balance + 0.3 * math.cos(2.0 * math.pi * hour / 24.0)
+            moisture = goal + (moisture - goal) * decay_rate
+        out_ref[kind] = moisture
+
+
 def shifted(block, axis, by):
     count = lax.axis_size(axis)
     pairs = [(i, i + by) for i in range(count) if 0 <= i + by < count]
@@ -453,143 +528,119 @@
     rows_in = column_owner.shape[1]
     capacity = rows_in // tiles
     slots = tiles * capacity
-    blocks = slots // 128
     layers, rows, cols = terrain_mask.shape
-    points = stencil_index.shape[0]
-    levels = vertical_weights.shape[1]
+    halves = cols // 128
     vmem = pl.BlockSpec(memory_space=pltpu.VMEM)
     smem = pl.BlockSpec(memory_space=pltpu.SMEM)
 
-    weights = jnp.where(gz == 0, vertical_weights, vertical_weights[::-1])
-    total = jnp.sum(vertical_weights, axis=0, keepdims=True)
-    edge = weights[: -DEEP - 1 : -1]
-
-    def at_field(value, field):
-        return jnp.pad(value, ((0, 0), (field * levels, (3 - field) * levels)))
-
-    rows_of_weights = jnp.concatenate(
-        [
-            at_field(weights, 0),
-            at_field(weights, 1),
-            jnp.zeros((2 * DEEP, 4 * levels), F32),
-            at_field(total, 2),
-            at_field(total, 3),
-            at_field(edge, 0),
-            at_field(edge, 1),
-            at_field(total, 2),
-            at_field(total, 3),
-        ],
-        axis=0,
-    )
-    own, leaving = pl.pallas_call(
+    def kernel(body, name, outs, operands, scratch=(), in_smem=0, cost=None):
+        shapes = [jax.ShapeDtypeStruct(shape, dtype) for shape, dtype in outs]
+        return pl.pallas_call(
+            body,
+            out_shape=tuple(shapes),
+            in_specs=[smem] * in_smem + [vmem] * (len(operands) - in_smem),
+            out_specs=(vmem,) * len(outs),
+            scratch_shapes=[pltpu.VMEM(shape, dtype) for shape, dtype in scratch],
+            compiler_params=params(),
+            cost_estimate=cost,
+            name=name,
+        )(*operands)
+
+    own, leaving = kernel(
         profile_kernel,
-        out_shape=(
-            jax.ShapeDtypeStruct((NF, rows_in), F32),
-            jax.ShapeDtypeStruct((8, rows_in), F32),
-        ),
-        in_specs=[vmem] * 2,
-        out_specs=(vmem, vmem),
-        compiler_params=params(),
-        name="profile",
-    )(rows_of_weights, era5_columns[0])
+        "profile",
+        [((NF, rows_in), F32), ((8, rows_in), F32)],
+        [block, vertical_weights, era5_columns[0]],
+        in_smem=1,
+    )
     other = swapped(leaving, "gz", 1)
     far_mask = swapped(terrain_mask[8:], "gz", 1).reshape(8 * rows, cols)
     near_mask = terrain_mask.reshape(layers * rows, cols)
-
-    outgoing = pl.pallas_call(
+    (outgoing,) = kernel(
         functools.partial(route_kernel, tiles=tiles, capacity=capacity),
-        out_shape=jax.ShapeDtypeStruct((slots, 128), F32),
-        in_specs=[smem, vmem, vmem, vmem],
-        out_specs=vmem,
-        compiler_params=params(),
-        name="route",
-    )(live_counts, column_owner, own, other)
+        "route",
+        [((slots, 128), F32)],
+        [live_counts, column_owner, own, other],
+        in_smem=1,
+    )
+    outgoing, far_mask, block = lax.optimization_barrier((outgoing, far_mask, block))
     received = lax.all_to_all(
         outgoing.reshape(tiles, capacity, 128), ("gx", "gy"), split_axis=0, concat_axis=0, tiled=True
     ).reshape(slots, 128)
 
-    strip_rows = NS * 3 + 24
-    grid, low_y, high_y, low_x, high_x = pl.pallas_call(
-        functools.partial(gather_kernel, blocks=blocks),
-        out_shape=(
-            jax.ShapeDtypeStruct((cols // 128, rows, NF, 128), F32),
-            jax.ShapeDtypeStruct((NS, 128), F32),
-            jax.ShapeDtypeStruct((NS, 128), F32),
-            jax.ShapeDtypeStruct((strip_rows, cols), F32),
-            jax.ShapeDtypeStruct((strip_rows, cols), F32),
-        ),
-        in_specs=[smem] + [vmem] * 5,
-        out_specs=(vmem,) * 5,
-        scratch_shapes=[
-            pltpu.VMEM((blocks, NF, 128), F32),
-            pltpu.VMEM((2, points, 1, 128), jnp.int32),
-            pltpu.VMEM((2, points, 1, 128), F32),
-            pltpu.VMEM((cols // 128, layers * rows, 128), F32),
+    table, edge, low_y, high_y, low_x, high_x = kernel(
+        edge_kernel,
+        "edge",
+        [
+            ((slots // 256 * NF, 512), BF16),
+            ((halves, 8, NF, 128), F32),
+            ((NS, 128), F32),
+            ((NS, 128), F32),
+            ((STRIP + NS, cols), F32),
+            ((STRIP + NS, cols), F32),
         ],
-        compiler_params=params(),
-        name="gather",
-    )(block, received, stencil_index, stencil_weight, near_mask, far_mask)
-
+        [block, received, stencil_index, stencil_weight, near_mask, far_mask],
+        scratch=[((halves, layers * rows, 128), F32)],
+        in_smem=1,
+    )
     right = shifted(low_y, "gy", -1)
     left = shifted(high_y, "gy", 1)
-    above = shifted(low_x, "gx", -1)
-    below = shifted(high_x, "gx", 1)
+    (middle,) = kernel(
+        middle_kernel,
+        "middle",
+        [((halves, rows - 8, NF, 128), F32)],
+        [table, stencil_index, stencil_weight],
+        cost=pl.CostEstimate(flops=4_000_000_000, bytes_accessed=1_600_000, transcendentals=0),
+    )
     corners = jnp.concatenate([right, left], axis=1)
-    above_corner = shifted(corners, "gx", -1)
-    below_corner = shifted(corners, "gx", 1)
-
-    basis, moments = pl.pallas_call(
+    above = shifted(low_x.at[STRIP:].set(corners), "gx", -1)
+    below = shifted(high_x.at[STRIP:].set(corners), "gx", 1)
+
+    devices = tiles * lax.axis_size("gz")
+    basis, moments = kernel(
         functools.partial(
             basis_kernel, last_gx=lax.axis_size("gx") - 1, last_gy=lax.axis_size("gy") - 1
         ),
-        out_shape=(
-            jax.ShapeDtypeStruct((3, LZ + 1, XR, YR), F32),
-            jax.ShapeDtypeStruct((8, 128), F32),
-        ),
-        in_specs=[smem] + [vmem] * 9,
-        out_specs=(vmem, vmem),
-        scratch_shapes=[
-            pltpu.VMEM((YR // 128, XR * NS, 128), F32),
-            pltpu.VMEM((YR // 128, XR * 24, 128), F32),
-            pltpu.VMEM((LZ + DEEP, XR, YR), F32),
-            pltpu.VMEM((2, DEEP - 1, XR, YR), F32),
+        "basis",
+        [((3, LZ + 1, XR, YR), F32), ((devices, 128), F32)],
+        [block, edge, middle, near_mask, far_mask, right, left, above, below],
+        scratch=[
+            ((YR // 128, XR * NS, 128), F32),
+            ((YR // 128, XR * 24, 128), F32),
+            ((LZ + DEEP, XR, YR), F32),
+            ((2, DEEP - 1, XR, YR), F32),
         ],
-        compiler_params=params(),
-        name="basis",
-    )(
-        block, grid, near_mask, far_mask,
-        right, left, above, above_corner, below, below_corner,
-    )
-
-    moments = moments + swapped(moments, "gz", 1)
-    for axis in ("gy", "gx"):
-        bit = 1
-        while bit < lax.axis_size(axis):
-            moments = moments + swapped(moments, axis, bit)
-            bit *= 2
-
-    potential, wind_field, speed, balance = pl.pallas_call(
+        in_smem=1,
+    )
+    moments = lax.all_to_all(
+        moments, ("gx", "gy", "gz"), split_axis=0, concat_axis=0, tiled=True
+    )
+    potential, wind_field, speed, balance = kernel(
         wind_kernel,
-        out_shape=(
-            jax.ShapeDtypeStruct((layers, rows, cols), F32),
-            jax.ShapeDtypeStruct((3, layers, rows, cols), F32),
-            jax.ShapeDtypeStruct((rows, cols), F32),
-            jax.ShapeDtypeStruct((rows, cols), F32),
-        ),
-        in_specs=[smem] + [vmem] * 4,
-        out_specs=(vmem,) * 4,
-        scratch_shapes=[pltpu.VMEM((LZ + 1, XR, YR), F32)],
-        compiler_params=params(),
-        name="wind",
-    )(block, moments, basis, grid.reshape(cols // 128, rows * NF, 128), terrain_mask)
-
-    speed_mean = (speed + swapped(speed, "gz", 1)) / 32.0
-    lags = jnp.asarray(LAGS, F32)[:, None, None]
-    decay_rate = jnp.exp(-(1.0 + 0.5 * speed_mean)[None] / lags)
-    fuel_moisture = fuel_start
-    for hour in range(PASSES):
-        goal = balance + 0.3 * math.cos(2.0 * math.pi * hour / 24.0)
-        fuel_moisture = goal + (fuel_moisture - goal) * decay_rate
+        "wind",
+        [
+            ((layers, rows, cols), F32),
+            ((3, layers, rows, cols), F32),
+            ((rows, cols), F32),
+            ((rows, cols), F32),
+        ],
+        [
+            block,
+            moments,
+            basis,
+            edge.reshape(halves, 8 * NF, 128),
+            middle.reshape(halves, (rows - 8) * NF, 128),
+            terrain_mask,
+        ],
+        scratch=[((LZ + 1, XR, YR), F32), ((halves, rows * NF, 128), F32)],
+        in_smem=1,
+    )
+    (fuel_moisture,) = kernel(
+        fuel_kernel,
+        "fuel",
+        [((len(LAGS), rows, cols), F32)],
+        [speed, swapped(speed, "gz", 1), balance, fuel_start],
+    )
     return (potential, wind_field, fuel_moisture)
 
 

time: 143 us -> 118 us (0.83)
  blocking collectives: 0 us -> 62.8 us
  starting transfers between devices: 52.9 us -> 12.1 us
  waiting for transfers between devices: 39.9 us -> 2.97 us
  other arithmetic: 4.96 us -> 0.65 us
  Pallas kernels: 36.8 us -> 34.1 us
  local copies, waits for them, and re-layouts: 5.59 us -> 3.63 us
    all_to_all x0 -> x2, blocking collectives: none -> 62.8 us  [the longest x1 33.4 us: shards(): lax.all_to_all(outgoing.reshape(tiles, capacity, 128), ('gx', 'gy'), spli...]
    ppermute x11 -> x3, starting transfers between devices: 25.4 us -> 4.05 us  [swapped(): return lax.ppermute(block, axis, [(i, i ^ bit) for i in range(count)])]
    all_to_all x1 -> x0, waiting for transfers between devices: 17.4 us -> none  [shards(): lax.all_to_all(outgoing.reshape(tiles, capacity, 128), ('gx', 'gy'), spli...]
    ppermute x11 -> x3, waiting for transfers between devices: 18.8 us -> 1.82 us  [swapped(): return lax.ppermute(block, axis, [(i, i ^ bit) for i in range(count)])]
    all_to_all x1 -> x0, starting transfers between devices: 13.8 us -> none  [shards(): lax.all_to_all(outgoing.reshape(tiles, capacity, 128), ('gx', 'gy'), spli...]
    ppermute x6 -> x4, starting transfers between devices: 13.8 us -> 8.03 us  [shifted(): return lax.ppermute(block, axis, pairs)]
    add x10 -> x0, other arithmetic: 2.83 us -> none  [the longest x1 0.77 us: shards(): goal = balance + 0.3 * math.cos(2.0 * math.pi * hour / 24.0)]
    pallas_call x5 -> x7, Pallas kernels: 36.8 us -> 34.1 us  [kernel(): pl.pallas_call(body, out_shape=tuple(shapes), in_specs=[smem] * in_smem +...]
  transfers between devices with their start and end apart: 18 -> 7, of which waited for: 14 -> 3; matrix products, arithmetic and copies ran while one was open for 1% -> 1% of each run, Pallas kernels for 0% -> 10%
where the time goes in v2:
time: 118 us
  blocking collectives  62.8 us (53%)
  Pallas kernels  34.1 us (29%)
  starting transfers between devices  12.1 us (10%)
  local copies, waits for them, and re-layouts  3.63 us (3%)
  waiting for transfers between devices  2.97 us (3%)
  between operations  1.38 us (1%)
    pallas_call x7, Pallas kernels, kernel(): pl.pallas_call(body, out_shape=tuple(shapes), in_specs=[smem] * in_smem +...  34.1 us
    all_to_all x1, blocking collectives, shards(): lax.all_to_all(outgoing.reshape(tiles, capacity, 128), ('gx', 'gy'), spli...  33.4 us
    all_to_all x1, blocking collectives, shards(): lax.all_to_all(moments, ('gx', 'gy', 'gz'), split_axis=0, concat_axis=0,...  29.4 us
    ppermute x4, starting transfers between devices, shifted(): return lax.ppermute(block, axis, pairs)  8.03 us
    ppermute x3, starting transfers between devices, swapped(): return lax.ppermute(block, axis, [(i, i ^ bit) for i in range(count)])  4.05 us
  transfers between devices with their start and end apart: 7, of which 3 were waited for; matrix products, arithmetic and copies ran while one was open for 1% of the time, Pallas kernels for 10%

profile of v2, /device:TPU:1, one launch (start us, length us, event | category | flops | bytes accessed | tf_op | source)
XLA Modules:
  0.0 117.7 jit_solution(12929583332236031939)
XLA Ops:
  0.6 1.0 slice.37
  1.6 3.3 %collective-permute-start.1 = (s32[8,32,256]{2,1,0:T(8,128)S(1)}, s32[8,32,256]{2,1,0:T(8,128)S(1)}, u32[]{:S(2)}, u32[]{:S(2)}) collective-permute-start(s32[8,32,256]{2,1,0:T(8,128)S(1)} %slice.37), channel_id=1, source_target_pairs={{0,1},{1,0},{2,3},{3,2},{4,5},{5,4},{6,7},{7,6},{8,9},{9,8},{10,11... | collective-permute-start | bytes 786440 | tf_op jit(solution)/shard_map/ppermute | solution.py:512
  4.9 0.7 pad_add_fusion.block_ref
  5.6 2.1 %profile.1 = (f32[40,1024]{1,0:T(8,128)}, f32[8,1024]{1,0:T(8,128)}) custom-call(s32[3]{0:T(128)} %pad_add_fusion.block_ref, f32[16,32]{1,0:T(8,128)} %weights_ref.1, f32[1024,128]{1,0:T(8,128)} %bitcast.23), custom_call_target="tpu_custom_call" | custom-call | tf_op jit(solution)/shard_map/profile/pallas_call | solution.py:538
  7.7 0.0 collective-permute-start
  8.4 0.7 collective-permute-done.other_ref
  9.1 0.6 copy-done.5
  9.7 2.8 %route.1 = f32[1024,128]{1,0:T(8,128)} custom-call(s32[1]{0:T(128)S(6)} %copy.15.live_ref, s32[1,1024]{1,0:T(1,128)} %owner_ref.1, f32[40,1024]{1,0:T(8,128)} %get-tuple-element.44.own_ref, f32[8,1024]{1,0:T(8,128)} %copy-done.5), custom_call_target="tpu_custom_call" | custom-call | tf_op jit(solution)/shard_map/route/pallas_call | solution.py:538
  12.6 0.0 collective-permute-done.1
  12.6 33.4 %all_to_all.16 = f32[128,8,128]{2,1,0:T(8,128)} all-to-all(f32[128,8,128]{2,1,0:T(8,128)} %bitcast.17), channel_id=1, replica_groups=mesh['gx'=16,'gy'=8,'gz'=2] {'gx','gy'}, dimensions={0} | all-to-all | bytes 1048576 | tf_op jit(solution)/shard_map/all_to_all | solution.py:567
  46.0 4.3 %edge.1 = (bf16[160,512]{1,0:T(8,128)(2,1)}, f32[2,8,40,128]{3,2,1,0:T(8,128)}, f32[56,128]{1,0:T(8,128)}, f32[56,128]{1,0:T(8,128)}, f32[248,256]{1,0:T(8,128)}, /*index=5*/f32[248,256]{1,0:T(8,128)}) custom-call(s32[3]{0:T(128)} %pad_add_fusion.block_ref, f32[1024,128]{1,0:T(8,128)} %bitcast.18, s32[4,32,256]{2,1,0:T(8,128)} %index_ref.3, ...), custom_call_target="tpu_custom_call" | custom-call | tf_op jit(solution)/shard_map/edge/pallas_call | solution.py:538
  50.4 1.3 %collective-permute-start.2 = (f32[56,128]{1,0:T(8,128)}, f32[56,128]{1,0:T(8,128)S(1)}, u32[]{:S(2)}, u32[]{:S(2)}) collective-permute-start(f32[56,128]{1,0:T(8,128)} %get-tuple-element.51), channel_id=1, source_target_pairs={{2,0},{4,2},{6,4},{8,6},{10,8},{12,10},{14,12},{3,1},{5,3},{7,5},{... | collective-permute-start | bytes 86024 | tf_op jit(solution)/shard_map/ppermute | solution.py:507
  51.6 4.0 %collective-permute-start.3 = (f32[56,128]{1,0:T(8,128)}, f32[56,128]{1,0:T(8,128)S(1)}, u32[]{:S(2)}, u32[]{:S(2)}) collective-permute-start(f32[56,128]{1,0:T(8,128)} %get-tuple-element.52), channel_id=1, source_target_pairs={{0,2},{2,4},{4,6},{6,8},{8,10},{10,12},{12,14},{1,3},{3,5},{5,7},{... | collective-permute-start | bytes 86024 | tf_op jit(solution)/shard_map/ppermute | solution.py:507
  55.6 0.0 collective-permute-done.2.right_ref
  55.6 0.0 copy-start.3
  55.7 1.1 collective-permute-done.3.left_ref
  56.8 0.7 constant_dynamic-update-slice_fusion.2
  57.5 1.3 %collective-permute-start.5 = (f32[248,256]{1,0:T(8,128)}, f32[248,256]{1,0:T(8,128)S(1)}, u32[]{:S(2)}, u32[]{:S(2)}) collective-permute-start(f32[248,256]{1,0:T(8,128)} %get-tuple-element.61), channel_id=1, source_target_pairs={{0,16},{16,32},{32,48},{48,64},{64,80},{80,96},{96,112},{112,128},... | collective-permute-start | bytes 761864 | tf_op jit(solution)/shard_map/ppermute | solution.py:507
  58.8 1.5 %collective-permute-start.4 = (f32[248,256]{1,0:T(8,128)}, f32[248,256]{1,0:T(8,128)S(1)}, u32[]{:S(2)}, u32[]{:S(2)}) collective-permute-start(f32[248,256]{1,0:T(8,128)} %get-tuple-element.62), channel_id=1, source_target_pairs={{16,0},{32,16},{48,32},{64,48},{80,64},{96,80},{112,96},{128,112},... | collective-permute-start | bytes 761864 | tf_op jit(solution)/shard_map/ppermute | solution.py:507
  60.3 6.8 %middle.1.middle_ref = f32[2,24,40,128]{3,2,1,0:T(8,128)} custom-call(bf16[160,512]{1,0:T(8,128)(2,1)} %get-tuple-element.50.table_ref, s32[4,32,256]{2,1,0:T(8,128)} %index_ref.3, f32[4,32,256]{2,1,0:T(8,128)} %weight_ref.3), custom_call_target="tpu_custom_call" | custom-call | flops 4000000000 | bytes 1600000 | tf_op jit(solution)/shard_map/middle/pallas_call | solution.py:538
  67.1 0.0 collective-permute-done.5.below_ref
  67.1 0.0 collective-permute-done.4.above_ref
  67.1 0.0 copy-start.2
  67.1 0.7 copy-done.1
  67.8 0.1 copy-done.2
  67.9 11.7 %basis.1 = (f32[3,17,40,384]{3,2,1,0:T(8,128)}, f32[256,128]{1,0:T(8,128)}) custom-call(s32[3]{0:T(128)} %pad_add_fusion.block_ref, f32[2,8,40,128]{3,2,1,0:T(8,128)} %get-tuple-element.49.edge_ref, f32[2,24,40,128]{3,2,1,0:T(8,128)} %middle.1.middle_ref, s32[512,256]{1,0:T(8,128)} %bitcast.15, s32[256,256]{1,0:T(8,128)} %bitcast.21, f32[56,128]{1,0:T(8,128)} %copy-done.3, ...), custom_call_target="tpu_custom_call" | custom-call | tf_op jit(solution)/shard_map/basis/pallas_call | solution.py:538
  79.6 29.4 %all_to_all.17 = f32[256,1,128]{2,1,0:T(1,128)} all-to-all(f32[256,1,128]{2,1,0:T(1,128)} %bitcast.24), channel_id=1, replica_groups=mesh['gx'=16,'gy'=8,'gz'=2] {'gx','gy','gz'}, dimensions={0} | all-to-all | bytes 262144 | tf_op jit(solution)/shard_map/all_to_all | solution.py:615
  108.9 4.7 %wind.1 = (f32[16,32,256]{2,1,0:T(8,128)}, f32[3,16,32,256]{3,2,1,0:T(8,128)}, f32[32,256]{1,0:T(8,128)}, f32[32,256]{1,0:T(8,128)}) custom-call(s32[3]{0:T(128)} %pad_add_fusion.block_ref, f32[256,128]{1,0:T(8,128)} %bitcast.22, f32[3,17,40,384]{3,2,1,0:T(8,128)} %get-tuple-element.56.basis_ref, f32[2,320,128]{2,1,0:T(8,128)} %bitcast.19, ...), custom_call_target="tpu_custom_call" | custom-call | tf_op jit(solution)/shard_map/wind/pallas_call | solution.py:538
  113.6 0.7 collective-permute-start.6
  114.3 1.1 collective-permute-done.6.other_ref
  115.4 0.6 copy-done.6
  116.0 1.7 %fuel.1 = f32[3,32,256]{2,1,0:T(8,128)} custom-call(f32[32,256]{1,0:T(8,128)} %get-tuple-element.59.speed_ref, f32[32,256]{1,0:T(8,128)} %copy-done.6, f32[32,256]{1,0:T(8,128)} %get-tuple-element.60.balance_ref, f32[3,32,256]{2,1,0:T(8,128)} %start_ref.1), custom_call_target="tpu_custom_call" | custom-call | tf_op jit(solution)/shard_map/fuel/pallas_call | solution.py:538
  (10 shorter events, 0.0 us)
Async XLA Ops:
  1.6 11.0 %collective-permute-start.1 = (s32[8,32,256]{2,1,0:T(8,128)S(1)}, s32[8,32,256]{2,1,0:T(8,128)S(1)}, u32[]{:S(2)}, u32[]{:S(2)}) collective-permute-start(s32[8,32,256]{2,1,0:T(8,128)S(1)} %slice.37), channel_id=1, source_target_pairs={{0,1},{1,0},{2,3},{3,2},{4,5},{5,4},{6,7},{7,6},{8,9},{9,8},{10,11... | collective-permute-start | bytes 786440 | tf_op jit(solution)/shard_map/ppermute | solution.py:512
  7.7 1.4 %collective-permute-start = (f32[8,1024]{1,0:T(8,128)}, f32[8,1024]{1,0:T(8,128)S(1)}, u32[]{:S(2)}, u32[]{:S(2)}) collective-permute-start(f32[8,1024]{1,0:T(8,128)} %get-tuple-element.45), channel_id=1, source_target_pairs={{0,1},{1,0},{2,3},{3,2},{4,5},{5,4},{6,7},{7,6},{8,9},{9,8},{10,11... | collective-permute-start | bytes 98312 | tf_op jit(solution)/shard_map/ppermute | solution.py:512
  9.1 0.6 copy-start.5
  12.6 33.4 %copy-start = (s32[8,32,256]{2,1,0:T(8,128)}, s32[8,32,256]{2,1,0:T(8,128)S(1)}, u32[]{:S(2)}) copy-start(s32[8,32,256]{2,1,0:T(8,128)S(1)} %collective-permute-done.1) | copy-start | bytes 786436
  50.4 5.3 %collective-permute-start.2 = (f32[56,128]{1,0:T(8,128)}, f32[56,128]{1,0:T(8,128)S(1)}, u32[]{:S(2)}, u32[]{:S(2)}) collective-permute-start(f32[56,128]{1,0:T(8,128)} %get-tuple-element.51), channel_id=1, source_target_pairs={{2,0},{4,2},{6,4},{8,6},{10,8},{12,10},{14,12},{3,1},{5,3},{7,5},{... | collective-permute-start | bytes 86024 | tf_op jit(solution)/shard_map/ppermute | solution.py:507
  51.6 5.2 %collective-permute-start.3 = (f32[56,128]{1,0:T(8,128)}, f32[56,128]{1,0:T(8,128)S(1)}, u32[]{:S(2)}, u32[]{:S(2)}) collective-permute-start(f32[56,128]{1,0:T(8,128)} %get-tuple-element.52), channel_id=1, source_target_pairs={{0,2},{2,4},{4,6},{6,8},{8,10},{10,12},{12,14},{1,3},{3,5},{5,7},{... | collective-permute-start | bytes 86024 | tf_op jit(solution)/shard_map/ppermute | solution.py:507
  55.6 11.5 %copy-start.3 = (f32[56,128]{1,0:T(8,128)}, f32[56,128]{1,0:T(8,128)S(1)}, u32[]{:S(2)}) copy-start(f32[56,128]{1,0:T(8,128)S(1)} %collective-permute-done.2.right_ref) | copy-start | bytes 86020
  56.8 10.3 %copy-start.4 = (f32[56,128]{1,0:T(8,128)}, f32[56,128]{1,0:T(8,128)S(1)}, u32[]{:S(2)}) copy-start(f32[56,128]{1,0:T(8,128)S(1)} %collective-permute-done.3.left_ref) | copy-start | bytes 86020
  57.5 9.6 %collective-permute-start.5 = (f32[248,256]{1,0:T(8,128)}, f32[248,256]{1,0:T(8,128)S(1)}, u32[]{:S(2)}, u32[]{:S(2)}) collective-permute-start(f32[248,256]{1,0:T(8,128)} %get-tuple-element.61), channel_id=1, source_target_pairs={{0,16},{16,32},{32,48},{48,64},{64,80},{80,96},{96,112},{112,128},... | collective-permute-start | bytes 761864 | tf_op jit(solution)/shard_map/ppermute | solution.py:507
  58.8 8.3 %collective-permute-start.4 = (f32[248,256]{1,0:T(8,128)}, f32[248,256]{1,0:T(8,128)S(1)}, u32[]{:S(2)}, u32[]{:S(2)}) collective-permute-start(f32[248,256]{1,0:T(8,128)} %get-tuple-element.62), channel_id=1, source_target_pairs={{16,0},{32,16},{48,32},{64,48},{80,64},{96,80},{112,96},{128,112},... | collective-permute-start | bytes 761864 | tf_op jit(solution)/shard_map/ppermute | solution.py:507
  67.1 0.7 copy-start.1
  67.1 0.8 copy-start.2
  113.6 1.8 %collective-permute-start.6 = (f32[32,256]{1,0:T(8,128)}, f32[32,256]{1,0:T(8,128)S(1)}, u32[]{:S(2)}, u32[]{:S(2)}) collective-permute-start(f32[32,256]{1,0:T(8,128)} %get-tuple-element.59.speed_ref), channel_id=1, source_target_pairs={{0,1},{1,0},{2,3},{3,2},{4,5},{5,4},{6,7},{7,6},{8,9},{9,8},{10,11... | collective-permute-start | bytes 98312 | tf_op jit(solution)/shard_map/ppermute | solution.py:512
  115.4 0.6 copy-start.6

commit v3 on v2

--- a/solution.py
+++ b/solution.py
@@ -36,10 +36,10 @@
     return lax.dot_general(a, b, (((1,), (1,)), ((), ())), preferred_element_type=F32)
 
 
-def profile_kernel(block_ref, weights_ref, columns_ref, own_ref, send_ref):
+def profile_kernel(gz_ref, weights_ref, columns_ref, own_ref, send_ref):
     plain = weights_ref[...]
     turned = jnp.concatenate([plain[LZ - 1 - i : LZ - i] for i in range(LZ)], axis=0)
-    weights = jnp.where(block_ref[2] == 0, plain, turned)
+    weights = jnp.where(gz_ref[0] == 0, plain, turned)
     total = jnp.sum(plain, axis=0, keepdims=True)
     edge = jnp.concatenate([weights[LZ - 1 - i : LZ - i] for i in range(DEEP)], axis=0)
 
@@ -64,7 +64,8 @@
 
 def route_kernel(live_ref, owner_ref, own_ref, other_ref, out_ref, *, tiles, capacity):
     rows = owner_ref.shape[1]
-    slots = out_ref.shape[0]
+    slots = tiles * capacity
+    half = capacity // 2
     position = lax.broadcasted_iota(jnp.int32, (1, rows), 1)
     owner = jnp.where(position < live_ref[0], owner_ref[...], -1)
     matches = lax.broadcasted_iota(jnp.int32, (tiles, rows), 0) == owner
@@ -76,39 +77,56 @@
         hits.astype(BF16), jnp.where(earlier, 1.0, 0.0).astype(BF16), preferred_element_type=F32
     )
     rank = jnp.sum(hits * before, axis=0, keepdims=True).astype(jnp.int32)
-    target = jnp.where(owner >= 0, owner * capacity + rank, -1)
+    upper = jnp.where(rank >= half, 1, 0)
+    target = jnp.where(owner >= 0, owner * half + rank + upper * (slots // 2 - half), -1)
     place = lax.broadcasted_iota(jnp.int32, (slots, rows), 0) == target
     profile = jnp.concatenate([own_ref[: NF - 8], own_ref[NF - 8 :] + other_ref[...]], axis=0)
     high, low = split(profile)
     pad = jnp.zeros((64 - NF, rows), BF16)
     both = jnp.concatenate([high, pad, low, pad], axis=0)
-    out_ref[...] = dot_nt(jnp.where(place, 1.0, 0.0).astype(BF16), both)
+    placed = dot_nt(jnp.where(place, 1.0, 0.0).astype(BF16), both)
+    placed = placed + pltpu.roll(placed, 64, 1)
+    lane = lax.broadcasted_iota(jnp.int32, (slots // 2, 128), 1)
+    out_ref[...] = jnp.where(lane < 64, placed[: slots // 2], placed[slots // 2 :])
 
 
 def fill_table(received_ref, table_ref):
-    parts = received_ref.shape[0] // 256
-    turned = [jnp.transpose(received_ref[256 * p : 256 * p + 256, :]) for p in range(parts)]
+    blocks = received_ref.shape[0] // 256
+    turned = [jnp.transpose(received_ref[256 * p : 256 * p + 256, :]) for p in range(blocks)]
+    parts = 2 * blocks
     for g in range(NF // 8):
-        for half, start in ((0, 0), (1, 64)):
-            rows = slice(start + 8 * g, start + 8 * g + 8)
-            value = jnp.concatenate([turned[p][rows] for p in range(parts)], axis=0)
-            table_ref[8 * parts * g : 8 * parts * (g + 1), 256 * half : 256 * half + 256] = (
-                value.astype(BF16)
-            )
-
-
-def pick_columns(table_ref, index, weight):
+        value = jnp.concatenate(
+            [
+                turned[p][64 * side + 8 * g : 64 * side + 8 * g + 8]
+                for side in range(2)
+                for p in range(blocks)
+            ],
+            axis=0,
+        )
+        rows = slice(8 * parts * g, 8 * parts * (g + 1))
+        table_ref[rows, 0:256], table_ref[rows, 256:512] = split(value)
+
+
+def place_of(slot, capacity):
+    half = capacity // 2
+    bits = half.bit_length() - 1
+    row = ((slot >> (bits + 1)) << bits) | (slot & (half - 1))
+    return row, (slot >> bits) & 1
+
+
+def pick_columns(table_ref, index, weight, capacity):
     parts = table_ref.shape[0] // NF
     total = weight[0] + weight[1] + weight[2] + weight[3]
     slot = lax.broadcasted_iota(jnp.int32, (256, 256), 0).astype(F32).astype(BF16)
     acc = [None] * (NF // 8)
     for point in range(len(index)):
-        low = jnp.broadcast_to((index[point] & 255).astype(F32), (16, 256)).astype(BF16)
+        row, side = place_of(index[point], capacity)
+        low = jnp.broadcast_to((row & 255).astype(F32), (16, 256)).astype(BF16)
         low = jnp.concatenate([low] * 16, axis=0)
         chosen = jnp.where(slot == low, jnp.ones((256, 256), BF16), jnp.zeros((256, 256), BF16))
         chosen = jnp.concatenate([chosen, chosen], axis=0)
         found = jnp.dot(table_ref[...], chosen, preferred_element_type=F32)
-        part = jnp.broadcast_to(index[point] >> 8, (8, 256))
+        part = jnp.broadcast_to((row >> 8) + side * (parts // 2), (8, 256))
         share = jnp.broadcast_to(weight[point] / total, (8, 256))
         for g in range(NF // 8):
             values = [
@@ -126,32 +144,52 @@
     return acc
 
 
-def pick_rows(table_ref, index_ref, weight_ref, first, steps, out_ref, base):
+def pick_rows(table_ref, index_ref, weight_ref, chosen, out_ref, capacity):
     points, _, cols = index_ref.shape
-    index = [index_ref[k, pl.ds(first, 8), :] for k in range(points)]
-    weight = [weight_ref[k, pl.ds(first, 8), :] for k in range(points)]
-    for j in steps:
+    for at, x in enumerate(chosen):
         got = pick_columns(
-            table_ref, [value[j : j + 1] for value in index], [value[j : j + 1] for value in weight]
+            table_ref,
+            [index_ref[k, x : x + 1, :] for k in range(points)],
+            [weight_ref[k, x : x + 1, :] for k in range(points)],
+            capacity,
         )
         for g in range(NF // 8):
             for h in range(cols // 128):
-                out_ref[h, base + j, 8 * g : 8 * g + 8, :] = got[g][:, 128 * h : 128 * h + 128]
-
-
-def edge_kernel(
-    block_ref, received_ref, index_ref, weight_ref, mask_ref, far_mask_ref,
-    table_ref, edge_ref, low_y_ref, high_y_ref, low_x_ref, high_x_ref, mask_f_ref
-):
-    lower = block_ref[2] == 0
-    points, rows, cols = index_ref.shape
-    fill_table(received_ref, table_ref)
-    for h in range(cols // 128):
+                out_ref[h, at, 8 * g : 8 * g + 8, :] = got[g][:, 128 * h : 128 * h + 128]
+
+
+def mask_kernel(gz_ref, mask_ref, far_mask_ref, mask_y_ref, mask_x_ref, mask_f_ref):
+    lower = gz_ref[0] == 0
+    halves = mask_f_ref.shape[0]
+    rows = mask_f_ref.shape[1] // LZ
+    cols = 128 * halves
+    lane = lax.broadcasted_iota(jnp.int32, (8, 128), 1)
+    for h in range(halves):
         at = slice(128 * h, 128 * h + 128)
         near = mask_ref[0 : 8 * rows, at]
         mask_f_ref[h, 0 : 8 * rows] = jnp.where(lower, near, far_mask_ref[:, at]).astype(F32)
         mask_f_ref[h, 8 * rows :] = mask_ref[8 * rows :, at].astype(F32)
-
+    for side, start, turn in ((0, 0, 0), (1, cols - 128, 4)):
+        for g in range(LZ // 8):
+            total = None
+            for x in range(rows):
+                value = mask_f_ref[start // 128, pl.ds(x + g * 8 * rows, 8, stride=rows), :]
+                value = pltpu.roll(value, (4 * x + turn) % 128, 1)
+                total = value if total is None else jnp.where((lane >> 2) == x, value, total)
+            mask_y_ref[side, 8 * g : 8 * g + 8] = total
+            for d in range(3):
+                x = d if side == 0 else rows - 1 - d
+                for h in range(halves):
+                    mask_x_ref[
+                        side, LZ * d + 8 * g : LZ * d + 8 * g + 8, 128 * h : 128 * h + 128
+                    ] = mask_f_ref[h, pl.ds(x + g * 8 * rows, 8, stride=rows), :]
+
+
+def table_kernel(
+    received_ref, index_ref, weight_ref, mask_y_ref, table_ref, low_y_ref, high_y_ref, *, capacity
+):
+    points, rows, cols = index_ref.shape
+    fill_table(received_ref, table_ref)
     lane = lax.broadcasted_iota(jnp.int32, (8, 128), 1)
     row = lax.broadcasted_iota(jnp.int32, (8, 128), 0)
 
@@ -171,48 +209,43 @@
         table_ref,
         [packed(index_ref, k) for k in range(points)],
         [packed(weight_ref, k) for k in range(points)],
-    )
-    for out, start, turn in ((low_y_ref, 0, 0), (high_y_ref, cols - 128, 4)):
-        half = 0 if start == 0 else 1
+        capacity,
+    )
+    for side, out in ((0, low_y_ref), (1, high_y_ref)):
         for g in range(NF // 8):
-            out[8 * g : 8 * g + 8] = got[g][:, 128 * half : 128 * half + 128]
-        for g in range(LZ // 8):
-            total = None
-            for x in range(rows):
-                value = mask_f_ref[start // 128, pl.ds(x + g * 8 * rows, 8, stride=rows), :]
-                value = pltpu.roll(value, (4 * x + turn) % 128, 1)
-                total = value if total is None else jnp.where((lane >> 2) == x, value, total)
-            out[NF + 8 * g : NF + 8 * g + 8] = total
-
-    pick_rows(table_ref, index_ref, weight_ref, 0, range(4), edge_ref, 0)
-    pick_rows(table_ref, index_ref, weight_ref, rows - 8, range(4, 8), edge_ref, 0)
+            out[8 * g : 8 * g + 8] = got[g][:, 128 * side : 128 * side + 128]
+        out[NF:] = mask_y_ref[side]
+
+
+def edge_kernel(
+    table_ref, index_ref, weight_ref, mask_x_ref, edge_ref, low_x_ref, high_x_ref, *, capacity
+):
+    _, rows, cols = index_ref.shape
+    chosen = [0, 1, 2, 3] + [rows - 4 + j for j in range(4)]
+    pick_rows(table_ref, index_ref, weight_ref, chosen, edge_ref, capacity)
     for d in range(4):
-        for out, x, kept in ((low_x_ref, d, d), (high_x_ref, rows - 1 - d, 7 - d)):
+        for side, out, kept in ((0, low_x_ref, d), (1, high_x_ref, 7 - d)):
             for h in range(cols // 128):
                 at = slice(128 * h, 128 * h + 128)
                 if d < 3:
                     out[NS * d : NS * d + NF, at] = edge_ref[h, kept]
-                    for g in range(LZ // 8):
-                        first = NS * d + NF + 8 * g
-                        out[first : first + 8, at] = mask_f_ref[
-                            h, pl.ds(x + g * 8 * rows, 8, stride=rows), :
-                        ]
+                    out[NS * d + NF : NS * d + NS, at] = mask_x_ref[side, LZ * d : LZ * d + LZ, at]
                 else:
                     out[NS * 3 : NS * 3 + 16, at] = edge_ref[h, kept, 0:16]
                     out[NS * 3 + 16 : NS * 3 + 24, at] = edge_ref[h, kept, 32:40]
 
 
-def middle_kernel(table_ref, index_ref, weight_ref, middle_ref):
-    rows = index_ref.shape[1]
-    pick_rows(table_ref, index_ref, weight_ref, 0, range(4, 8), middle_ref, -4)
-
-    def body(group, carry):
-        first = pl.multiple_of(8 * group, 8)
-        pick_rows(table_ref, index_ref, weight_ref, first, range(8), middle_ref, first - 4)
-        return carry
-
-    lax.fori_loop(1, rows // 8 - 1, body, 0)
-    pick_rows(table_ref, index_ref, weight_ref, rows - 8, range(4), middle_ref, rows - 12)
+def middle_kernel(table_ref, index_ref, weight_ref, middle_ref, *, first, capacity):
+    chosen = list(range(first, first + 8))
+    pick_rows(table_ref, index_ref, weight_ref, chosen, middle_ref, capacity)
+
+
+def holder(x, rows, edge_ref, middle_refs):
+    if x < 4:
+        return edge_ref, x
+    if x >= rows - 4:
+        return edge_ref, x - rows + 8
+    return middle_refs[(x - 4) // 8], (x - 4) % 8
 
 
 def ring_smooth(plane):
@@ -221,39 +254,28 @@
 
 
 def basis_kernel(
-    block_ref, edge_ref, middle_ref, mask_ref, far_mask_ref,
+    gx_ref, gy_ref, gz_ref, edge_ref, middle_0_ref, middle_1_ref, middle_2_ref, mask_ref, far_mask_ref,
     right_ref, left_ref, above_ref, below_ref,
     basis_ref, moments_ref,
     ext_ref, source_ref, air_ref, last_ref, *, last_gx, last_gy
 ):
-    gx, gy, gz = block_ref[0], block_ref[1], block_ref[2]
-    lower = gz == 0
-    halves, rows = middle_ref.shape[0], middle_ref.shape[1] + 8
+    gx, gy = gx_ref[0], gy_ref[0]
+    lower = gz_ref[0] == 0
+    halves, rows = edge_ref.shape[0], mask_ref.shape[0] // LZ
     cols = 128 * halves
     lane = lax.broadcasted_iota(jnp.int32, (8, 128), 1)
 
-    for h in range(halves):
-        for j in range(8):
-            x = j if j < 4 else rows - 8 + j
-            ext_ref[h, NS * x : NS * x + NF] = edge_ref[h, j]
-
-    def middle_row(x, carry):
+    for x in range(rows):
+        held_ref, j = holder(x, rows, edge_ref, (middle_0_ref, middle_1_ref, middle_2_ref))
         for h in range(halves):
-            ext_ref[h, pl.ds(pl.multiple_of(x * NS, 8), NF), :] = middle_ref[h, x - 4]
-        return carry
-
-    lax.fori_loop(4, rows - 4, middle_row, 0)
-
-    def own_row(x, carry):
+            ext_ref[h, NS * x : NS * x + NF] = held_ref[h, j]
         for g in range(NS // 8):
             at = slice(8 * g, 8 * g + 8)
-            right = pltpu.roll(right_ref[at], (128 - 4 * x) & 127, 1)
-            left = pltpu.roll(left_ref[at], (124 - 4 * x) & 127, 1)
+            right = pltpu.roll(right_ref[at], (128 - 4 * x) % 128, 1)
+            left = pltpu.roll(left_ref[at], (124 - 4 * x) % 128, 1)
             side = jnp.where(lane < 4, right, jnp.where(lane >= 124, left, 0.0))
-            ext_ref[halves, pl.ds(pl.multiple_of(x * NS + 8 * g, 8), 8), :] = side
-        return carry
-
-    lax.fori_loop(0, rows, own_row, 0)
+            ext_ref[halves, NS * x + 8 * g : NS * x + 8 * g + 8] = side
+
     for d in range(4):
         for near_ref, ring, origin in (
             (above_ref, rows + d, d),
@@ -276,14 +298,12 @@
                 side = jnp.where(lane < 4, right, jnp.where(lane >= 124, left, 0.0))
                 ext_ref[halves, base + 8 * g : base + 8 * g + 8] = side
 
-    def source_row(x, carry):
-        here = pl.multiple_of(x * NS, 8)
-        after = pl.multiple_of(jnp.where(x == XR - 1, 0, x + 1) * NS, 8)
-        prior = pl.multiple_of(jnp.where(x == 0, XR - 1, x - 1) * NS, 8)
+    def source_row(x):
+        here, after, prior = x * NS, (x + 1) % XR * NS, (x - 1) % XR * NS
 
         def row_of(start, f):
             return jnp.concatenate(
-                [ext_ref[h, pl.ds(start + f, 8), :] for h in range(halves + 1)], axis=1
+                [ext_ref[h, start + f : start + f + 8, :] for h in range(halves + 1)], axis=1
             )
 
         def east(f):
@@ -293,7 +313,7 @@
             value = row_of(here, f)
             return pltpu.roll(value, YR - 1, 1) - pltpu.roll(value, 1, 1)
 
-        out = pl.multiple_of(x * 24, 8)
+        out = x * 24
         values = (
             0.5 * east(0) + 0.5 * north(16),
             0.5 * east(8) + 0.5 * north(24),
@@ -301,10 +321,12 @@
         )
         for g, value in enumerate(values):
             for h in range(halves + 1):
-                source_ref[h, pl.ds(out + 8 * g, 8), :] = value[:, 128 * h : 128 * h + 128]
-        return carry
-
-    lax.fori_loop(0, XR, source_row, 0)
+                source_ref[h, out + 8 * g : out + 8 * g + 8, :] = value[
+                    :, 128 * h : 128 * h + 128
+                ]
+
+    for x in range(XR):
+        source_row(x)
 
     row_id = lax.broadcasted_iota(jnp.int32, (XR, YR), 0)
     col_id = lax.broadcasted_iota(jnp.int32, (XR, YR), 1)
@@ -424,15 +446,16 @@
 
 
 def wind_kernel(
-    block_ref, moments_ref, basis_ref, edge_ref, middle_ref, mask_ref,
+    gz_ref, moments_ref, basis_ref, edge_ref, middle_0_ref, middle_1_ref, middle_2_ref, mask_ref,
     potential_ref, wind_ref, speed_ref, balance_ref, p_ref, grid_ref
 ):
-    gz = block_ref[2]
+    gz = gz_ref[0]
     rows, cols = speed_ref.shape
     near = 4 * NF
     for h in range(cols // 128):
         grid_ref[h, 0:near] = edge_ref[h, 0:near]
-        grid_ref[h, near : (rows - 4) * NF] = middle_ref[h]
+        for i, held_ref in enumerate((middle_0_ref, middle_1_ref, middle_2_ref)):
+            grid_ref[h, near + 8 * NF * i : near + 8 * NF * (i + 1)] = held_ref[h]
         grid_ref[h, (rows - 4) * NF :] = edge_ref[h, near:]
     totals = jnp.sum(moments_ref[...], axis=0, keepdims=True)
     factors = iterate([totals[:, k : k + 1] for k in range(6)])
@@ -523,7 +546,7 @@
     fuel_start,
 ):
     gx, gy, gz = (lax.axis_index(a).astype(jnp.int32) for a in ("gx", "gy", "gz"))
-    block = jnp.stack([gx, gy, gz])
+    gx, gy, gz = gx.reshape(1), gy.reshape(1), gz.reshape(1)
     tiles = lax.axis_size(("gx", "gy"))
     rows_in = column_owner.shape[1]
     capacity = rows_in // tiles
@@ -550,51 +573,81 @@
         profile_kernel,
         "profile",
         [((NF, rows_in), F32), ((8, rows_in), F32)],
-        [block, vertical_weights, era5_columns[0]],
+        [gz, vertical_weights, era5_columns[0]],
         in_smem=1,
     )
     other = swapped(leaving, "gz", 1)
     far_mask = swapped(terrain_mask[8:], "gz", 1).reshape(8 * rows, cols)
     near_mask = terrain_mask.reshape(layers * rows, cols)
+    mask_y, mask_x = kernel(
+        mask_kernel,
+        "mask",
+        [((2, LZ, 128), F32), ((2, 3 * LZ, cols), F32)],
+        [gz, near_mask, far_mask],
+        scratch=[((halves, layers * rows, 128), F32)],
+        in_smem=1,
+        cost=pl.CostEstimate(flops=3_000_000, bytes_accessed=3_000_000, transcendentals=0),
+    )
+    other, mask_y, mask_x = lax.optimization_barrier((other, mask_y, mask_x))
     (outgoing,) = kernel(
         functools.partial(route_kernel, tiles=tiles, capacity=capacity),
         "route",
-        [((slots, 128), F32)],
+        [((slots // 2, 128), F32)],
         [live_counts, column_owner, own, other],
         in_smem=1,
     )
-    outgoing, far_mask, block = lax.optimization_barrier((outgoing, far_mask, block))
+    outgoing, far_mask, mask_y, mask_x, gx, gy, gz = lax.optimization_barrier(
+        (outgoing, far_mask, mask_y, mask_x, gx, gy, gz)
+    )
     received = lax.all_to_all(
-        outgoing.reshape(tiles, capacity, 128), ("gx", "gy"), split_axis=0, concat_axis=0, tiled=True
-    ).reshape(slots, 128)
-
-    table, edge, low_y, high_y, low_x, high_x = kernel(
-        edge_kernel,
+        outgoing.reshape(tiles, capacity // 2, 128),
+        ("gx", "gy"),
+        split_axis=0,
+        concat_axis=0,
+        tiled=True,
+    ).reshape(slots // 2, 128)
+
+    def middle(table, first):
+        return kernel(
+            functools.partial(middle_kernel, first=first, capacity=capacity),
+            "middle" + str(first),
+            [((halves, 8, NF, 128), F32)],
+            [table, stencil_index, stencil_weight],
+            cost=pl.CostEstimate(flops=1_500_000_000, bytes_accessed=1_000_000, transcendentals=0),
+        )[0]
+
+    table, low_y, high_y = kernel(
+        functools.partial(table_kernel, capacity=capacity),
+        "table",
+        [((slots // 256 * NF, 512), BF16), ((NS, 128), F32), ((NS, 128), F32)],
+        [received, stencil_index, stencil_weight, mask_y],
+    )
+    right = shifted(low_y, "gy", -1)
+    edge, low_x, high_x = kernel(
+        functools.partial(edge_kernel, capacity=capacity),
         "edge",
         [
-            ((slots // 256 * NF, 512), BF16),
             ((halves, 8, NF, 128), F32),
-            ((NS, 128), F32),
-            ((NS, 128), F32),
             ((STRIP + NS, cols), F32),
             ((STRIP + NS, cols), F32),
         ],
-        [block, received, stencil_index, stencil_weight, near_mask, far_mask],
-        scratch=[((halves, layers * rows, 128), F32)],
-        in_smem=1,
-    )
-    right = shifted(low_y, "gy", -1)
+        [table, stencil_index, stencil_weight, mask_x],
+        cost=pl.CostEstimate(flops=1_500_000_000, bytes_accessed=1_500_000, transcendentals=0),
+    )
+    edge, high_y = lax.optimization_barrier((edge, high_y))
     left = shifted(high_y, "gy", 1)
-    (middle,) = kernel(
-        middle_kernel,
-        "middle",
-        [((halves, rows - 8, NF, 128), F32)],
-        [table, stencil_index, stencil_weight],
-        cost=pl.CostEstimate(flops=4_000_000_000, bytes_accessed=1_600_000, transcendentals=0),
-    )
+    table, right = lax.optimization_barrier((table, right))
+    middle_0 = middle(table, 4)
+    middle_0, low_x, high_x = lax.optimization_barrier((middle_0, low_x, high_x))
     corners = jnp.concatenate([right, left], axis=1)
-    above = shifted(low_x.at[STRIP:].set(corners), "gx", -1)
-    below = shifted(high_x.at[STRIP:].set(corners), "gx", 1)
+    low_x, high_x = low_x.at[STRIP:].set(corners), high_x.at[STRIP:].set(corners)
+    table, low_x, high_x = lax.optimization_barrier((table, low_x, high_x))
+    above = shifted(low_x, "gx", -1)
+    middle_1 = middle(table, 12)
+    middle_1, table, high_x = lax.optimization_barrier((middle_1, table, high_x))
+    below = shifted(high_x, "gx", 1)
+    middle_2 = middle(table, 20)
+    middles = (middle_0, middle_1, middle_2)
 
     devices = tiles * lax.axis_size("gz")
     basis, moments = kernel(
@@ -603,14 +656,14 @@
         ),
         "basis",
         [((3, LZ + 1, XR, YR), F32), ((devices, 128), F32)],
-        [block, edge, middle, near_mask, far_mask, right, left, above, below],
+        [gx, gy, gz, edge, *middles, near_mask, far_mask, right, left, above, below],
         scratch=[
             ((YR // 128, XR * NS, 128), F32),
             ((YR // 128, XR * 24, 128), F32),
             ((LZ + DEEP, XR, YR), F32),
             ((2, DEEP - 1, XR, YR), F32),
         ],
-        in_smem=1,
+        in_smem=3,
     )
     moments = lax.all_to_all(
         moments, ("gx", "gy", "gz"), split_axis=0, concat_axis=0, tiled=True
@@ -625,11 +678,10 @@
             ((rows, cols), F32),
         ],
         [
-            block,
+            gz,
             moments,
             basis,
-            edge.reshape(halves, 8 * NF, 128),
-            middle.reshape(halves, (rows - 8) * NF, 128),
+            *(piece.reshape(halves, 8 * NF, 128) for piece in (edge, *middles)),
             terrain_mask,
         ],
         scratch=[((LZ + 1, XR, YR), F32), ((halves, rows * NF, 128), F32)],

time: 118 us -> 113 us (0.958)
  blocking collectives: 62.8 us -> 54.4 us
  starting transfers between devices: 12.1 us -> 14.9 us
  waiting for transfers between devices: 2.97 us -> 1.09 us
  Pallas kernels: 34.1 us -> 35.8 us
    all_to_all x1, blocking collectives: 33.4 us -> 27.9 us  [shards(): lax.all_to_all(outgoing.reshape(tiles, capacity // 2, 128), ('gx', 'gy'),...]
    ppermute x4, starting transfers between devices: 8.03 us -> 11 us  [shifted(): return lax.ppermute(block, axis, pairs)]
    all_to_all x1, blocking collectives: 29.4 us -> 26.6 us  [shards(): lax.all_to_all(moments, ('gx', 'gy', 'gz'), split_axis=0, concat_axis=0,...]
    pallas_call x7 -> x11, Pallas kernels: 34.1 us -> 35.8 us  [kernel(): pl.pallas_call(body, out_shape=tuple(shapes), in_specs=[smem] * in_smem +...]
    unnamed x15 -> x21, local copies, waits for them, and re-layouts: 2 us -> 3.33 us
  transfers between devices with their start and end apart: 7 -> 7, of which waited for: 3 -> 1; matrix products, arithmetic and copies ran while one was open for 1% -> 0% of each run, Pallas kernels for 10% -> 16%
where the time goes in v3:
time: 113 us; the launch traced here: 112 us
  blocking collectives  54.4 us (48%)
  Pallas kernels  35.8 us (32%)
  starting transfers between devices  14.9 us (13%)
  local copies, waits for them, and re-layouts  4.32 us (4%)
  between operations  1.42 us (1%)
    pallas_call x11, Pallas kernels, kernel(): pl.pallas_call(body, out_shape=tuple(shapes), in_specs=[smem] * in_smem +...  35.8 us
    all_to_all x1, blocking collectives, shards(): lax.all_to_all(outgoing.reshape(tiles, capacity // 2, 128), ('gx', 'gy'),...  27.9 us
    all_to_all x1, blocking collectives, shards(): lax.all_to_all(moments, ('gx', 'gy', 'gz'), split_axis=0, concat_axis=0,...  26.6 us
    ppermute x4, starting transfers between devices, shifted(): return lax.ppermute(block, axis, pairs)  11 us
    ppermute x3, starting transfers between devices, swapped(): return lax.ppermute(block, axis, [(i, i ^ bit) for i in range(count)])  3.95 us
    unnamed x21, local copies, waits for them, and re-layouts  3.33 us
  transfers between devices with their start and end apart: 7, of which 1 were waited for; matrix products, arithmetic and copies ran while one was open for 0% of the time, Pallas kernels for 16%

profile of v3, /device:TPU:1, one launch (start us, length us, event | category | flops | bytes accessed | tf_op | source)
XLA Modules:
  0.0 112.0 jit_solution(7460098790279071145)
XLA Ops:
  0.6 1.0 slice.37
  1.6 3.3 %collective-permute-start.1 = (s32[8,32,256]{2,1,0:T(8,128)S(1)}, s32[8,32,256]{2,1,0:T(8,128)S(1)}, u32[]{:S(2)}, u32[]{:S(2)}) collective-permute-start(s32[8,32,256]{2,1,0:T(8,128)S(1)} %slice.37), channel_id=1, source_target_pairs={{0,1},{1,0},{2,3},{3,2},{4,5},{5,4},{6,7},{7,6},{8,9},{9,8},{10,11... | collective-permute-start | bytes 786440 | tf_op jit(solution)/shard_map/ppermute | solution.py:535
  4.9 2.1 %profile.1 = (f32[40,1024]{1,0:T(8,128)}, f32[8,1024]{1,0:T(8,128)}) custom-call(s32[1]{0:T(128)} %bitcast.gz_ref, f32[16,32]{1,0:T(8,128)} %weights_ref.1, f32[1024,128]{1,0:T(8,128)} %bitcast.27), custom_call_target="tpu_custom_call" | custom-call | tf_op jit(solution)/shard_map/profile/pallas_call | solution.py:561
  7.0 0.0 collective-permute-start
  7.7 0.0 copy-start
  7.7 0.7 copy-done
  8.4 2.1 %mask.1 = (f32[2,16,128]{2,1,0:T(8,128)}, f32[2,48,256]{2,1,0:T(8,128)}) custom-call(s32[1]{0:T(128)} %bitcast.gz_ref, s32[512,256]{1,0:T(8,128)} %bitcast.16, s32[256,256]{1,0:T(8,128)} %bitcast.24), custom_call_target="tpu_custom_call" | custom-call | flops 3000000 | bytes 3000000 | tf_op jit(solution)/shard_map/mask/pallas_call | solution.py:561
  10.6 0.0 collective-permute-done.other_ref
  10.6 0.6 copy-done.5
  11.2 2.8 %route.1 = f32[512,128]{1,0:T(8,128)} custom-call(s32[1]{0:T(128)S(6)} %copy.15.live_ref, s32[1,1024]{1,0:T(1,128)} %owner_ref.1, f32[40,1024]{1,0:T(8,128)} %get-tuple-element.66.own_ref, f32[8,1024]{1,0:T(8,128)} %copy-done.5), custom_call_target="tpu_custom_call" | custom-call | tf_op jit(solution)/shard_map/route/pallas_call | solution.py:561
  14.0 27.9 %all_to_all.16 = f32[128,4,128]{2,1,0:T(4,128)} all-to-all(f32[128,4,128]{2,1,0:T(4,128)} %bitcast.23), channel_id=1, replica_groups=mesh['gx'=16,'gy'=8,'gz'=2] {'gx','gy'}, dimensions={0} | all-to-all | bytes 524288 | tf_op jit(solution)/shard_map/all_to_all | solution.py:602
  41.9 2.2 %table.1 = (bf16[160,512]{1,0:T(8,128)(2,1)}, f32[56,128]{1,0:T(8,128)}, f32[56,128]{1,0:T(8,128)}) custom-call(f32[512,128]{1,0:T(8,128)} %bitcast.22, s32[4,32,256]{2,1,0:T(8,128)} %index_ref.9, f32[4,32,256]{2,1,0:T(8,128)} %weight_ref.9, f32[2,16,128]{2,1,0:T(8,128)} %get-tuple-element.77.mask_y_ref), custom_call_target="tpu_custom_call" | custom-call | tf_op jit(solution)/shard_map/table/pallas_call | solution.py:561
  44.0 1.4 %collective-permute-start.2 = (f32[56,128]{1,0:T(8,128)}, f32[56,128]{1,0:T(8,128)S(1)}, u32[]{:S(2)}, u32[]{:S(2)}) collective-permute-start(f32[56,128]{1,0:T(8,128)} %get-tuple-element.83), channel_id=1, source_target_pairs={{2,0},{4,2},{6,4},{8,6},{10,8},{12,10},{14,12},{3,1},{5,3},{7,5},{... | collective-permute-start | bytes 86024 | tf_op jit(solution)/shard_map/ppermute | solution.py:530
  45.4 3.5 %edge.1 = (f32[2,8,40,128]{3,2,1,0:T(8,128)}, f32[248,256]{1,0:T(8,128)}, f32[248,256]{1,0:T(8,128)}) custom-call(bf16[160,512]{1,0:T(8,128)(2,1)} %get-tuple-element.95.table_ref, s32[4,32,256]{2,1,0:T(8,128)} %index_ref.9, f32[4,32,256]{2,1,0:T(8,128)} %weight_ref.9, f32[2,48,256]{2,1,0:T(8,128)} %get-tuple-element.79.mask_x_ref), custom_call_target="tpu_custom_call" | custom-call | flops 1500000000 | bytes 1500000 | tf_op jit(solution)/shard_map/edge/pallas_call | solution.py:561
  48.9 4.1 %collective-permute-start.3 = (f32[56,128]{1,0:T(8,128)S(1)}, f32[56,128]{1,0:T(8,128)S(1)}, u32[]{:S(2)}, u32[]{:S(2)}) collective-permute-start(f32[56,128]{1,0:T(8,128)S(1)} %copy-done.9), channel_id=1, source_target_pairs={{0,2},{2,4},{4,6},{6,8},{8,10},{10,12},{12,14},{1,3},{3,5},{5,7},{... | collective-permute-start | bytes 86024 | tf_op jit(solution)/shard_map/ppermute | solution.py:530
  53.1 0.0 copy-start.3
  53.1 3.3 %middle4.1.middle_0_ref = f32[2,8,40,128]{3,2,1,0:T(8,128)} custom-call(bf16[160,512]{1,0:T(8,128)(2,1)} %get-tuple-element.95.table_ref, s32[4,32,256]{2,1,0:T(8,128)} %index_ref.9, f32[4,32,256]{2,1,0:T(8,128)} %weight_ref.9), custom_call_target="tpu_custom_call" | custom-call | flops 1500000000 | bytes 1000000 | tf_op jit(solution)/shard_map/middle4/pallas_call | solution.py:561
  56.4 0.0 collective-permute-done.3.left_ref
  56.5 1.3 %collective-permute-start.4 = (f32[248,256]{1,0:T(8,128)S(1)}, f32[248,256]{1,0:T(8,128)S(1)}, u32[]{:S(2)}, u32[]{:S(2)}) collective-permute-start(f32[248,256]{1,0:T(8,128)S(1)} %get-tuple-element.97), channel_id=1, source_target_pairs={{16,0},{32,16},{48,32},{64,48},{80,64},{96,80},{112,96},{128,112},... | collective-permute-start | bytes 761864 | tf_op jit(solution)/shard_map/ppermute | solution.py:530
  57.8 3.3 %middle12.1.middle_1_ref = f32[2,8,40,128]{3,2,1,0:T(8,128)} custom-call(bf16[160,512]{1,0:T(8,128)(2,1)} %get-tuple-element.95.table_ref, s32[4,32,256]{2,1,0:T(8,128)} %index_ref.9, f32[4,32,256]{2,1,0:T(8,128)} %weight_ref.9), custom_call_target="tpu_custom_call" | custom-call | flops 1500000000 | bytes 1000000 | tf_op jit(solution)/shard_map/middle12/pallas_call | solution.py:561
  61.1 4.2 %collective-permute-start.5 = (f32[248,256]{1,0:T(8,128)S(1)}, f32[248,256]{1,0:T(8,128)S(1)}, u32[]{:S(2)}, u32[]{:S(2)}) collective-permute-start(f32[248,256]{1,0:T(8,128)S(1)} %get-tuple-element.98), channel_id=1, source_target_pairs={{0,16},{16,32},{32,48},{48,64},{64,80},{80,96},{96,112},{112,128},... | collective-permute-start | bytes 761864 | tf_op jit(solution)/shard_map/ppermute | solution.py:530
  65.3 3.3 %middle20.1.middle_2_ref = f32[2,8,40,128]{3,2,1,0:T(8,128)} custom-call(bf16[160,512]{1,0:T(8,128)(2,1)} %get-tuple-element.95.table_ref, s32[4,32,256]{2,1,0:T(8,128)} %index_ref.9, f32[4,32,256]{2,1,0:T(8,128)} %weight_ref.9), custom_call_target="tpu_custom_call" | custom-call | flops 1500000000 | bytes 1000000 | tf_op jit(solution)/shard_map/middle20/pallas_call | solution.py:561
  68.6 0.0 collective-permute-done.4.above_ref
  68.6 0.7 copy-done.1
  69.3 0.7 copy-done.2
  70.0 6.8 %basis.1 = (f32[3,17,40,384]{3,2,1,0:T(8,128)}, f32[256,128]{1,0:T(8,128)}) custom-call(s32[1]{0:T(128)} %bitcast.4.gx_ref, s32[1]{0:T(128)} %bitcast.5.gy_ref, s32[1]{0:T(128)} %bitcast.gz_ref, f32[2,8,40,128]{3,2,1,0:T(8,128)} %get-tuple-element.82.edge_ref, f32[2,8,40,128]{3,2,1,0:T(8,128)} %middle4.1.middle_0_ref, ...), custom_call_target="tpu_custom_call" | custom-call | tf_op jit(solution)/shard_map/basis/pallas_call | solution.py:561
  76.8 26.6 %all_to_all.17 = f32[256,1,128]{2,1,0:T(1,128)} all-to-all(f32[256,1,128]{2,1,0:T(1,128)} %bitcast.28), channel_id=1, replica_groups=mesh['gx'=16,'gy'=8,'gz'=2] {'gx','gy','gz'}, dimensions={0} | all-to-all | bytes 262144 | tf_op jit(solution)/shard_map/all_to_all | solution.py:668
  103.4 4.7 %wind.1 = (f32[16,32,256]{2,1,0:T(8,128)}, f32[3,16,32,256]{3,2,1,0:T(8,128)}, f32[32,256]{1,0:T(8,128)}, f32[32,256]{1,0:T(8,128)}) custom-call(s32[1]{0:T(128)} %bitcast.gz_ref, f32[256,128]{1,0:T(8,128)} %bitcast.26, f32[3,17,40,384]{3,2,1,0:T(8,128)} %get-tuple-element.100.basis_ref, f32[2,320,128]{2,1,0:T(8,128)} %bitcast.18, f32[2,320,128]{2,1,0:T(8,128)} %bitcast.19, ...), custom_call_target="tpu_custom_call" | custom-call | tf_op jit(solution)/shard_map/wind/pallas_call | solution.py:561
  108.1 0.6 collective-permute-start.6
  108.7 1.1 collective-permute-done.6.other_ref
  109.7 0.6 copy-done.6
  110.3 1.7 %fuel.1 = f32[3,32,256]{2,1,0:T(8,128)} custom-call(f32[32,256]{1,0:T(8,128)} %get-tuple-element.103.speed_ref, f32[32,256]{1,0:T(8,128)} %copy-done.6, f32[32,256]{1,0:T(8,128)} %get-tuple-element.104.balance_ref, f32[3,32,256]{2,1,0:T(8,128)} %start_ref.1), custom_call_target="tpu_custom_call" | custom-call | tf_op jit(solution)/shard_map/fuel/pallas_call | solution.py:561
  (19 shorter events, 0.0 us)
Async XLA Ops:
  1.6 6.1 %collective-permute-start.1 = (s32[8,32,256]{2,1,0:T(8,128)S(1)}, s32[8,32,256]{2,1,0:T(8,128)S(1)}, u32[]{:S(2)}, u32[]{:S(2)}) collective-permute-start(s32[8,32,256]{2,1,0:T(8,128)S(1)} %slice.37), channel_id=1, source_target_pairs={{0,1},{1,0},{2,3},{3,2},{4,5},{5,4},{6,7},{7,6},{8,9},{9,8},{10,11... | collective-permute-start | bytes 786440 | tf_op jit(solution)/shard_map/ppermute | solution.py:535
  7.0 3.5 %collective-permute-start = (f32[8,1024]{1,0:T(8,128)}, f32[8,1024]{1,0:T(8,128)S(1)}, u32[]{:S(2)}, u32[]{:S(2)}) collective-permute-start(f32[8,1024]{1,0:T(8,128)} %get-tuple-element.67), channel_id=1, source_target_pairs={{0,1},{1,0},{2,3},{3,2},{4,5},{5,4},{6,7},{7,6},{8,9},{9,8},{10,11... | collective-permute-start | bytes 98312 | tf_op jit(solution)/shard_map/ppermute | solution.py:535
  7.7 0.7 copy-start
  10.6 0.6 copy-start.5
  44.0 4.9 %copy-start.9 = (f32[56,128]{1,0:T(8,128)S(1)}, f32[56,128]{1,0:T(8,128)}, u32[]{:S(2)}) copy-start(f32[56,128]{1,0:T(8,128)} %get-tuple-element.90) | copy-start | bytes 86020
  44.0 9.0 %collective-permute-start.2 = (f32[56,128]{1,0:T(8,128)}, f32[56,128]{1,0:T(8,128)S(1)}, u32[]{:S(2)}, u32[]{:S(2)}) collective-permute-start(f32[56,128]{1,0:T(8,128)} %get-tuple-element.83), channel_id=1, source_target_pairs={{2,0},{4,2},{6,4},{8,6},{10,8},{12,10},{14,12},{3,1},{5,3},{7,5},{... | collective-permute-start | bytes 86024 | tf_op jit(solution)/shard_map/ppermute | solution.py:530
  48.9 7.5 %copy-start.7 = (f32[248,256]{1,0:T(8,128)S(1)}, f32[248,256]{1,0:T(8,128)}, u32[]{:S(2)}) copy-start(f32[248,256]{1,0:T(8,128)} %get-tuple-element.88) | copy-start | bytes 761860
  48.9 7.5 %copy-start.8 = (f32[248,256]{1,0:T(8,128)S(1)}, f32[248,256]{1,0:T(8,128)}, u32[]{:S(2)}) copy-start(f32[248,256]{1,0:T(8,128)} %get-tuple-element.91) | copy-start | bytes 761860
  48.9 7.5 %collective-permute-start.3 = (f32[56,128]{1,0:T(8,128)S(1)}, f32[56,128]{1,0:T(8,128)S(1)}, u32[]{:S(2)}, u32[]{:S(2)}) collective-permute-start(f32[56,128]{1,0:T(8,128)S(1)} %copy-done.9), channel_id=1, source_target_pairs={{0,2},{2,4},{4,6},{6,8},{8,10},{10,12},{12,14},{1,3},{3,5},{5,7},{... | collective-permute-start | bytes 86024 | tf_op jit(solution)/shard_map/ppermute | solution.py:530
  53.1 8.0 %copy-start.3 = (f32[56,128]{1,0:T(8,128)}, f32[56,128]{1,0:T(8,128)S(1)}, u32[]{:S(2)}) copy-start(f32[56,128]{1,0:T(8,128)S(1)} %collective-permute-done.2.right_ref) | copy-start | bytes 86020
  56.4 12.2 %copy-start.4 = (f32[56,128]{1,0:T(8,128)}, f32[56,128]{1,0:T(8,128)S(1)}, u32[]{:S(2)}) copy-start(f32[56,128]{1,0:T(8,128)S(1)} %collective-permute-done.3.left_ref) | copy-start | bytes 86020
  56.5 12.1 %collective-permute-start.4 = (f32[248,256]{1,0:T(8,128)S(1)}, f32[248,256]{1,0:T(8,128)S(1)}, u32[]{:S(2)}, u32[]{:S(2)}) collective-permute-start(f32[248,256]{1,0:T(8,128)S(1)} %get-tuple-element.97), channel_id=1, source_target_pairs={{16,0},{32,16},{48,32},{64,48},{80,64},{96,80},{112,96},{128,112},... | collective-permute-start | bytes 761864 | tf_op jit(solution)/shard_map/ppermute | solution.py:530
  61.1 7.5 %collective-permute-start.5 = (f32[248,256]{1,0:T(8,128)S(1)}, f32[248,256]{1,0:T(8,128)S(1)}, u32[]{:S(2)}, u32[]{:S(2)}) collective-permute-start(f32[248,256]{1,0:T(8,128)S(1)} %get-tuple-element.98), channel_id=1, source_target_pairs={{0,16},{16,32},{32,48},{48,64},{64,80},{80,96},{96,112},{112,128},... | collective-permute-start | bytes 761864 | tf_op jit(solution)/shard_map/ppermute | solution.py:530
  68.6 0.7 copy-start.1
  69.3 0.7 copy-start.2
  108.1 1.7 %collective-permute-start.6 = (f32[32,256]{1,0:T(8,128)}, f32[32,256]{1,0:T(8,128)S(1)}, u32[]{:S(2)}, u32[]{:S(2)}) collective-permute-start(f32[32,256]{1,0:T(8,128)} %get-tuple-element.103.speed_ref), channel_id=1, source_target_pairs={{0,1},{1,0},{2,3},{3,2},{4,5},{5,4},{6,7},{7,6},{8,9},{9,8},{10,11... | collective-permute-start | bytes 98312 | tf_op jit(solution)/shard_map/ppermute | solution.py:535
  109.7 0.6 copy-start.6

commit v4 on v3

--- a/solution.py
+++ b/solution.py
@@ -20,7 +20,7 @@
 STRIP = NS * 3 + 24
 XR = 40
 YR = 384
-VMEM = 56 * 1024 * 1024
+VMEM = 28 * 1024 * 1024
 
 
 def params():
@@ -36,7 +36,9 @@
     return lax.dot_general(a, b, (((1,), (1,)), ((), ())), preferred_element_type=F32)
 
 
-def profile_kernel(gz_ref, weights_ref, columns_ref, own_ref, send_ref):
+def route_kernel(
+    gz_ref, live_ref, weights_ref, columns_ref, owner_ref, out_ref, *, tiles, capacity
+):
     plain = weights_ref[...]
     turned = jnp.concatenate([plain[LZ - 1 - i : LZ - i] for i in range(LZ)], axis=0)
     weights = jnp.where(gz_ref[0] == 0, plain, turned)
@@ -57,12 +59,8 @@
     )
     w_high, w_low = split(stack)
     c_high, c_low = split(columns_ref[...])
-    result = dot_nt(w_high, c_high) + dot_nt(w_high, c_low) + dot_nt(w_low, c_high)
-    own_ref[...] = result[:NF]
-    send_ref[...] = result[NF:]
-
-
-def route_kernel(live_ref, owner_ref, own_ref, other_ref, out_ref, *, tiles, capacity):
+    profile = dot_nt(w_high, c_high) + dot_nt(w_high, c_low) + dot_nt(w_low, c_high)
+
     rows = owner_ref.shape[1]
     slots = tiles * capacity
     half = capacity // 2
@@ -80,9 +78,8 @@
     upper = jnp.where(rank >= half, 1, 0)
     target = jnp.where(owner >= 0, owner * half + rank + upper * (slots // 2 - half), -1)
     place = lax.broadcasted_iota(jnp.int32, (slots, rows), 0) == target
-    profile = jnp.concatenate([own_ref[: NF - 8], own_ref[NF - 8 :] + other_ref[...]], axis=0)
     high, low = split(profile)
-    pad = jnp.zeros((64 - NF, rows), BF16)
+    pad = jnp.zeros((64 - NF - 8, rows), BF16)
     both = jnp.concatenate([high, pad, low, pad], axis=0)
     placed = dot_nt(jnp.where(place, 1.0, 0.0).astype(BF16), both)
     placed = placed + pltpu.roll(placed, 64, 1)
@@ -90,9 +87,10 @@
     out_ref[...] = jnp.where(lane < 64, placed[: slots // 2], placed[slots // 2 :])
 
 
-def fill_table(received_ref, table_ref):
+def fill_table(received_ref, other_ref, table_ref):
     blocks = received_ref.shape[0] // 256
     turned = [jnp.transpose(received_ref[256 * p : 256 * p + 256, :]) for p in range(blocks)]
+    beyond = [jnp.transpose(other_ref[256 * p : 256 * p + 256, :]) for p in range(blocks)]
     parts = 2 * blocks
     for g in range(NF // 8):
         value = jnp.concatenate(
@@ -103,6 +101,15 @@
             ],
             axis=0,
         )
+        if g == NF // 8 - 1:
+            value = value + jnp.concatenate(
+                [
+                    beyond[p][64 * side + NF : 64 * side + NF + 8]
+                    for side in range(2)
+                    for p in range(blocks)
+                ],
+                axis=0,
+            )
         rows = slice(8 * parts * g, 8 * parts * (g + 1))
         table_ref[rows, 0:256], table_ref[rows, 256:512] = split(value)
 
@@ -158,38 +165,25 @@
                 out_ref[h, at, 8 * g : 8 * g + 8, :] = got[g][:, 128 * h : 128 * h + 128]
 
 
-def mask_kernel(gz_ref, mask_ref, far_mask_ref, mask_y_ref, mask_x_ref, mask_f_ref):
-    lower = gz_ref[0] == 0
-    halves = mask_f_ref.shape[0]
-    rows = mask_f_ref.shape[1] // LZ
-    cols = 128 * halves
-    lane = lax.broadcasted_iota(jnp.int32, (8, 128), 1)
-    for h in range(halves):
+def fill_mask(lower, mask_ref, far_mask_ref, mask_f_ref):
+    first = mask_ref.shape[0] // 2 - far_mask_ref.shape[0]
+    last = first + far_mask_ref.shape[0]
+    for h in range(mask_f_ref.shape[0]):
         at = slice(128 * h, 128 * h + 128)
-        near = mask_ref[0 : 8 * rows, at]
-        mask_f_ref[h, 0 : 8 * rows] = jnp.where(lower, near, far_mask_ref[:, at]).astype(F32)
-        mask_f_ref[h, 8 * rows :] = mask_ref[8 * rows :, at].astype(F32)
-    for side, start, turn in ((0, 0, 0), (1, cols - 128, 4)):
-        for g in range(LZ // 8):
-            total = None
-            for x in range(rows):
-                value = mask_f_ref[start // 128, pl.ds(x + g * 8 * rows, 8, stride=rows), :]
-                value = pltpu.roll(value, (4 * x + turn) % 128, 1)
-                total = value if total is None else jnp.where((lane >> 2) == x, value, total)
-            mask_y_ref[side, 8 * g : 8 * g + 8] = total
-            for d in range(3):
-                x = d if side == 0 else rows - 1 - d
-                for h in range(halves):
-                    mask_x_ref[
-                        side, LZ * d + 8 * g : LZ * d + 8 * g + 8, 128 * h : 128 * h + 128
-                    ] = mask_f_ref[h, pl.ds(x + g * 8 * rows, 8, stride=rows), :]
+        mask_f_ref[h, 0:first] = mask_ref[0:first, at].astype(F32)
+        mask_f_ref[h, first:last] = jnp.where(
+            lower, mask_ref[first:last, at], far_mask_ref[:, at]
+        ).astype(F32)
+        mask_f_ref[h, last:] = mask_ref[last:, at].astype(F32)
 
 
 def table_kernel(
-    received_ref, index_ref, weight_ref, mask_y_ref, table_ref, low_y_ref, high_y_ref, *, capacity
+    gz_ref, received_ref, other_ref, index_ref, weight_ref, mask_ref, far_mask_ref,
+    table_ref, low_y_ref, high_y_ref, mask_f_ref, *, capacity
 ):
     points, rows, cols = index_ref.shape
-    fill_table(received_ref, table_ref)
+    fill_table(received_ref, other_ref, table_ref)
+    fill_mask(gz_ref[0] == 0, mask_ref, far_mask_ref, mask_f_ref)
     lane = lax.broadcasted_iota(jnp.int32, (8, 128), 1)
     row = lax.broadcasted_iota(jnp.int32, (8, 128), 0)
 
@@ -214,29 +208,43 @@
     for side, out in ((0, low_y_ref), (1, high_y_ref)):
         for g in range(NF // 8):
             out[8 * g : 8 * g + 8] = got[g][:, 128 * side : 128 * side + 128]
-        out[NF:] = mask_y_ref[side]
+        start, turn = ((0, 0), (cols - 128, 4))[side]
+        for g in range(LZ // 8):
+            total = None
+            for x in range(rows):
+                value = mask_f_ref[start // 128, pl.ds(x + g * 8 * rows, 8, stride=rows), :]
+                value = pltpu.roll(value, (4 * x + turn) % 128, 1)
+                total = value if total is None else jnp.where((lane >> 2) == x, value, total)
+            out[NF + 8 * g : NF + 8 * g + 8] = total
 
 
 def edge_kernel(
-    table_ref, index_ref, weight_ref, mask_x_ref, edge_ref, low_x_ref, high_x_ref, *, capacity
+    gz_ref, table_ref, index_ref, weight_ref, mask_ref, far_mask_ref,
+    edge_ref, middle_ref, low_x_ref, high_x_ref, mask_f_ref, *, capacity
 ):
     _, rows, cols = index_ref.shape
     chosen = [0, 1, 2, 3] + [rows - 4 + j for j in range(4)]
     pick_rows(table_ref, index_ref, weight_ref, chosen, edge_ref, capacity)
+    fill_mask(gz_ref[0] == 0, mask_ref, far_mask_ref, mask_f_ref)
     for d in range(4):
-        for side, out, kept in ((0, low_x_ref, d), (1, high_x_ref, 7 - d)):
+        for out, x, kept in ((low_x_ref, d, d), (high_x_ref, rows - 1 - d, 7 - d)):
             for h in range(cols // 128):
                 at = slice(128 * h, 128 * h + 128)
                 if d < 3:
                     out[NS * d : NS * d + NF, at] = edge_ref[h, kept]
-                    out[NS * d + NF : NS * d + NS, at] = mask_x_ref[side, LZ * d : LZ * d + LZ, at]
+                    for g in range(LZ // 8):
+                        first = NS * d + NF + 8 * g
+                        out[first : first + 8, at] = mask_f_ref[
+                            h, pl.ds(x + g * 8 * rows, 8, stride=rows), :
+                        ]
                 else:
                     out[NS * 3 : NS * 3 + 16, at] = edge_ref[h, kept, 0:16]
                     out[NS * 3 + 16 : NS * 3 + 24, at] = edge_ref[h, kept, 32:40]
+    pick_rows(table_ref, index_ref, weight_ref, list(range(4, 12)), middle_ref, capacity)
 
 
 def middle_kernel(table_ref, index_ref, weight_ref, middle_ref, *, first, capacity):
-    chosen = list(range(first, first + 8))
+    chosen = list(range(first, first + middle_ref.shape[1]))
     pick_rows(table_ref, index_ref, weight_ref, chosen, middle_ref, capacity)
 
 
@@ -245,7 +253,7 @@
         return edge_ref, x
     if x >= rows - 4:
         return edge_ref, x - rows + 8
-    return middle_refs[(x - 4) // 8], (x - 4) % 8
+    return (middle_refs[0], x - 4) if x < 12 else (middle_refs[1], x - 12)
 
 
 def ring_smooth(plane):
@@ -254,7 +262,7 @@
 
 
 def basis_kernel(
-    gx_ref, gy_ref, gz_ref, edge_ref, middle_0_ref, middle_1_ref, middle_2_ref, mask_ref, far_mask_ref,
+    gx_ref, gy_ref, gz_ref, edge_ref, middle_0_ref, middle_1_ref, mask_ref, far_mask_ref,
     right_ref, left_ref, above_ref, below_ref,
     basis_ref, moments_ref,
     ext_ref, source_ref, air_ref, last_ref, *, last_gx, last_gy
@@ -266,7 +274,7 @@
     lane = lax.broadcasted_iota(jnp.int32, (8, 128), 1)
 
     for x in range(rows):
-        held_ref, j = holder(x, rows, edge_ref, (middle_0_ref, middle_1_ref, middle_2_ref))
+        held_ref, j = holder(x, rows, edge_ref, (middle_0_ref, middle_1_ref))
         for h in range(halves):
             ext_ref[h, NS * x : NS * x + NF] = held_ref[h, j]
         for g in range(NS // 8):
@@ -345,7 +353,8 @@
                     if layer < LZ:
                         known = mask_ref[rows * picked + 8 * group : rows * picked + 8 * group + 8, at]
                     else:
-                        known = far_mask_ref[rows * picked + 8 * group : rows * picked + 8 * group + 8, at]
+                        first = rows * (picked - 5) + 8 * group
+                        known = far_mask_ref[first : first + 8, at]
                     known = known.astype(F32)
                 else:
                     known = ext_ref[h, pl.ds(8 * group * NS + NF + picked, 8, stride=NS), :]
@@ -446,7 +455,7 @@
 
 
 def wind_kernel(
-    gz_ref, moments_ref, basis_ref, edge_ref, middle_0_ref, middle_1_ref, middle_2_ref, mask_ref,
+    gz_ref, moments_ref, basis_ref, edge_ref, middle_0_ref, middle_1_ref, mask_ref,
     potential_ref, wind_ref, speed_ref, balance_ref, p_ref, grid_ref
 ):
     gz = gz_ref[0]
@@ -454,8 +463,8 @@
     near = 4 * NF
     for h in range(cols // 128):
         grid_ref[h, 0:near] = edge_ref[h, 0:near]
-        for i, held_ref in enumerate((middle_0_ref, middle_1_ref, middle_2_ref)):
-            grid_ref[h, near + 8 * NF * i : near + 8 * NF * (i + 1)] = held_ref[h]
+        grid_ref[h, near : near + 8 * NF] = middle_0_ref[h]
+        grid_ref[h, near + 8 * NF : (rows - 4) * NF] = middle_1_ref[h]
         grid_ref[h, (rows - 4) * NF :] = edge_ref[h, near:]
     totals = jnp.sum(moments_ref[...], axis=0, keepdims=True)
     factors = iterate([totals[:, k : k + 1] for k in range(6)])
@@ -556,49 +565,50 @@
     vmem = pl.BlockSpec(memory_space=pltpu.VMEM)
     smem = pl.BlockSpec(memory_space=pltpu.SMEM)
 
-    def kernel(body, name, outs, operands, scratch=(), in_smem=0, cost=None):
-        shapes = [jax.ShapeDtypeStruct(shape, dtype) for shape, dtype in outs]
+    def kernel(body, name, outs, operands, scratch=(), in_smem=0, anywhere=(), cost=None):
+        inputs = len(operands)
+        own_refs = inputs + len(outs) + len(scratch)
+
+        def whole(*refs):
+            refs, extra = list(refs[:own_refs]), refs[own_refs:]
+            copies = []
+            for i, at in enumerate(anywhere):
+                copies.append(pltpu.make_async_copy(refs[at], extra[2 * i], extra[2 * i + 1]))
+                refs[at] = extra[2 * i]
+            for copy in copies:
+                copy.start()
+            for copy in copies:
+                copy.wait()
+            body(*refs)
+
+        specs = [smem if at < in_smem else vmem for at in range(inputs)]
+        more = []
+        for at in anywhere:
+            specs[at] = pl.BlockSpec(memory_space=pl.ANY)
+            more.append(pltpu.VMEM(operands[at].shape, operands[at].dtype))
+            more.append(pltpu.SemaphoreType.DMA)
         return pl.pallas_call(
-            body,
-            out_shape=tuple(shapes),
-            in_specs=[smem] * in_smem + [vmem] * (len(operands) - in_smem),
+            whole,
+            out_shape=tuple(jax.ShapeDtypeStruct(shape, dtype) for shape, dtype in outs),
+            in_specs=specs,
             out_specs=(vmem,) * len(outs),
-            scratch_shapes=[pltpu.VMEM(shape, dtype) for shape, dtype in scratch],
+            scratch_shapes=[pltpu.VMEM(shape, dtype) for shape, dtype in scratch] + more,
             compiler_params=params(),
             cost_estimate=cost,
             name=name,
         )(*operands)
 
-    own, leaving = kernel(
-        profile_kernel,
-        "profile",
-        [((NF, rows_in), F32), ((8, rows_in), F32)],
-        [gz, vertical_weights, era5_columns[0]],
-        in_smem=1,
-    )
-    other = swapped(leaving, "gz", 1)
-    far_mask = swapped(terrain_mask[8:], "gz", 1).reshape(8 * rows, cols)
     near_mask = terrain_mask.reshape(layers * rows, cols)
-    mask_y, mask_x = kernel(
-        mask_kernel,
-        "mask",
-        [((2, LZ, 128), F32), ((2, 3 * LZ, cols), F32)],
-        [gz, near_mask, far_mask],
-        scratch=[((halves, layers * rows, 128), F32)],
-        in_smem=1,
-        cost=pl.CostEstimate(flops=3_000_000, bytes_accessed=3_000_000, transcendentals=0),
-    )
-    other, mask_y, mask_x = lax.optimization_barrier((other, mask_y, mask_x))
+    far_mask = swapped(terrain_mask[LZ - DEEP :], "gz", 1).reshape(DEEP * rows, cols)
     (outgoing,) = kernel(
         functools.partial(route_kernel, tiles=tiles, capacity=capacity),
         "route",
         [((slots // 2, 128), F32)],
-        [live_counts, column_owner, own, other],
-        in_smem=1,
-    )
-    outgoing, far_mask, mask_y, mask_x, gx, gy, gz = lax.optimization_barrier(
-        (outgoing, far_mask, mask_y, mask_x, gx, gy, gz)
-    )
+        [gz, live_counts, vertical_weights, era5_columns[0], column_owner],
+        in_smem=2,
+        cost=pl.CostEstimate(flops=1_000_000_000, bytes_accessed=1_000_000, transcendentals=0),
+    )
+    outgoing, far_mask, gx, gy, gz = lax.optimization_barrier((outgoing, far_mask, gx, gy, gz))
     received = lax.all_to_all(
         outgoing.reshape(tiles, capacity // 2, 128),
         ("gx", "gy"),
@@ -606,48 +616,47 @@
         concat_axis=0,
         tiled=True,
     ).reshape(slots // 2, 128)
-
-    def middle(table, first):
-        return kernel(
-            functools.partial(middle_kernel, first=first, capacity=capacity),
-            "middle" + str(first),
-            [((halves, 8, NF, 128), F32)],
-            [table, stencil_index, stencil_weight],
-            cost=pl.CostEstimate(flops=1_500_000_000, bytes_accessed=1_000_000, transcendentals=0),
-        )[0]
+    other = swapped(received, "gz", 1)
 
     table, low_y, high_y = kernel(
         functools.partial(table_kernel, capacity=capacity),
         "table",
         [((slots // 256 * NF, 512), BF16), ((NS, 128), F32), ((NS, 128), F32)],
-        [received, stencil_index, stencil_weight, mask_y],
+        [gz, received, other, stencil_index, stencil_weight, near_mask, far_mask],
+        scratch=[((halves, layers * rows, 128), F32)],
+        in_smem=1,
+        anywhere=(2, 6),
     )
     right = shifted(low_y, "gy", -1)
-    edge, low_x, high_x = kernel(
+    left = shifted(high_y, "gy", 1)
+    edge, middle_0, low_x, high_x = kernel(
         functools.partial(edge_kernel, capacity=capacity),
         "edge",
         [
             ((halves, 8, NF, 128), F32),
+            ((halves, 8, NF, 128), F32),
             ((STRIP + NS, cols), F32),
             ((STRIP + NS, cols), F32),
         ],
-        [table, stencil_index, stencil_weight, mask_x],
-        cost=pl.CostEstimate(flops=1_500_000_000, bytes_accessed=1_500_000, transcendentals=0),
-    )
-    edge, high_y = lax.optimization_barrier((edge, high_y))
-    left = shifted(high_y, "gy", 1)
-    table, right = lax.optimization_barrier((table, right))
-    middle_0 = middle(table, 4)
-    middle_0, low_x, high_x = lax.optimization_barrier((middle_0, low_x, high_x))
+        [gz, table, stencil_index, stencil_weight, near_mask, far_mask],
+        scratch=[((halves, layers * rows, 128), F32)],
+        in_smem=1,
+        anywhere=(5,),
+        cost=pl.CostEstimate(flops=3_000_000_000, bytes_accessed=2_500_000, transcendentals=0),
+    )
     corners = jnp.concatenate([right, left], axis=1)
     low_x, high_x = low_x.at[STRIP:].set(corners), high_x.at[STRIP:].set(corners)
     table, low_x, high_x = lax.optimization_barrier((table, low_x, high_x))
     above = shifted(low_x, "gx", -1)
-    middle_1 = middle(table, 12)
-    middle_1, table, high_x = lax.optimization_barrier((middle_1, table, high_x))
     below = shifted(high_x, "gx", 1)
-    middle_2 = middle(table, 20)
-    middles = (middle_0, middle_1, middle_2)
+    (middle_1,) = kernel(
+        functools.partial(middle_kernel, first=12, capacity=capacity),
+        "middle",
+        [((halves, rows - 16, NF, 128), F32)],
+        [table, stencil_index, stencil_weight],
+        cost=pl.CostEstimate(flops=3_000_000_000, bytes_accessed=1_600_000, transcendentals=0),
+    )
+    middles = (middle_0, middle_1)
 
     devices = tiles * lax.axis_size("gz")
     basis, moments = kernel(
@@ -664,6 +673,7 @@
             ((2, DEEP - 1, XR, YR), F32),
         ],
         in_smem=3,
+        anywhere=(7, 8, 9, 10, 11),
     )
     moments = lax.all_to_all(
         moments, ("gx", "gy", "gz"), split_axis=0, concat_axis=0, tiled=True
@@ -681,7 +691,7 @@
             gz,
             moments,
             basis,
-            *(piece.reshape(halves, 8 * NF, 128) for piece in (edge, *middles)),
+            *(piece.reshape(halves, -1, 128) for piece in (edge, *middles)),
             terrain_mask,
         ],
         scratch=[((LZ + 1, XR, YR), F32), ((halves, rows * NF, 128), F32)],
@@ -692,6 +702,7 @@
         "fuel",
         [((len(LAGS), rows, cols), F32)],
         [speed, swapped(speed, "gz", 1), balance, fuel_start],
+        anywhere=(1,),
     )
     return (potential, wind_field, fuel_moisture)
 

time: 113 us -> 93.7 us (0.83)
  Pallas kernels: 35.8 us -> 16.5 us
  blocking collectives: 54.4 us -> 52.3 us
  waiting for transfers between devices: 1.09 us -> 3.01 us
  starting transfers between devices: 14.9 us -> 16.5 us
    pallas_call x11 -> x7, Pallas kernels: 35.8 us -> 16.5 us  [kernel(): pl.pallas_call(whole, out_shape=tuple((jax.ShapeDtypeStruct(shape, dtype)...]
    all_to_all x1, blocking collectives: 26.6 us -> 24.3 us  [shards(): lax.all_to_all(moments, ('gx', 'gy', 'gz'), split_axis=0, concat_axis=0,...]
    ppermute x3, starting transfers between devices: 3.95 us -> 5.76 us  [swapped(): return lax.ppermute(block, axis, [(i, i ^ bit) for i in range(count)])]
    unnamed x21 -> x15, local copies, waits for them, and re-layouts: 3.33 us -> 2.44 us
  transfers between devices with their start and end apart: 7 -> 7, of which waited for: 1 -> 4; matrix products, arithmetic and copies ran while one was open for 0% -> 0% of each run, Pallas kernels for 16% -> 8%
where the time goes in v4:
time: 93.7 us; the launch traced here: 93.3 us
  blocking collectives  52.3 us (56%)
  starting transfers between devices  16.5 us (18%)
  Pallas kernels  16.5 us (18%)
  local copies, waits for them, and re-layouts  3.43 us (4%)
  waiting for transfers between devices  3.01 us (3%)
  between operations  1.61 us (2%)
    all_to_all x1, blocking collectives, shards(): lax.all_to_all(outgoing.reshape(tiles, capacity // 2, 128), ('gx', 'gy'),...  28 us
    all_to_all x1, blocking collectives, shards(): lax.all_to_all(moments, ('gx', 'gy', 'gz'), split_axis=0, concat_axis=0,...  24.3 us
    pallas_call x7, Pallas kernels, kernel(): pl.pallas_call(whole, out_shape=tuple((jax.ShapeDtypeStruct(shape, dtype)...  16.5 us
    ppermute x4, starting transfers between devices, shifted(): return lax.ppermute(block, axis, pairs)  10.8 us
    ppermute x3, starting transfers between devices, swapped(): return lax.ppermute(block, axis, [(i, i ^ bit) for i in range(count)])  5.76 us
    unnamed x15, local copies, waits for them, and re-layouts  2.44 us
    ppermute x3, waiting for transfers between devices, swapped(): return lax.ppermute(block, axis, [(i, i ^ bit) for i in range(count)])  2.02 us
  transfers between devices with their start and end apart: 7, of which 4 were waited for; matrix products, arithmetic and copies ran while one was open for 0% of the time, Pallas kernels for 8%

profile of v4, /device:TPU:1, one launch (start us, length us, event | category | flops | bytes accessed | tf_op | source)
XLA Modules:
  0.0 93.3 jit_solution(6644174163322549420)
XLA Ops:
  0.6 0.0 copy-start
  0.6 0.0 copy-start.2
  0.7 0.0 copy-start.1
  0.7 1.0 %slice.37 = s32[3,32,256]{2,1,0:T(8,128)S(1)} slice(s32[16,32,256]{2,1,0:T(8,128)} %refs_6_.1), slice={[13:16], [0:32], [0:256]} | slice | bytes 196608 | tf_op jit(solution)/shard_map/slice | solution.py:602
  1.6 3.2 %collective-permute-start = (s32[3,32,256]{2,1,0:T(8,128)S(1)}, s32[3,32,256]{2,1,0:T(8,128)S(1)}, u32[]{:S(2)}, u32[]{:S(2)}) collective-permute-start(s32[3,32,256]{2,1,0:T(8,128)S(1)} %slice.37), channel_id=1, source_target_pairs={{0,1},{1,0},{2,3},{3,2},{4,5},{5,4},{6,7},{7,6},{8,9},{9,8},{10,11... | collective-permute-start | bytes 294920 | tf_op jit(solution)/shard_map/ppermute | solution.py:544
  5.5 0.0 copy-start.4
  5.5 1.0 %copy-done.4 = f32[1,1024,128]{2,1,0:T(8,128)S(1)} copy-done((f32[1,1024,128]{2,1,0:T(8,128)S(1)}, f32[1,1024,128]{2,1,0:T(8,128)}, u32[]{:S(2)}) %copy-start.4) | copy-done | bytes 524312
  6.6 0.7 copy-done.5
  7.3 0.7 copy-done.6
  8.0 1.5 %route.1 = f32[512,128]{1,0:T(8,128)S(1)} custom-call(s32[1]{0:T(128)} %bitcast.refs_0_.refs_2_, s32[1]{0:T(128)S(6)} %copy.15.refs_1_, f32[16,32]{1,0:T(8,128)S(1)} %copy-done.5, f32[1024,128]{1,0:T(8,128)S(1)} %bitcast.29, s32[1,1024]{1,0:T(1,128)S(1)} %copy-done.6), custom_call_target="tpu_custom_call" | custom-call | flops 1000000000 | bytes 1000000 | tf_op jit(solution)/shard_map/route/pallas_call | solution.py:590
  9.4 0.0 collective-permute-done
  9.4 28.0 %all_to_all.16 = f32[128,4,128]{2,1,0:T(4,128)S(1)} all-to-all(f32[128,4,128]{2,1,0:T(4,128)S(1)} %bitcast.27), channel_id=1, replica_groups=mesh['gx'=16,'gy'=8,'gz'=2] {'gx','gy'}, dimensions={0} | all-to-all | bytes 524288 | tf_op jit(solution)/shard_map/all_to_all | solution.py:612
  37.4 1.6 %collective-permute-start.1 = (f32[512,128]{1,0:T(8,128)S(1)}, f32[512,128]{1,0:T(8,128)S(1)}, u32[]{:S(2)}, u32[]{:S(2)}) collective-permute-start(f32[512,128]{1,0:T(8,128)S(1)} %bitcast.21), channel_id=1, source_target_pairs={{0,1},{1,0},{2,3},{3,2},{4,5},{5,4},{6,7},{7,6},{8,9},{9,8},{10,11... | collective-permute-start | bytes 786440 | tf_op jit(solution)/shard_map/ppermute | solution.py:544
  39.0 1.2 %collective-permute-done.1.refs_2_ = f32[512,128]{1,0:T(8,128)S(1)} collective-permute-done((f32[512,128]{1,0:T(8,128)S(1)}, f32[512,128]{1,0:T(8,128)S(1)}, u32[]{:S(2)}, u32[]{:S(2)}) %collective-permute-start.1) | collective-permute-done | bytes 262176 | tf_op jit(solution)/shard_map/ppermute | solution.py:544
  40.2 0.9 table.1
  41.1 1.3 %collective-permute-start.2 = (f32[56,128]{1,0:T(8,128)S(1)}, f32[56,128]{1,0:T(8,128)S(1)}, u32[]{:S(2)}, u32[]{:S(2)}) collective-permute-start(f32[56,128]{1,0:T(8,128)S(1)} %get-tuple-element.57), channel_id=1, source_target_pairs={{2,0},{4,2},{6,4},{8,6},{10,8},{12,10},{14,12},{3,1},{5,3},{7,5},{... | collective-permute-start | bytes 86024 | tf_op jit(solution)/shard_map/ppermute | solution.py:539
  42.4 4.0 %collective-permute-start.3 = (f32[56,128]{1,0:T(8,128)S(1)}, f32[56,128]{1,0:T(8,128)S(1)}, u32[]{:S(2)}, u32[]{:S(2)}) collective-permute-start(f32[56,128]{1,0:T(8,128)S(1)} %get-tuple-element.58), channel_id=1, source_target_pairs={{0,2},{2,4},{4,6},{6,8},{8,10},{10,12},{12,14},{1,3},{3,5},{5,7},{... | collective-permute-start | bytes 86024 | tf_op jit(solution)/shard_map/ppermute | solution.py:539
  46.4 3.2 %edge.1 = (f32[2,8,40,128]{3,2,1,0:T(8,128)S(1)}, f32[2,8,40,128]{3,2,1,0:T(8,128)S(1)}, f32[248,256]{1,0:T(8,128)S(1)}, f32[248,256]{1,0:T(8,128)S(1)}) custom-call(s32[1]{0:T(128)} %bitcast.refs_0_.refs_2_, bf16[160,512]{1,0:T(8,128)(2,1)S(1)} %get-tuple-element.60.refs_1_.refs_0_, s32[4,32,256]{2,1,0:T(8,128)S(1)} %copy-done.1, ...), custom_call_target="tpu_custom_call" | custom-call | flops 3000000000 | bytes 2500000 | tf_op jit(solution)/shard_map/edge/pallas_call | solution.py:590
  49.6 0.0 collective-permute-done.2.refs_8_
  49.7 0.0 collective-permute-done.3.refs_9_
  49.7 1.3 %collective-permute-start.4 = (f32[248,256]{1,0:T(8,128)S(1)}, f32[248,256]{1,0:T(8,128)S(1)}, u32[]{:S(2)}, u32[]{:S(2)}) collective-permute-start(f32[248,256]{1,0:T(8,128)S(1)} %get-tuple-element.61), channel_id=1, source_target_pairs={{16,0},{32,16},{48,32},{64,48},{80,64},{96,80},{112,96},{128,112},... | collective-permute-start | bytes 761864 | tf_op jit(solution)/shard_map/ppermute | solution.py:539
  51.0 4.2 %collective-permute-start.5 = (f32[248,256]{1,0:T(8,128)S(1)}, f32[248,256]{1,0:T(8,128)S(1)}, u32[]{:S(2)}, u32[]{:S(2)}) collective-permute-start(f32[248,256]{1,0:T(8,128)S(1)} %get-tuple-element.62), channel_id=1, source_target_pairs={{0,16},{16,32},{32,48},{48,64},{64,80},{80,96},{96,112},{112,128},... | collective-permute-start | bytes 761864 | tf_op jit(solution)/shard_map/ppermute | solution.py:539
  55.2 3.0 %middle.1.refs_5_ = f32[2,16,40,128]{3,2,1,0:T(8,128)S(1)} custom-call(bf16[160,512]{1,0:T(8,128)(2,1)S(1)} %get-tuple-element.60.refs_1_.refs_0_, s32[4,32,256]{2,1,0:T(8,128)S(1)} %copy-done.1, f32[4,32,256]{2,1,0:T(8,128)S(1)} %copy-done.2), custom_call_target="tpu_custom_call" | custom-call | flops 3000000000 | bytes 1600000 | tf_op jit(solution)/shard_map/middle/pallas_call | solution.py:590
  58.2 0.1 collective-permute-done.4.refs_10_
  58.3 0.9 collective-permute-done.5.refs_11_
  59.2 4.8 %basis.1 = (f32[3,17,40,384]{3,2,1,0:T(8,128)S(1)}, f32[256,128]{1,0:T(8,128)S(1)}) custom-call(s32[1]{0:T(128)} %bitcast.3.refs_0_, s32[1]{0:T(128)} %bitcast.4.refs_1_, s32[1]{0:T(128)} %bitcast.refs_0_.refs_2_, f32[2,8,40,128]{3,2,1,0:T(8,128)S(1)} %get-tuple-element.54.refs_3_, f32[2,8,40,128]{3,2,1,0:T(8,128)S(1)} %get-tuple-element.55.refs_4_, ...), custom_call_target="tpu_custom_call" | custom-call | tf_op jit(solution)/shard_map/basis/pallas_call | solution.py:590
  64.0 0.0 copy-start.3
  64.0 24.3 %all_to_all.17 = f32[256,1,128]{2,1,0:T(1,128)S(1)} all-to-all(f32[256,1,128]{2,1,0:T(1,128)S(1)} %bitcast.28), channel_id=1, replica_groups=mesh['gx'=16,'gy'=8,'gz'=2] {'gx','gy','gz'}, dimensions={0} | all-to-all | bytes 262144 | tf_op jit(solution)/shard_map/all_to_all | solution.py:678
  88.3 2.3 %wind.1 = (f32[16,32,256]{2,1,0:T(8,128)}, f32[3,16,32,256]{3,2,1,0:T(8,128)}, f32[32,256]{1,0:T(8,128)S(1)}, f32[32,256]{1,0:T(8,128)S(1)}) custom-call(s32[1]{0:T(128)} %bitcast.refs_0_.refs_2_, f32[256,128]{1,0:T(8,128)S(1)} %bitcast.23, f32[3,17,40,384]{3,2,1,0:T(8,128)S(1)} %get-tuple-element.64.refs_2_, f32[2,320,128]{2,1,0:T(8,128)S(1)} %bitcast.19, ...), custom_call_target="tpu_custom_call" | custom-call | tf_op jit(solution)/shard_map/wind/pallas_call | solution.py:590
  90.6 0.9 collective-permute-start.6
  91.5 0.9 collective-permute-done.6.refs_1_
  92.4 0.7 fuel.1
  (9 shorter events, 0.0 us)
Async XLA Ops:
  0.6 39.6 %copy-start = (s32[16,32,256]{2,1,0:T(8,128)S(1)}, s32[16,32,256]{2,1,0:T(8,128)}, u32[]{:S(2)}) copy-start(s32[16,32,256]{2,1,0:T(8,128)} %refs_6_.1) | copy-start | bytes 1572868
  0.6 39.6 %copy-start.2 = (f32[4,32,256]{2,1,0:T(8,128)S(1)}, f32[4,32,256]{2,1,0:T(8,128)}, u32[]{:S(2)}) copy-start(f32[4,32,256]{2,1,0:T(8,128)} %refs_2_.5) | copy-start | bytes 393220
  0.7 39.6 %copy-start.1 = (s32[4,32,256]{2,1,0:T(8,128)S(1)}, s32[4,32,256]{2,1,0:T(8,128)}, u32[]{:S(2)}) copy-start(s32[4,32,256]{2,1,0:T(8,128)} %refs_1_.2) | copy-start | bytes 393220
  1.6 7.8 %collective-permute-start = (s32[3,32,256]{2,1,0:T(8,128)S(1)}, s32[3,32,256]{2,1,0:T(8,128)S(1)}, u32[]{:S(2)}, u32[]{:S(2)}) collective-permute-start(s32[3,32,256]{2,1,0:T(8,128)S(1)} %slice.37), channel_id=1, source_target_pairs={{0,1},{1,0},{2,3},{3,2},{4,5},{5,4},{6,7},{7,6},{8,9},{9,8},{10,11... | collective-permute-start | bytes 294920 | tf_op jit(solution)/shard_map/ppermute | solution.py:544
  5.5 1.0 %copy-start.4 = (f32[1,1024,128]{2,1,0:T(8,128)S(1)}, f32[1,1024,128]{2,1,0:T(8,128)}, u32[]{:S(2)}) copy-start(f32[1,1024,128]{2,1,0:T(8,128)} %param.12) | copy-start | bytes 1572868
  6.6 0.7 copy-start.5
  7.3 0.7 copy-start.6
  37.4 2.8 %collective-permute-start.1 = (f32[512,128]{1,0:T(8,128)S(1)}, f32[512,128]{1,0:T(8,128)S(1)}, u32[]{:S(2)}, u32[]{:S(2)}) collective-permute-start(f32[512,128]{1,0:T(8,128)S(1)} %bitcast.21), channel_id=1, source_target_pairs={{0,1},{1,0},{2,3},{3,2},{4,5},{5,4},{6,7},{7,6},{8,9},{9,8},{10,11... | collective-permute-start | bytes 786440 | tf_op jit(solution)/shard_map/ppermute | solution.py:544
  41.1 8.5 %collective-permute-start.2 = (f32[56,128]{1,0:T(8,128)S(1)}, f32[56,128]{1,0:T(8,128)S(1)}, u32[]{:S(2)}, u32[]{:S(2)}) collective-permute-start(f32[56,128]{1,0:T(8,128)S(1)} %get-tuple-element.57), channel_id=1, source_target_pairs={{2,0},{4,2},{6,4},{8,6},{10,8},{12,10},{14,12},{3,1},{5,3},{7,5},{... | collective-permute-start | bytes 86024 | tf_op jit(solution)/shard_map/ppermute | solution.py:539
  42.4 7.2 %collective-permute-start.3 = (f32[56,128]{1,0:T(8,128)S(1)}, f32[56,128]{1,0:T(8,128)S(1)}, u32[]{:S(2)}, u32[]{:S(2)}) collective-permute-start(f32[56,128]{1,0:T(8,128)S(1)} %get-tuple-element.58), channel_id=1, source_target_pairs={{0,2},{2,4},{4,6},{6,8},{8,10},{10,12},{12,14},{1,3},{3,5},{5,7},{... | collective-permute-start | bytes 86024 | tf_op jit(solution)/shard_map/ppermute | solution.py:539
  49.7 8.6 %collective-permute-start.4 = (f32[248,256]{1,0:T(8,128)S(1)}, f32[248,256]{1,0:T(8,128)S(1)}, u32[]{:S(2)}, u32[]{:S(2)}) collective-permute-start(f32[248,256]{1,0:T(8,128)S(1)} %get-tuple-element.61), channel_id=1, source_target_pairs={{16,0},{32,16},{48,32},{64,48},{80,64},{96,80},{112,96},{128,112},... | collective-permute-start | bytes 761864 | tf_op jit(solution)/shard_map/ppermute | solution.py:539
  51.0 8.2 %collective-permute-start.5 = (f32[248,256]{1,0:T(8,128)S(1)}, f32[248,256]{1,0:T(8,128)S(1)}, u32[]{:S(2)}, u32[]{:S(2)}) collective-permute-start(f32[248,256]{1,0:T(8,128)S(1)} %get-tuple-element.62), channel_id=1, source_target_pairs={{0,16},{16,32},{32,48},{48,64},{64,80},{80,96},{96,112},{112,128},... | collective-permute-start | bytes 761864 | tf_op jit(solution)/shard_map/ppermute | solution.py:539
  64.0 28.4 %copy-start.3 = (f32[3,32,256]{2,1,0:T(8,128)S(1)}, f32[3,32,256]{2,1,0:T(8,128)}, u32[]{:S(2)}) copy-start(f32[3,32,256]{2,1,0:T(8,128)} %refs_3_.5) | copy-start | bytes 294916
  90.6 1.7 %collective-permute-start.6 = (f32[32,256]{1,0:T(8,128)S(1)}, f32[32,256]{1,0:T(8,128)S(1)}, u32[]{:S(2)}, u32[]{:S(2)}) collective-permute-start(f32[32,256]{1,0:T(8,128)S(1)} %get-tuple-element.67.refs_0_), channel_id=1, source_target_pairs={{0,1},{1,0},{2,3},{3,2},{4,5},{5,4},{6,7},{7,6},{8,9},{9,8},{10,11... | collective-permute-start | bytes 98312 | tf_op jit(solution)/shard_map/ppermute | solution.py:544

commit v5 on v4

--- a/solution.py
+++ b/solution.py
@@ -20,11 +20,9 @@
 STRIP = NS * 3 + 24
 XR = 40
 YR = 384
-VMEM = 28 * 1024 * 1024
-
-
-def params():
-    return pltpu.CompilerParams(vmem_limit_bytes=VMEM)
+
+
+GY = ("zh", "zl")
 
 
 def split(value):
@@ -455,7 +453,7 @@
 
 
 def wind_kernel(
-    gz_ref, moments_ref, basis_ref, edge_ref, middle_0_ref, middle_1_ref, mask_ref,
+    gz_ref, moments_ref, other_moments_ref, basis_ref, edge_ref, middle_0_ref, middle_1_ref, mask_ref,
     potential_ref, wind_ref, speed_ref, balance_ref, p_ref, grid_ref
 ):
     gz = gz_ref[0]
@@ -466,7 +464,7 @@
         grid_ref[h, near : near + 8 * NF] = middle_0_ref[h]
         grid_ref[h, near + 8 * NF : (rows - 4) * NF] = middle_1_ref[h]
         grid_ref[h, (rows - 4) * NF :] = edge_ref[h, near:]
-    totals = jnp.sum(moments_ref[...], axis=0, keepdims=True)
+    totals = moments_ref[...] + other_moments_ref[...]
     factors = iterate([totals[:, k : k + 1] for k in range(6)])
     factors = [jnp.broadcast_to(c, (8, 128)) for c in factors]
     factors = [jnp.tile(c, (XR // 8, YR // 128)) for c in factors]
@@ -554,9 +552,9 @@
     terrain_mask,
     fuel_start,
 ):
-    gx, gy, gz = (lax.axis_index(a).astype(jnp.int32) for a in ("gx", "gy", "gz"))
+    gx, gy, gz = (lax.axis_index(a).astype(jnp.int32) for a in ("gx", GY, "gz"))
     gx, gy, gz = gx.reshape(1), gy.reshape(1), gz.reshape(1)
-    tiles = lax.axis_size(("gx", "gy"))
+    tiles = lax.axis_size(("gx", *GY))
     rows_in = column_owner.shape[1]
     capacity = rows_in // tiles
     slots = tiles * capacity
@@ -565,7 +563,9 @@
     vmem = pl.BlockSpec(memory_space=pltpu.VMEM)
     smem = pl.BlockSpec(memory_space=pltpu.SMEM)
 
-    def kernel(body, name, outs, operands, scratch=(), in_smem=0, anywhere=(), cost=None):
+    def kernel(
+        body, name, outs, operands, scratch=(), in_smem=0, anywhere=(), tail=None, vmem_mib=28, cost=None
+    ):
         inputs = len(operands)
         own_refs = inputs + len(outs) + len(scratch)
 
@@ -573,7 +573,10 @@
             refs, extra = list(refs[:own_refs]), refs[own_refs:]
             copies = []
             for i, at in enumerate(anywhere):
-                copies.append(pltpu.make_async_copy(refs[at], extra[2 * i], extra[2 * i + 1]))
+                from_ref = refs[at]
+                if at == tail:
+                    from_ref = from_ref.at[pl.ds(from_ref.shape[0] - far_rows, far_rows)]
+                copies.append(pltpu.make_async_copy(from_ref, extra[2 * i], extra[2 * i + 1]))
                 refs[at] = extra[2 * i]
             for copy in copies:
                 copy.start()
@@ -585,7 +588,8 @@
         more = []
         for at in anywhere:
             specs[at] = pl.BlockSpec(memory_space=pl.ANY)
-            more.append(pltpu.VMEM(operands[at].shape, operands[at].dtype))
+            shape = (far_rows, cols) if at == tail else operands[at].shape
+            more.append(pltpu.VMEM(shape, operands[at].dtype))
             more.append(pltpu.SemaphoreType.DMA)
         return pl.pallas_call(
             whole,
@@ -593,25 +597,27 @@
             in_specs=specs,
             out_specs=(vmem,) * len(outs),
             scratch_shapes=[pltpu.VMEM(shape, dtype) for shape, dtype in scratch] + more,
-            compiler_params=params(),
+            compiler_params=pltpu.CompilerParams(vmem_limit_bytes=vmem_mib * 1024 * 1024),
             cost_estimate=cost,
             name=name,
         )(*operands)
 
     near_mask = terrain_mask.reshape(layers * rows, cols)
-    far_mask = swapped(terrain_mask[LZ - DEEP :], "gz", 1).reshape(DEEP * rows, cols)
+    far_mask = swapped(terrain_mask, "gz", 1).reshape(layers * rows, cols)
+    far_rows = DEEP * rows
     (outgoing,) = kernel(
         functools.partial(route_kernel, tiles=tiles, capacity=capacity),
         "route",
         [((slots // 2, 128), F32)],
         [gz, live_counts, vertical_weights, era5_columns[0], column_owner],
         in_smem=2,
+        vmem_mib=60,
         cost=pl.CostEstimate(flops=1_000_000_000, bytes_accessed=1_000_000, transcendentals=0),
     )
     outgoing, far_mask, gx, gy, gz = lax.optimization_barrier((outgoing, far_mask, gx, gy, gz))
     received = lax.all_to_all(
         outgoing.reshape(tiles, capacity // 2, 128),
-        ("gx", "gy"),
+        ("gx", *GY),
         split_axis=0,
         concat_axis=0,
         tiled=True,
@@ -626,9 +632,10 @@
         scratch=[((halves, layers * rows, 128), F32)],
         in_smem=1,
         anywhere=(2, 6),
-    )
-    right = shifted(low_y, "gy", -1)
-    left = shifted(high_y, "gy", 1)
+        tail=6,
+    )
+    right = shifted(low_y, GY, -1)
+    left = shifted(high_y, GY, 1)
     edge, middle_0, low_x, high_x = kernel(
         functools.partial(edge_kernel, capacity=capacity),
         "edge",
@@ -642,6 +649,7 @@
         scratch=[((halves, layers * rows, 128), F32)],
         in_smem=1,
         anywhere=(5,),
+        tail=5,
         cost=pl.CostEstimate(flops=3_000_000_000, bytes_accessed=2_500_000, transcendentals=0),
     )
     corners = jnp.concatenate([right, left], axis=1)
@@ -658,13 +666,13 @@
     )
     middles = (middle_0, middle_1)
 
-    devices = tiles * lax.axis_size("gz")
+    near_group = lax.axis_size(("gx", "zl"))
     basis, moments = kernel(
         functools.partial(
-            basis_kernel, last_gx=lax.axis_size("gx") - 1, last_gy=lax.axis_size("gy") - 1
+            basis_kernel, last_gx=lax.axis_size("gx") - 1, last_gy=lax.axis_size(GY) - 1
         ),
         "basis",
-        [((3, LZ + 1, XR, YR), F32), ((devices, 128), F32)],
+        [((3, LZ + 1, XR, YR), F32), ((near_group, 128), F32)],
         [gx, gy, gz, edge, *middles, near_mask, far_mask, right, left, above, below],
         scratch=[
             ((YR // 128, XR * NS, 128), F32),
@@ -674,10 +682,17 @@
         ],
         in_smem=3,
         anywhere=(7, 8, 9, 10, 11),
+        tail=7,
     )
     moments = lax.all_to_all(
-        moments, ("gx", "gy", "gz"), split_axis=0, concat_axis=0, tiled=True
-    )
+        moments, ("gx", "zl"), split_axis=0, concat_axis=0, tiled=True
+    )
+    moments = jnp.sum(moments, axis=0, keepdims=True)
+    bit = 1
+    while bit < lax.axis_size("zh"):
+        moments = moments + swapped(moments, "zh", bit)
+        bit *= 2
+    other_moments = swapped(moments, "gz", 1)
     potential, wind_field, speed, balance = kernel(
         wind_kernel,
         "wind",
@@ -690,6 +705,7 @@
         [
             gz,
             moments,
+            other_moments,
             basis,
             *(piece.reshape(halves, -1, 128) for piece in (edge, *middles)),
             terrain_mask,
@@ -708,20 +724,25 @@
 
 
 def solution(mesh):
+    count_gx, count_gy, count_gz = mesh.devices.shape
+    near = math.gcd(count_gy, 4)
+    finer = jax.sharding.Mesh(
+        mesh.devices.reshape(count_gx, count_gy // near, near, count_gz), ("gx", *GY, "gz")
+    )
     placed = (
-        P(("gx", "gy"), None, "gz"),
-        P(("gx", "gy"), None),
-        P(("gx", "gy")),
+        P(("gx", *GY), None, "gz"),
+        P(("gx", *GY), None),
+        P(("gx", *GY)),
         P("gz", None),
-        P(None, "gx", "gy"),
-        P(None, "gx", "gy"),
-        P("gz", "gx", "gy"),
-        P(None, "gx", "gy"),
+        P(None, "gx", GY),
+        P(None, "gx", GY),
+        P("gz", "gx", GY),
+        P(None, "gx", GY),
     )
     return jax.shard_map(
         shards,
-        mesh=mesh,
+        mesh=finer,
         in_specs=placed,
-        out_specs=(P("gz", "gx", "gy"), P(None, "gz", "gx", "gy"), P(None, "gx", "gy")),
+        out_specs=(P("gz", "gx", GY), P(None, "gz", "gx", GY), P(None, "gx", GY)),
         check_vma=False,
     )

time: 93.7 us -> 101 us (1.078)
  waiting for transfers between devices: 3.01 us -> 9.92 us
  blocking collectives: 52.3 us -> 46 us
  starting transfers between devices: 16.5 us -> 21.1 us
  Pallas kernels: 16.5 us -> 18.2 us
    ppermute x3 -> x5, waiting for transfers between devices: 2.02 us -> 8.93 us  [swapped(): return lax.ppermute(block, axis, [(i, i ^ bit) for i in range(count)])]
    all_to_all x2, blocking collectives: 52.3 us -> 46 us  [the longest x1 28.2 us: shards(): lax.all_to_all(outgoing.reshape(tiles, capacity // 2, 128), ('gx', *GY),...]
    ppermute x3 -> x5, starting transfers between devices: 5.76 us -> 10.3 us  [swapped(): return lax.ppermute(block, axis, [(i, i ^ bit) for i in range(count)])]
    pallas_call x7, Pallas kernels: 16.5 us -> 18.2 us  [kernel(): pl.pallas_call(whole, out_shape=tuple((jax.ShapeDtypeStruct(shape, dtype)...]
    unnamed x15 -> x13, local copies, waits for them, and re-layouts: 2.44 us -> 3.55 us
  transfers between devices with their start and end apart: 7 -> 9, of which waited for: 4 -> 6; matrix products, arithmetic and copies ran while one was open for 0% -> 0% of each run, Pallas kernels for 8% -> 9%
where the time goes in v5:
time: 101 us; the launch traced here: 100 us
  blocking collectives  46 us (46%)
  starting transfers between devices  21.1 us (21%)
  Pallas kernels  18.2 us (18%)
  waiting for transfers between devices  9.92 us (10%)
  local copies, waits for them, and re-layouts  3.56 us (4%)
  between operations  1.59 us (2%)
    all_to_all x1, blocking collectives, shards(): lax.all_to_all(outgoing.reshape(tiles, capacity // 2, 128), ('gx', *GY),...  28.2 us
    pallas_call x7, Pallas kernels, kernel(): pl.pallas_call(whole, out_shape=tuple((jax.ShapeDtypeStruct(shape, dtype)...  18.2 us
    all_to_all x1, blocking collectives, shards(): lax.all_to_all(moments, ('gx', 'zl'), split_axis=0, concat_axis=0, tiled=...  17.8 us
    ppermute x4, starting transfers between devices, shifted(): return lax.ppermute(block, axis, pairs)  10.8 us
    ppermute x5, starting transfers between devices, swapped(): return lax.ppermute(block, axis, [(i, i ^ bit) for i in range(count)])  10.3 us
    ppermute x5, waiting for transfers between devices, swapped(): return lax.ppermute(block, axis, [(i, i ^ bit) for i in range(count)])  8.93 us
    unnamed x13, local copies, waits for them, and re-layouts  3.55 us
  transfers between devices with their start and end apart: 9, of which 6 were waited for; matrix products, arithmetic and copies ran while one was open for 0% of the time, Pallas kernels for 9%

profile of v5, /device:TPU:1, one launch (start us, length us, event | category | flops | bytes accessed | tf_op | source)
XLA Modules:
  0.0 100.4 jit_solution(8538763026336899455)
XLA Ops:
  0.6 0.0 copy-start
  0.7 3.3 %collective-permute-start = (s32[16,32,256]{2,1,0:T(8,128)}, s32[16,32,256]{2,1,0:T(8,128)S(1)}, u32[]{:S(2)}, u32[]{:S(2)}) collective-permute-start(s32[16,32,256]{2,1,0:T(8,128)} %refs_7_.1), channel_id=1, source_target_pairs={{0,1},{1,0},{2,3},{3,2},{4,5},{5,4},{6,7},{7,6},{8,9},{9,8},{10,11... | collective-permute-start | bytes 1572872 | tf_op jit(solution)/shard_map/ppermute | solution.py:542
  4.6 3.2 %route.1 = f32[512,128]{1,0:T(8,128)} custom-call(s32[1]{0:T(128)} %bitcast.refs_0_.refs_2_, s32[1]{0:T(128)S(6)} %copy.15.refs_1_, f32[16,32]{1,0:T(8,128)} %refs_2_.3, f32[1024,128]{1,0:T(8,128)} %bitcast.30, s32[1,1024]{1,0:T(1,128)} %refs_4_.2), custom_call_target="tpu_custom_call" | custom-call | flops 1000000000 | bytes 1000000 | tf_op jit(solution)/shard_map/route/pallas_call | solution.py:594
  7.9 0.0 collective-permute-done
  7.9 28.2 %all_to_all.14 = f32[128,4,128]{2,1,0:T(4,128)S(1)} all-to-all(f32[128,4,128]{2,1,0:T(4,128)} %bitcast.28), channel_id=1, replica_groups=mesh['gx'=16,'zh'=2,'zl'=4,'gz'=2] {'gx','zh','zl'}, dimensions={0} | all-to-all | bytes 524288 | tf_op jit(solution)/shard_map/all_to_all | solution.py:618
  36.1 1.6 %collective-permute-start.1 = (f32[512,128]{1,0:T(8,128)S(1)}, f32[512,128]{1,0:T(8,128)S(1)}, u32[]{:S(2)}, u32[]{:S(2)}) collective-permute-start(f32[512,128]{1,0:T(8,128)S(1)} %bitcast.25), channel_id=1, source_target_pairs={{0,1},{1,0},{2,3},{3,2},{4,5},{5,4},{6,7},{7,6},{8,9},{9,8},{10,11... | collective-permute-start | bytes 786440 | tf_op jit(solution)/shard_map/ppermute | solution.py:542
  37.7 1.2 %collective-permute-done.1.refs_2_ = f32[512,128]{1,0:T(8,128)S(1)} collective-permute-done((f32[512,128]{1,0:T(8,128)S(1)}, f32[512,128]{1,0:T(8,128)S(1)}, u32[]{:S(2)}, u32[]{:S(2)}) %collective-permute-start.1) | collective-permute-done | bytes 262176 | tf_op jit(solution)/shard_map/ppermute | solution.py:542
  38.8 0.0 copy-done
  38.9 0.9 table.1
  39.8 1.3 %collective-permute-start.2 = (f32[56,128]{1,0:T(8,128)S(1)}, f32[56,128]{1,0:T(8,128)S(1)}, u32[]{:S(2)}, u32[]{:S(2)}) collective-permute-start(f32[56,128]{1,0:T(8,128)S(1)} %get-tuple-element.57), channel_id=1, source_target_pairs={{2,0},{4,2},{6,4},{8,6},{10,8},{12,10},{14,12},{3,1},{5,3},{7,5},{... | collective-permute-start | bytes 86024 | tf_op jit(solution)/shard_map/ppermute | solution.py:537
  41.1 4.0 %collective-permute-start.3 = (f32[56,128]{1,0:T(8,128)S(1)}, f32[56,128]{1,0:T(8,128)S(1)}, u32[]{:S(2)}, u32[]{:S(2)}) collective-permute-start(f32[56,128]{1,0:T(8,128)S(1)} %get-tuple-element.58), channel_id=1, source_target_pairs={{0,2},{2,4},{4,6},{6,8},{8,10},{10,12},{12,14},{1,3},{3,5},{5,7},{... | collective-permute-start | bytes 86024 | tf_op jit(solution)/shard_map/ppermute | solution.py:537
  45.1 3.2 %edge.1 = (f32[2,8,40,128]{3,2,1,0:T(8,128)S(1)}, f32[2,8,40,128]{3,2,1,0:T(8,128)S(1)}, f32[248,256]{1,0:T(8,128)S(1)}, f32[248,256]{1,0:T(8,128)S(1)}) custom-call(s32[1]{0:T(128)} %bitcast.refs_0_.refs_2_, bf16[160,512]{1,0:T(8,128)(2,1)S(1)} %get-tuple-element.60.refs_1_.refs_0_, s32[4,32,256]{2,1,0:T(8,128)S(1)} %copy-done.3, ...), custom_call_target="tpu_custom_call" | custom-call | flops 3000000000 | bytes 2500000 | tf_op jit(solution)/shard_map/edge/pallas_call | solution.py:594
  48.3 0.0 collective-permute-done.2.refs_8_
  48.3 0.0 collective-permute-done.3.refs_9_
  48.4 1.3 %collective-permute-start.4 = (f32[248,256]{1,0:T(8,128)S(1)}, f32[248,256]{1,0:T(8,128)S(1)}, u32[]{:S(2)}, u32[]{:S(2)}) collective-permute-start(f32[248,256]{1,0:T(8,128)S(1)} %get-tuple-element.61), channel_id=1, source_target_pairs={{16,0},{32,16},{48,32},{64,48},{80,64},{96,80},{112,96},{128,112},... | collective-permute-start | bytes 761864 | tf_op jit(solution)/shard_map/ppermute | solution.py:537
  49.7 4.2 %collective-permute-start.5 = (f32[248,256]{1,0:T(8,128)S(1)}, f32[248,256]{1,0:T(8,128)S(1)}, u32[]{:S(2)}, u32[]{:S(2)}) collective-permute-start(f32[248,256]{1,0:T(8,128)S(1)} %get-tuple-element.62), channel_id=1, source_target_pairs={{0,16},{16,32},{32,48},{48,64},{64,80},{80,96},{96,112},{112,128},... | collective-permute-start | bytes 761864 | tf_op jit(solution)/shard_map/ppermute | solution.py:537
  53.8 3.0 %middle.1.refs_5_ = f32[2,16,40,128]{3,2,1,0:T(8,128)S(1)} custom-call(bf16[160,512]{1,0:T(8,128)(2,1)S(1)} %get-tuple-element.60.refs_1_.refs_0_, s32[4,32,256]{2,1,0:T(8,128)S(1)} %copy-done.3, f32[4,32,256]{2,1,0:T(8,128)S(1)} %copy-done.4), custom_call_target="tpu_custom_call" | custom-call | flops 3000000000 | bytes 1600000 | tf_op jit(solution)/shard_map/middle/pallas_call | solution.py:594
  56.8 0.1 collective-permute-done.4.refs_10_
  56.9 0.9 collective-permute-done.5.refs_11_
  57.8 4.8 %basis.1 = (f32[3,17,40,384]{3,2,1,0:T(8,128)S(1)}, f32[64,128]{1,0:T(8,128)S(1)}) custom-call(s32[1]{0:T(128)} %bitcast.3.refs_0_, s32[1]{0:T(128)} %bitcast.4.refs_1_, s32[1]{0:T(128)} %bitcast.refs_0_.refs_2_, f32[2,8,40,128]{3,2,1,0:T(8,128)S(1)} %get-tuple-element.54.refs_3_, f32[2,8,40,128]{3,2,1,0:T(8,128)S(1)} %get-tuple-element.55.refs_4_, ...), custom_call_target="tpu_custom_call" | custom-call | tf_op jit(solution)/shard_map/basis/pallas_call | solution.py:594
  62.7 1.6 %copy-done.1 = f32[3,17,40,384]{3,2,1,0:T(8,128)} copy-done((f32[3,17,40,384]{3,2,1,0:T(8,128)}, f32[3,17,40,384]{3,2,1,0:T(8,128)S(1)}, u32[]{:S(2)}) %copy-start.1) | copy-done | bytes 3133464
  64.3 17.8 %all_to_all.15 = f32[64,1,128]{2,1,0:T(1,128)S(1)} all-to-all(f32[64,1,128]{2,1,0:T(1,128)S(1)} %bitcast.27), channel_id=1, replica_groups=mesh['gx'=16,'zh'=2,'zl'=4,'gz'=2] {'gx','zl'}, dimensions={0} | all-to-all | bytes 65536 | tf_op jit(solution)/shard_map/all_to_all | solution.py:687
  82.1 0.1 reduce_sum.9
  82.2 0.3 collective-permute-start.6
  82.5 6.0 %collective-permute-done.6 = f32[1,128]{1,0:T(1,128)S(1)} collective-permute-done((f32[1,128]{1,0:T(1,128)S(1)}, f32[1,128]{1,0:T(1,128)S(1)}, u32[]{:S(2)}, u32[]{:S(2)}) %collective-permute-start.6) | collective-permute-done | bytes 544 | tf_op jit(solution)/shard_map/ppermute | solution.py:542
  88.6 4.7 %collective-permute-start.7 = (f32[1,128]{1,0:T(1,128)S(1)}, f32[1,128]{1,0:T(1,128)S(1)}, u32[]{:S(2)}, u32[]{:S(2)}) collective-permute-start(f32[1,128]{1,0:T(1,128)S(1)} %bitcast_add_fusion.refs_1_), channel_id=1, source_target_pairs={{0,1},{1,0},{2,3},{3,2},{4,5},{5,4},{6,7},{7,6},{8,9},{9,8},{10,11... | collective-permute-start | bytes 1544 | tf_op jit(solution)/shard_map/ppermute | solution.py:542
  93.3 0.8 collective-permute-done.7.refs_2_
  94.1 1.9 %copy-done.2 = f32[3,17,40,384]{3,2,1,0:T(8,128)S(1)} copy-done((f32[3,17,40,384]{3,2,1,0:T(8,128)S(1)}, f32[3,17,40,384]{3,2,1,0:T(8,128)}, u32[]{:S(2)}) %copy-start.2) | copy-done | bytes 3133464
  96.0 2.3 %wind.1 = (f32[16,32,256]{2,1,0:T(8,128)}, f32[3,16,32,256]{3,2,1,0:T(8,128)}, f32[32,256]{1,0:T(8,128)S(1)}, f32[32,256]{1,0:T(8,128)S(1)}) custom-call(s32[1]{0:T(128)} %bitcast.refs_0_.refs_2_, f32[1,128]{1,0:T(1,128)S(1)} %bitcast_add_fusion.refs_1_, f32[1,128]{1,0:T(1,128)S(1)} %collective-permute-done.7.refs_2_, f32[3,17,40,384]{3,2,1,0:T(8,128)S(1)} %copy-done.2, ...), custom_call_target="tpu_custom_call" | custom-call | tf_op jit(solution)/shard_map/wind/pallas_call | solution.py:594
  98.3 0.3 collective-permute-start.8
  98.6 0.9 collective-permute-done.8.refs_1_
  99.5 0.7 fuel.1
  (12 shorter events, 0.0 us)
Async XLA Ops:
  0.6 38.2 %copy-start = (s32[16,32,256]{2,1,0:T(8,128)S(1)}, s32[16,32,256]{2,1,0:T(8,128)}, u32[]{:S(2)}) copy-start(s32[16,32,256]{2,1,0:T(8,128)} %refs_7_.1) | copy-start | bytes 1572868
  0.6 38.2 %copy-start.4 = (f32[4,32,256]{2,1,0:T(8,128)S(1)}, f32[4,32,256]{2,1,0:T(8,128)}, u32[]{:S(2)}) copy-start(f32[4,32,256]{2,1,0:T(8,128)} %refs_2_.5) | copy-start | bytes 393220
  0.7 38.2 %copy-start.3 = (s32[4,32,256]{2,1,0:T(8,128)S(1)}, s32[4,32,256]{2,1,0:T(8,128)}, u32[]{:S(2)}) copy-start(s32[4,32,256]{2,1,0:T(8,128)} %refs_1_.2) | copy-start | bytes 393220
  0.7 7.2 %collective-permute-start = (s32[16,32,256]{2,1,0:T(8,128)}, s32[16,32,256]{2,1,0:T(8,128)S(1)}, u32[]{:S(2)}, u32[]{:S(2)}) collective-permute-start(s32[16,32,256]{2,1,0:T(8,128)} %refs_7_.1), channel_id=1, source_target_pairs={{0,1},{1,0},{2,3},{3,2},{4,5},{5,4},{6,7},{7,6},{8,9},{9,8},{10,11... | collective-permute-start | bytes 1572872 | tf_op jit(solution)/shard_map/ppermute | solution.py:542
  36.1 2.8 %collective-permute-start.1 = (f32[512,128]{1,0:T(8,128)S(1)}, f32[512,128]{1,0:T(8,128)S(1)}, u32[]{:S(2)}, u32[]{:S(2)}) collective-permute-start(f32[512,128]{1,0:T(8,128)S(1)} %bitcast.25), channel_id=1, source_target_pairs={{0,1},{1,0},{2,3},{3,2},{4,5},{5,4},{6,7},{7,6},{8,9},{9,8},{10,11... | collective-permute-start | bytes 786440 | tf_op jit(solution)/shard_map/ppermute | solution.py:542
  39.8 8.5 %collective-permute-start.2 = (f32[56,128]{1,0:T(8,128)S(1)}, f32[56,128]{1,0:T(8,128)S(1)}, u32[]{:S(2)}, u32[]{:S(2)}) collective-permute-start(f32[56,128]{1,0:T(8,128)S(1)} %get-tuple-element.57), channel_id=1, source_target_pairs={{2,0},{4,2},{6,4},{8,6},{10,8},{12,10},{14,12},{3,1},{5,3},{7,5},{... | collective-permute-start | bytes 86024 | tf_op jit(solution)/shard_map/ppermute | solution.py:537
  41.1 7.3 %collective-permute-start.3 = (f32[56,128]{1,0:T(8,128)S(1)}, f32[56,128]{1,0:T(8,128)S(1)}, u32[]{:S(2)}, u32[]{:S(2)}) collective-permute-start(f32[56,128]{1,0:T(8,128)S(1)} %get-tuple-element.58), channel_id=1, source_target_pairs={{0,2},{2,4},{4,6},{6,8},{8,10},{10,12},{12,14},{1,3},{3,5},{5,7},{... | collective-permute-start | bytes 86024 | tf_op jit(solution)/shard_map/ppermute | solution.py:537
  48.4 8.6 %collective-permute-start.4 = (f32[248,256]{1,0:T(8,128)S(1)}, f32[248,256]{1,0:T(8,128)S(1)}, u32[]{:S(2)}, u32[]{:S(2)}) collective-permute-start(f32[248,256]{1,0:T(8,128)S(1)} %get-tuple-element.61), channel_id=1, source_target_pairs={{16,0},{32,16},{48,32},{64,48},{80,64},{96,80},{112,96},{128,112},... | collective-permute-start | bytes 761864 | tf_op jit(solution)/shard_map/ppermute | solution.py:537
  49.7 8.2 %collective-permute-start.5 = (f32[248,256]{1,0:T(8,128)S(1)}, f32[248,256]{1,0:T(8,128)S(1)}, u32[]{:S(2)}, u32[]{:S(2)}) collective-permute-start(f32[248,256]{1,0:T(8,128)S(1)} %get-tuple-element.62), channel_id=1, source_target_pairs={{0,16},{16,32},{32,48},{48,64},{64,80},{80,96},{96,112},{112,128},... | collective-permute-start | bytes 761864 | tf_op jit(solution)/shard_map/ppermute | solution.py:537
  62.7 1.7 %copy-start.1 = (f32[3,17,40,384]{3,2,1,0:T(8,128)}, f32[3,17,40,384]{3,2,1,0:T(8,128)S(1)}, u32[]{:S(2)}) copy-start(f32[3,17,40,384]{3,2,1,0:T(8,128)S(1)} %get-tuple-element.64.refs_3_) | copy-start | bytes 9400324
  64.3 35.2 %copy-start.5 = (f32[3,32,256]{2,1,0:T(8,128)S(1)}, f32[3,32,256]{2,1,0:T(8,128)}, u32[]{:S(2)}) copy-start(f32[3,32,256]{2,1,0:T(8,128)} %refs_3_.5) | copy-start | bytes 294916
  82.2 6.4 %collective-permute-start.6 = (f32[1,128]{1,0:T(1,128)S(1)}, f32[1,128]{1,0:T(1,128)S(1)}, u32[]{:S(2)}, u32[]{:S(2)}) collective-permute-start(f32[1,128]{1,0:T(1,128)S(1)} %bitcast.29), channel_id=1, source_target_pairs={{0,8},{8,0},{1,9},{9,1},{2,10},{10,2},{3,11},{11,3},{4,12},{12,4},... | collective-permute-start | bytes 1544 | tf_op jit(solution)/shard_map/ppermute | solution.py:542
  88.6 5.5 %collective-permute-start.7 = (f32[1,128]{1,0:T(1,128)S(1)}, f32[1,128]{1,0:T(1,128)S(1)}, u32[]{:S(2)}, u32[]{:S(2)}) collective-permute-start(f32[1,128]{1,0:T(1,128)S(1)} %bitcast_add_fusion.refs_1_), channel_id=1, source_target_pairs={{0,1},{1,0},{2,3},{3,2},{4,5},{5,4},{6,7},{7,6},{8,9},{9,8},{10,11... | collective-permute-start | bytes 1544 | tf_op jit(solution)/shard_map/ppermute | solution.py:542
  94.1 1.9 %copy-start.2 = (f32[3,17,40,384]{3,2,1,0:T(8,128)S(1)}, f32[3,17,40,384]{3,2,1,0:T(8,128)}, u32[]{:S(2)}) copy-start(f32[3,17,40,384]{3,2,1,0:T(8,128)} %copy-done.1) | copy-start | bytes 9400324
  98.3 1.2 %collective-permute-start.8 = (f32[32,256]{1,0:T(8,128)S(1)}, f32[32,256]{1,0:T(8,128)S(1)}, u32[]{:S(2)}, u32[]{:S(2)}) collective-permute-start(f32[32,256]{1,0:T(8,128)S(1)} %get-tuple-element.67.refs_0_), channel_id=1, source_target_pairs={{0,1},{1,0},{2,3},{3,2},{4,5},{5,4},{6,7},{7,6},{8,9},{9,8},{10,11... | collective-permute-start | bytes 98312 | tf_op jit(solution)/shard_map/ppermute | solution.py:542

commit v6 on v5

--- a/solution.py
+++ b/solution.py
@@ -22,7 +22,9 @@
 YR = 384
 
 
-GY = ("zh", "zl")
+SPLIT = 8
+PROFILE = 60
+GY = ("gy",)
 
 
 def split(value):
@@ -34,9 +36,7 @@
     return lax.dot_general(a, b, (((1,), (1,)), ((), ())), preferred_element_type=F32)
 
 
-def route_kernel(
-    gz_ref, live_ref, weights_ref, columns_ref, owner_ref, out_ref, *, tiles, capacity
-):
+def profile_kernel(gz_ref, weights_ref, columns_ref, own_ref, leaving_ref):
     plain = weights_ref[...]
     turned = jnp.concatenate([plain[LZ - 1 - i : LZ - i] for i in range(LZ)], axis=0)
     weights = jnp.where(gz_ref[0] == 0, plain, turned)
@@ -58,7 +58,11 @@
     w_high, w_low = split(stack)
     c_high, c_low = split(columns_ref[...])
     profile = dot_nt(w_high, c_high) + dot_nt(w_high, c_low) + dot_nt(w_low, c_high)
-
+    own_ref[...] = profile[:NF]
+    leaving_ref[...] = profile[NF:]
+
+
+def rank_kernel(live_ref, owner_ref, target_ref, *, tiles, capacity):
     rows = owner_ref.shape[1]
     slots = tiles * capacity
     half = capacity // 2
@@ -74,10 +78,19 @@
     )
     rank = jnp.sum(hits * before, axis=0, keepdims=True).astype(jnp.int32)
     upper = jnp.where(rank >= half, 1, 0)
-    target = jnp.where(owner >= 0, owner * half + rank + upper * (slots // 2 - half), -1)
+    target_ref[...] = jnp.where(
+        owner >= 0, owner * half + rank + upper * (slots // 2 - half), -1
+    )
+
+
+def place_kernel(target_ref, own_ref, other_ref, out_ref):
+    slots = 2 * out_ref.shape[0]
+    rows = target_ref.shape[1]
+    profile = jnp.concatenate([own_ref[: NF - 8], own_ref[NF - 8 :] + other_ref[...]], axis=0)
+    target = target_ref[...]
     place = lax.broadcasted_iota(jnp.int32, (slots, rows), 0) == target
     high, low = split(profile)
-    pad = jnp.zeros((64 - NF - 8, rows), BF16)
+    pad = jnp.zeros((64 - NF, rows), BF16)
     both = jnp.concatenate([high, pad, low, pad], axis=0)
     placed = dot_nt(jnp.where(place, 1.0, 0.0).astype(BF16), both)
     placed = placed + pltpu.roll(placed, 64, 1)
@@ -85,10 +98,9 @@
     out_ref[...] = jnp.where(lane < 64, placed[: slots // 2], placed[slots // 2 :])
 
 
-def fill_table(received_ref, other_ref, table_ref):
+def fill_table(received_ref, table_ref):
     blocks = received_ref.shape[0] // 256
     turned = [jnp.transpose(received_ref[256 * p : 256 * p + 256, :]) for p in range(blocks)]
-    beyond = [jnp.transpose(other_ref[256 * p : 256 * p + 256, :]) for p in range(blocks)]
     parts = 2 * blocks
     for g in range(NF // 8):
         value = jnp.concatenate(
@@ -99,15 +111,6 @@
             ],
             axis=0,
         )
-        if g == NF // 8 - 1:
-            value = value + jnp.concatenate(
-                [
-                    beyond[p][64 * side + NF : 64 * side + NF + 8]
-                    for side in range(2)
-                    for p in range(blocks)
-                ],
-                axis=0,
-            )
         rows = slice(8 * parts * g, 8 * parts * (g + 1))
         table_ref[rows, 0:256], table_ref[rows, 256:512] = split(value)
 
@@ -176,11 +179,11 @@
 
 
 def table_kernel(
-    gz_ref, received_ref, other_ref, index_ref, weight_ref, mask_ref, far_mask_ref,
+    gz_ref, received_ref, index_ref, weight_ref, mask_ref, far_mask_ref,
     table_ref, low_y_ref, high_y_ref, mask_f_ref, *, capacity
 ):
     points, rows, cols = index_ref.shape
-    fill_table(received_ref, other_ref, table_ref)
+    fill_table(received_ref, table_ref)
     fill_mask(gz_ref[0] == 0, mask_ref, far_mask_ref, mask_f_ref)
     lane = lax.broadcasted_iota(jnp.int32, (8, 128), 1)
     row = lax.broadcasted_iota(jnp.int32, (8, 128), 0)
@@ -238,7 +241,7 @@
                 else:
                     out[NS * 3 : NS * 3 + 16, at] = edge_ref[h, kept, 0:16]
                     out[NS * 3 + 16 : NS * 3 + 24, at] = edge_ref[h, kept, 32:40]
-    pick_rows(table_ref, index_ref, weight_ref, list(range(4, 12)), middle_ref, capacity)
+    pick_rows(table_ref, index_ref, weight_ref, list(range(4, SPLIT)), middle_ref, capacity)
 
 
 def middle_kernel(table_ref, index_ref, weight_ref, middle_ref, *, first, capacity):
@@ -251,7 +254,7 @@
         return edge_ref, x
     if x >= rows - 4:
         return edge_ref, x - rows + 8
-    return (middle_refs[0], x - 4) if x < 12 else (middle_refs[1], x - 12)
+    return (middle_refs[0], x - 4) if x < SPLIT else (middle_refs[1], x - SPLIT)
 
 
 def ring_smooth(plane):
@@ -453,7 +456,7 @@
 
 
 def wind_kernel(
-    gz_ref, moments_ref, other_moments_ref, basis_ref, edge_ref, middle_0_ref, middle_1_ref, mask_ref,
+    gz_ref, moments_ref, basis_ref, edge_ref, middle_0_ref, middle_1_ref, mask_ref,
     potential_ref, wind_ref, speed_ref, balance_ref, p_ref, grid_ref
 ):
     gz = gz_ref[0]
@@ -461,10 +464,10 @@
     near = 4 * NF
     for h in range(cols // 128):
         grid_ref[h, 0:near] = edge_ref[h, 0:near]
-        grid_ref[h, near : near + 8 * NF] = middle_0_ref[h]
-        grid_ref[h, near + 8 * NF : (rows - 4) * NF] = middle_1_ref[h]
+        grid_ref[h, near : SPLIT * NF] = middle_0_ref[h]
+        grid_ref[h, SPLIT * NF : (rows - 4) * NF] = middle_1_ref[h]
         grid_ref[h, (rows - 4) * NF :] = edge_ref[h, near:]
-    totals = moments_ref[...] + other_moments_ref[...]
+    totals = jnp.sum(moments_ref[...], axis=0, keepdims=True)
     factors = iterate([totals[:, k : k + 1] for k in range(6)])
     factors = [jnp.broadcast_to(c, (8, 128)) for c in factors]
     factors = [jnp.tile(c, (XR // 8, YR // 128)) for c in factors]
@@ -605,14 +608,29 @@
     near_mask = terrain_mask.reshape(layers * rows, cols)
     far_mask = swapped(terrain_mask, "gz", 1).reshape(layers * rows, cols)
     far_rows = DEEP * rows
+    own, leaving = kernel(
+        profile_kernel,
+        "profile",
+        [((NF, rows_in), F32), ((8, rows_in), F32)],
+        [gz, vertical_weights, era5_columns[0]],
+        in_smem=1,
+        vmem_mib=PROFILE,
+    )
+    other = swapped(leaving, "gz", 1)
+    (target,) = kernel(
+        functools.partial(rank_kernel, tiles=tiles, capacity=capacity),
+        "rank",
+        [((1, rows_in), jnp.int32)],
+        [live_counts, column_owner],
+        in_smem=1,
+        cost=pl.CostEstimate(flops=300_000_000, bytes_accessed=3_000_000, transcendentals=0),
+    )
+    target, other = lax.optimization_barrier((target, other))
     (outgoing,) = kernel(
-        functools.partial(route_kernel, tiles=tiles, capacity=capacity),
-        "route",
+        place_kernel,
+        "place",
         [((slots // 2, 128), F32)],
-        [gz, live_counts, vertical_weights, era5_columns[0], column_owner],
-        in_smem=2,
-        vmem_mib=60,
-        cost=pl.CostEstimate(flops=1_000_000_000, bytes_accessed=1_000_000, transcendentals=0),
+        [target, own, other],
     )
     outgoing, far_mask, gx, gy, gz = lax.optimization_barrier((outgoing, far_mask, gx, gy, gz))
     received = lax.all_to_all(
@@ -622,17 +640,15 @@
         concat_axis=0,
         tiled=True,
     ).reshape(slots // 2, 128)
-    other = swapped(received, "gz", 1)
-
     table, low_y, high_y = kernel(
         functools.partial(table_kernel, capacity=capacity),
         "table",
         [((slots // 256 * NF, 512), BF16), ((NS, 128), F32), ((NS, 128), F32)],
-        [gz, received, other, stencil_index, stencil_weight, near_mask, far_mask],
+        [gz, received, stencil_index, stencil_weight, near_mask, far_mask],
         scratch=[((halves, layers * rows, 128), F32)],
         in_smem=1,
-        anywhere=(2, 6),
-        tail=6,
+        anywhere=(5,),
+        tail=5,
     )
     right = shifted(low_y, GY, -1)
     left = shifted(high_y, GY, 1)
@@ -641,7 +657,7 @@
         "edge",
         [
             ((halves, 8, NF, 128), F32),
-            ((halves, 8, NF, 128), F32),
+            ((halves, SPLIT - 4, NF, 128), F32),
             ((STRIP + NS, cols), F32),
             ((STRIP + NS, cols), F32),
         ],
@@ -658,21 +674,21 @@
     above = shifted(low_x, "gx", -1)
     below = shifted(high_x, "gx", 1)
     (middle_1,) = kernel(
-        functools.partial(middle_kernel, first=12, capacity=capacity),
+        functools.partial(middle_kernel, first=SPLIT, capacity=capacity),
         "middle",
-        [((halves, rows - 16, NF, 128), F32)],
+        [((halves, rows - 4 - SPLIT, NF, 128), F32)],
         [table, stencil_index, stencil_weight],
         cost=pl.CostEstimate(flops=3_000_000_000, bytes_accessed=1_600_000, transcendentals=0),
     )
     middles = (middle_0, middle_1)
 
-    near_group = lax.axis_size(("gx", "zl"))
+    devices = tiles * lax.axis_size("gz")
     basis, moments = kernel(
         functools.partial(
             basis_kernel, last_gx=lax.axis_size("gx") - 1, last_gy=lax.axis_size(GY) - 1
         ),
         "basis",
-        [((3, LZ + 1, XR, YR), F32), ((near_group, 128), F32)],
+        [((3, LZ + 1, XR, YR), F32), ((devices, 128), F32)],
         [gx, gy, gz, edge, *middles, near_mask, far_mask, right, left, above, below],
         scratch=[
             ((YR // 128, XR * NS, 128), F32),
@@ -685,14 +701,8 @@
         tail=7,
     )
     moments = lax.all_to_all(
-        moments, ("gx", "zl"), split_axis=0, concat_axis=0, tiled=True
-    )
-    moments = jnp.sum(moments, axis=0, keepdims=True)
-    bit = 1
-    while bit < lax.axis_size("zh"):
-        moments = moments + swapped(moments, "zh", bit)
-        bit *= 2
-    other_moments = swapped(moments, "gz", 1)
+        moments, ("gx", *GY, "gz"), split_axis=0, concat_axis=0, tiled=True
+    )
     potential, wind_field, speed, balance = kernel(
         wind_kernel,
         "wind",
@@ -705,7 +715,6 @@
         [
             gz,
             moments,
-            other_moments,
             basis,
             *(piece.reshape(halves, -1, 128) for piece in (edge, *middles)),
             terrain_mask,
@@ -724,11 +733,6 @@
 
 
 def solution(mesh):
-    count_gx, count_gy, count_gz = mesh.devices.shape
-    near = math.gcd(count_gy, 4)
-    finer = jax.sharding.Mesh(
-        mesh.devices.reshape(count_gx, count_gy // near, near, count_gz), ("gx", *GY, "gz")
-    )
     placed = (
         P(("gx", *GY), None, "gz"),
         P(("gx", *GY), None),
@@ -741,7 +745,7 @@
     )
     return jax.shard_map(
         shards,
-        mesh=finer,
+        mesh=mesh,
         in_specs=placed,
         out_specs=(P("gz", "gx", GY), P(None, "gz", "gx", GY), P(None, "gx", GY)),
         check_vma=False,

time: 101 us -> 95 us (0.941)
  waiting for transfers between devices: 9.92 us -> 0.88 us
  blocking collectives: 46 us -> 54.2 us
  starting transfers between devices: 21.1 us -> 15.1 us
    all_to_all x1, blocking collectives: 17.8 us -> 26.6 us  [shards(): lax.all_to_all(moments, ('gx', *GY, 'gz'), split_axis=0, concat_axis=0, t...]
    ppermute x5 -> x3, waiting for transfers between devices: 8.93 us -> 0.87 us  [swapped(): return lax.ppermute(block, axis, [(i, i ^ bit) for i in range(count)])]
    ppermute x5 -> x3, starting transfers between devices: 10.3 us -> 4.3 us  [swapped(): return lax.ppermute(block, axis, [(i, i ^ bit) for i in range(count)])]
    unnamed x13 -> x19, local copies, waits for them, and re-layouts: 3.55 us -> 4.47 us
    pallas_call x7 -> x9, Pallas kernels: 18.2 us -> 18.3 us  [kernel(): pl.pallas_call(whole, out_shape=tuple((jax.ShapeDtypeStruct(shape, dtype)...]
  transfers between devices with their start and end apart: 9 -> 7, of which waited for: 6 -> 1; matrix products, arithmetic and copies ran while one was open for 0% -> 0% of each run, Pallas kernels for 9% -> 10%
where the time goes in v6:
time: 95 us; the launch traced here: 94.6 us
  blocking collectives  54.2 us (57%)
  Pallas kernels  18.3 us (19%)
  starting transfers between devices  15.1 us (16%)
  local copies, waits for them, and re-layouts  4.49 us (5%)
  between operations  1.67 us (2%)
    all_to_all x1, blocking collectives, shards(): lax.all_to_all(outgoing.reshape(tiles, capacity // 2, 128), ('gx', *GY),...  27.6 us
    all_to_all x1, blocking collectives, shards(): lax.all_to_all(moments, ('gx', *GY, 'gz'), split_axis=0, concat_axis=0, t...  26.6 us
    pallas_call x9, Pallas kernels, kernel(): pl.pallas_call(whole, out_shape=tuple((jax.ShapeDtypeStruct(shape, dtype)...  18.3 us
    ppermute x4, starting transfers between devices, shifted(): return lax.ppermute(block, axis, pairs)  10.8 us
    unnamed x19, local copies, waits for them, and re-layouts  4.47 us
    ppermute x3, starting transfers between devices, swapped(): return lax.ppermute(block, axis, [(i, i ^ bit) for i in range(count)])  4.3 us
  transfers between devices with their start and end apart: 7, of which 1 were waited for; matrix products, arithmetic and copies ran while one was open for 0% of the time, Pallas kernels for 10%

profile of v6, /device:TPU:1, one launch (start us, length us, event | category | flops | bytes accessed | tf_op | source)
XLA Modules:
  0.0 94.6 jit_solution(9701737267474603238)
XLA Ops:
  0.6 0.0 copy-start.1
  0.6 0.0 copy-start.6
  0.7 0.0 copy-start.4
  0.7 3.3 %collective-permute-start.1 = (s32[16,32,256]{2,1,0:T(8,128)}, s32[16,32,256]{2,1,0:T(8,128)S(1)}, u32[]{:S(2)}, u32[]{:S(2)}) collective-permute-start(s32[16,32,256]{2,1,0:T(8,128)} %refs_6_.1), channel_id=1, source_target_pairs={{0,1},{1,0},{2,3},{3,2},{4,5},{5,4},{6,7},{7,6},{8,9},{9,8},{10,11... | collective-permute-start | bytes 1572872 | tf_op jit(solution)/shard_map/ppermute | solution.py:545
  4.0 2.1 %profile.1 = (f32[40,1024]{1,0:T(8,128)}, f32[8,1024]{1,0:T(8,128)}) custom-call(s32[1]{0:T(128)} %bitcast.refs_0_.refs_2_, f32[16,32]{1,0:T(8,128)} %refs_1_.4, f32[1024,128]{1,0:T(8,128)} %bitcast.28), custom_call_target="tpu_custom_call" | custom-call | tf_op jit(solution)/shard_map/profile/pallas_call | solution.py:597
  6.1 0.1 collective-permute-start
  6.8 0.0 copy-start.8
  6.9 0.7 copy-done.8
  7.5 0.5 rank.1.refs_0_
  8.0 0.0 collective-permute-done.refs_2_
  8.0 0.0 copy-start.2
  8.0 0.9 copy-done.2
  8.9 0.8 place.1
  9.7 0.0 collective-permute-done.1
  9.7 27.6 %all_to_all.16 = f32[128,4,128]{2,1,0:T(4,128)S(1)} all-to-all(f32[128,4,128]{2,1,0:T(4,128)S(1)} %bitcast.23), channel_id=1, replica_groups=mesh['gx'=16,'gy'=8,'gz'=2] {'gx','gy'}, dimensions={0} | all-to-all | bytes 524288 | tf_op jit(solution)/shard_map/all_to_all | solution.py:636
  37.3 1.0 %copy-done = s32[16,32,256]{2,1,0:T(8,128)S(1)} copy-done((s32[16,32,256]{2,1,0:T(8,128)S(1)}, s32[16,32,256]{2,1,0:T(8,128)}, u32[]{:S(2)}) %copy-start) | copy-done | bytes 524312
  38.4 0.9 copy-done.3
  39.3 0.9 copy-done.5
  40.2 0.8 table.1
  41.0 1.3 %collective-permute-start.2 = (f32[56,128]{1,0:T(8,128)S(1)}, f32[56,128]{1,0:T(8,128)S(1)}, u32[]{:S(2)}, u32[]{:S(2)}) collective-permute-start(f32[56,128]{1,0:T(8,128)S(1)} %get-tuple-element.65), channel_id=1, source_target_pairs={{2,0},{4,2},{6,4},{8,6},{10,8},{12,10},{14,12},{3,1},{5,3},{7,5},{... | collective-permute-start | bytes 86024 | tf_op jit(solution)/shard_map/ppermute | solution.py:540
  42.3 4.0 %collective-permute-start.3 = (f32[56,128]{1,0:T(8,128)S(1)}, f32[56,128]{1,0:T(8,128)S(1)}, u32[]{:S(2)}, u32[]{:S(2)}) collective-permute-start(f32[56,128]{1,0:T(8,128)S(1)} %get-tuple-element.66), channel_id=1, source_target_pairs={{0,2},{2,4},{4,6},{6,8},{8,10},{10,12},{12,14},{1,3},{3,5},{5,7},{... | collective-permute-start | bytes 86024 | tf_op jit(solution)/shard_map/ppermute | solution.py:540
  46.3 2.5 %edge.1 = (f32[2,8,40,128]{3,2,1,0:T(8,128)S(1)}, f32[2,4,40,128]{3,2,1,0:T(8,128)S(1)}, f32[248,256]{1,0:T(8,128)S(1)}, f32[248,256]{1,0:T(8,128)S(1)}) custom-call(s32[1]{0:T(128)} %bitcast.refs_0_.refs_2_, bf16[160,512]{1,0:T(8,128)(2,1)S(1)} %get-tuple-element.68.refs_1_.refs_0_, s32[4,32,256]{2,1,0:T(8,128)S(1)} %copy-done.4, ...), custom_call_target="tpu_custom_call" | custom-call | flops 3000000000 | bytes 2500000 | tf_op jit(solution)/shard_map/edge/pallas_call | solution.py:597
  48.9 1.3 %collective-permute-start.4 = (f32[248,256]{1,0:T(8,128)S(1)}, f32[248,256]{1,0:T(8,128)S(1)}, u32[]{:S(2)}, u32[]{:S(2)}) collective-permute-start(f32[248,256]{1,0:T(8,128)S(1)} %get-tuple-element.69), channel_id=1, source_target_pairs={{16,0},{32,16},{48,32},{64,48},{80,64},{96,80},{112,96},{128,112},... | collective-permute-start | bytes 761864 | tf_op jit(solution)/shard_map/ppermute | solution.py:540
  50.2 4.2 %collective-permute-start.5 = (f32[248,256]{1,0:T(8,128)S(1)}, f32[248,256]{1,0:T(8,128)S(1)}, u32[]{:S(2)}, u32[]{:S(2)}) collective-permute-start(f32[248,256]{1,0:T(8,128)S(1)} %get-tuple-element.70), channel_id=1, source_target_pairs={{0,16},{16,32},{32,48},{48,64},{64,80},{80,96},{96,112},{112,128},... | collective-permute-start | bytes 761864 | tf_op jit(solution)/shard_map/ppermute | solution.py:540
  54.4 3.7 %middle.1.refs_5_ = f32[2,20,40,128]{3,2,1,0:T(8,128)S(1)} custom-call(bf16[160,512]{1,0:T(8,128)(2,1)S(1)} %get-tuple-element.68.refs_1_.refs_0_, s32[4,32,256]{2,1,0:T(8,128)S(1)} %copy-done.4, f32[4,32,256]{2,1,0:T(8,128)S(1)} %copy-done.6), custom_call_target="tpu_custom_call" | custom-call | flops 3000000000 | bytes 1600000 | tf_op jit(solution)/shard_map/middle/pallas_call | solution.py:597
  58.1 4.9 %basis.1 = (f32[3,17,40,384]{3,2,1,0:T(8,128)S(1)}, f32[256,128]{1,0:T(8,128)S(1)}) custom-call(s32[1]{0:T(128)} %bitcast.3.refs_0_, s32[1]{0:T(128)} %bitcast.4.refs_1_, s32[1]{0:T(128)} %bitcast.refs_0_.refs_2_, f32[2,8,40,128]{3,2,1,0:T(8,128)S(1)} %get-tuple-element.62.refs_3_, f32[2,4,40,128]{3,2,1,0:T(8,128)S(1)} %get-tuple-element.63.refs_4_, ...), custom_call_target="tpu_custom_call" | custom-call | tf_op jit(solution)/shard_map/basis/pallas_call | solution.py:597
  63.0 0.0 copy-start.7
  63.0 26.6 %all_to_all.17 = f32[256,1,128]{2,1,0:T(1,128)S(1)} all-to-all(f32[256,1,128]{2,1,0:T(1,128)S(1)} %bitcast.27), channel_id=1, replica_groups=mesh['gx'=16,'gy'=8,'gz'=2] {'gx','gy','gz'}, dimensions={0} | all-to-all | bytes 262144 | tf_op jit(solution)/shard_map/all_to_all | solution.py:703
  89.6 2.3 %wind.1 = (f32[16,32,256]{2,1,0:T(8,128)}, f32[3,16,32,256]{3,2,1,0:T(8,128)}, f32[32,256]{1,0:T(8,128)S(1)}, f32[32,256]{1,0:T(8,128)S(1)}) custom-call(s32[1]{0:T(128)} %bitcast.refs_0_.refs_2_, f32[256,128]{1,0:T(8,128)S(1)} %bitcast.26, f32[3,17,40,384]{3,2,1,0:T(8,128)S(1)} %get-tuple-element.72.refs_2_, f32[2,320,128]{2,1,0:T(8,128)S(1)} %bitcast.22, ...), custom_call_target="tpu_custom_call" | custom-call | tf_op jit(solution)/shard_map/wind/pallas_call | solution.py:597
  91.9 0.9 collective-permute-start.6
  92.8 0.9 collective-permute-done.6.refs_1_
  93.7 0.7 fuel.1
  (14 shorter events, 0.0 us)
Async XLA Ops:
  0.6 45.7 %copy-start.1 = (s32[16,32,256]{2,1,0:T(8,128)S(1)}, s32[16,32,256]{2,1,0:T(8,128)}, u32[]{:S(2)}) copy-start(s32[16,32,256]{2,1,0:T(8,128)} %refs_6_.1) | copy-start | bytes 1572868
  0.6 45.7 %copy-start.6 = (f32[4,32,256]{2,1,0:T(8,128)S(1)}, f32[4,32,256]{2,1,0:T(8,128)}, u32[]{:S(2)}) copy-start(f32[4,32,256]{2,1,0:T(8,128)} %refs_2_.5) | copy-start | bytes 393220
  0.7 45.7 %copy-start.4 = (s32[4,32,256]{2,1,0:T(8,128)S(1)}, s32[4,32,256]{2,1,0:T(8,128)}, u32[]{:S(2)}) copy-start(s32[4,32,256]{2,1,0:T(8,128)} %refs_1_.5) | copy-start | bytes 393220
  0.7 9.0 %collective-permute-start.1 = (s32[16,32,256]{2,1,0:T(8,128)}, s32[16,32,256]{2,1,0:T(8,128)S(1)}, u32[]{:S(2)}, u32[]{:S(2)}) collective-permute-start(s32[16,32,256]{2,1,0:T(8,128)} %refs_6_.1), channel_id=1, source_target_pairs={{0,1},{1,0},{2,3},{3,2},{4,5},{5,4},{6,7},{7,6},{8,9},{9,8},{10,11... | collective-permute-start | bytes 1572872 | tf_op jit(solution)/shard_map/ppermute | solution.py:545
  6.1 1.9 %collective-permute-start = (f32[8,1024]{1,0:T(8,128)}, f32[8,1024]{1,0:T(8,128)S(1)}, u32[]{:S(2)}, u32[]{:S(2)}) collective-permute-start(f32[8,1024]{1,0:T(8,128)} %get-tuple-element.52), channel_id=1, source_target_pairs={{0,1},{1,0},{2,3},{3,2},{4,5},{5,4},{6,7},{7,6},{8,9},{9,8},{10,11... | collective-permute-start | bytes 98312 | tf_op jit(solution)/shard_map/ppermute | solution.py:545
  6.8 0.7 copy-start.8
  8.0 0.9 copy-start.2
  37.3 1.0 %copy-start = (s32[16,32,256]{2,1,0:T(8,128)S(1)}, s32[16,32,256]{2,1,0:T(8,128)}, u32[]{:S(2)}) copy-start(s32[16,32,256]{2,1,0:T(8,128)} %refs_6_.1) | copy-start | bytes 1572868
  38.4 0.9 copy-start.3
  39.3 0.9 copy-start.5
  41.0 7.8 %collective-permute-start.2 = (f32[56,128]{1,0:T(8,128)S(1)}, f32[56,128]{1,0:T(8,128)S(1)}, u32[]{:S(2)}, u32[]{:S(2)}) collective-permute-start(f32[56,128]{1,0:T(8,128)S(1)} %get-tuple-element.65), channel_id=1, source_target_pairs={{2,0},{4,2},{6,4},{8,6},{10,8},{12,10},{14,12},{3,1},{5,3},{7,5},{... | collective-permute-start | bytes 86024 | tf_op jit(solution)/shard_map/ppermute | solution.py:540
  42.3 6.6 %collective-permute-start.3 = (f32[56,128]{1,0:T(8,128)S(1)}, f32[56,128]{1,0:T(8,128)S(1)}, u32[]{:S(2)}, u32[]{:S(2)}) collective-permute-start(f32[56,128]{1,0:T(8,128)S(1)} %get-tuple-element.66), channel_id=1, source_target_pairs={{0,2},{2,4},{4,6},{6,8},{8,10},{10,12},{12,14},{1,3},{3,5},{5,7},{... | collective-permute-start | bytes 86024 | tf_op jit(solution)/shard_map/ppermute | solution.py:540
  48.9 9.2 %collective-permute-start.4 = (f32[248,256]{1,0:T(8,128)S(1)}, f32[248,256]{1,0:T(8,128)S(1)}, u32[]{:S(2)}, u32[]{:S(2)}) collective-permute-start(f32[248,256]{1,0:T(8,128)S(1)} %get-tuple-element.69), channel_id=1, source_target_pairs={{16,0},{32,16},{48,32},{64,48},{80,64},{96,80},{112,96},{128,112},... | collective-permute-start | bytes 761864 | tf_op jit(solution)/shard_map/ppermute | solution.py:540
  50.2 7.9 %collective-permute-start.5 = (f32[248,256]{1,0:T(8,128)S(1)}, f32[248,256]{1,0:T(8,128)S(1)}, u32[]{:S(2)}, u32[]{:S(2)}) collective-permute-start(f32[248,256]{1,0:T(8,128)S(1)} %get-tuple-element.70), channel_id=1, source_target_pairs={{0,16},{16,32},{32,48},{48,64},{64,80},{80,96},{96,112},{112,128},... | collective-permute-start | bytes 761864 | tf_op jit(solution)/shard_map/ppermute | solution.py:540
  63.0 30.7 %copy-start.7 = (f32[3,32,256]{2,1,0:T(8,128)S(1)}, f32[3,32,256]{2,1,0:T(8,128)}, u32[]{:S(2)}) copy-start(f32[3,32,256]{2,1,0:T(8,128)} %refs_3_.5) | copy-start | bytes 294916
  91.9 1.7 %collective-permute-start.6 = (f32[32,256]{1,0:T(8,128)S(1)}, f32[32,256]{1,0:T(8,128)S(1)}, u32[]{:S(2)}, u32[]{:S(2)}) collective-permute-start(f32[32,256]{1,0:T(8,128)S(1)} %get-tuple-element.75.refs_0_), channel_id=1, source_target_pairs={{0,1},{1,0},{2,3},{3,2},{4,5},{5,4},{6,7},{7,6},{8,9},{9,8},{10,11... | collective-permute-start | bytes 98312 | tf_op jit(solution)/shard_map/ppermute | solution.py:545

commit v7 on v6

--- a/solution.py
+++ b/solution.py
@@ -23,7 +23,7 @@
 
 
 SPLIT = 8
-PROFILE = 60
+LOADING = 60
 GY = ("gy",)
 
 
@@ -614,7 +614,7 @@
         [((NF, rows_in), F32), ((8, rows_in), F32)],
         [gz, vertical_weights, era5_columns[0]],
         in_smem=1,
-        vmem_mib=PROFILE,
+        vmem_mib=LOADING,
     )
     other = swapped(leaving, "gz", 1)
     (target,) = kernel(
@@ -649,6 +649,7 @@
         in_smem=1,
         anywhere=(5,),
         tail=5,
+        vmem_mib=LOADING,
     )
     right = shifted(low_y, GY, -1)
     left = shifted(high_y, GY, 1)

time: 95 us -> 95.3 us (level)
  Pallas kernels: 18.3 us -> 20.7 us
  blocking collectives: 54.2 us -> 52.8 us
    pallas_call x9, Pallas kernels: 18.3 us -> 20.7 us  [kernel(): pl.pallas_call(whole, out_shape=tuple((jax.ShapeDtypeStruct(shape, dtype)...]
    all_to_all x1, blocking collectives: 26.6 us -> 25.1 us  [shards(): lax.all_to_all(moments, ('gx', *GY, 'gz'), split_axis=0, concat_axis=0, t...]
    unnamed x19 -> x23, local copies, waits for them, and re-layouts: 4.47 us -> 3.59 us
where the time goes in v7:
time: 95.3 us; the launch traced here: 94.8 us
  blocking collectives  52.8 us (55%)
  Pallas kernels  20.7 us (22%)
  starting transfers between devices  15.2 us (16%)
  local copies, waits for them, and re-layouts  3.61 us (4%)
  between operations  1.71 us (2%)
    all_to_all x1, blocking collectives, shards(): lax.all_to_all(outgoing.reshape(tiles, capacity // 2, 128), ('gx', *GY),...  27.7 us
    all_to_all x1, blocking collectives, shards(): lax.all_to_all(moments, ('gx', *GY, 'gz'), split_axis=0, concat_axis=0, t...  25.1 us
    pallas_call x9, Pallas kernels, kernel(): pl.pallas_call(whole, out_shape=tuple((jax.ShapeDtypeStruct(shape, dtype)...  20.7 us
    ppermute x4, starting transfers between devices, shifted(): return lax.ppermute(block, axis, pairs)  10.9 us
    ppermute x3, starting transfers between devices, swapped(): return lax.ppermute(block, axis, [(i, i ^ bit) for i in range(count)])  4.3 us
    unnamed x23, local copies, waits for them, and re-layouts  3.59 us
  transfers between devices with their start and end apart: 7, of which 1 were waited for; matrix products, arithmetic and copies ran while one was open for 0% of the time, Pallas kernels for 10%

profile of v7, /device:TPU:1, one launch (start us, length us, event | category | flops | bytes accessed | tf_op | source)
XLA Modules:
  0.0 94.8 jit_solution(3065027997799312569)
XLA Ops:
  0.6 0.0 copy-start
  0.6 0.0 copy-start.6
  0.7 0.0 copy-start.5
  0.7 3.3 %collective-permute-start.1 = (s32[16,32,256]{2,1,0:T(8,128)}, s32[16,32,256]{2,1,0:T(8,128)S(1)}, u32[]{:S(2)}, u32[]{:S(2)}) collective-permute-start(s32[16,32,256]{2,1,0:T(8,128)} %refs_6_.1), channel_id=1, source_target_pairs={{0,1},{1,0},{2,3},{3,2},{4,5},{5,4},{6,7},{7,6},{8,9},{9,8},{10,11... | collective-permute-start | bytes 1572872 | tf_op jit(solution)/shard_map/ppermute | solution.py:545
  4.0 2.1 %profile.1 = (f32[40,1024]{1,0:T(8,128)}, f32[8,1024]{1,0:T(8,128)}) custom-call(s32[1]{0:T(128)} %bitcast.refs_0_.refs_2_, f32[16,32]{1,0:T(8,128)} %refs_1_.4, f32[1024,128]{1,0:T(8,128)} %bitcast.28), custom_call_target="tpu_custom_call" | custom-call | tf_op jit(solution)/shard_map/profile/pallas_call | solution.py:597
  6.1 0.1 collective-permute-start
  6.8 0.0 copy-start.10
  6.9 0.7 copy-done.10
  7.5 0.5 rank.1.refs_0_
  8.0 0.0 copy-start.4
  8.0 0.9 copy-done.4
  8.9 0.8 place.1
  9.7 0.0 copy-start.1
  9.7 27.7 %all_to_all.16 = f32[128,4,128]{2,1,0:T(4,128)} all-to-all(f32[128,4,128]{2,1,0:T(4,128)S(1)} %bitcast.23), channel_id=1, replica_groups=mesh['gx'=16,'gy'=8,'gz'=2] {'gx','gy'}, dimensions={0} | all-to-all | bytes 524288 | tf_op jit(solution)/shard_map/all_to_all | solution.py:636
  37.4 3.4 %table.1 = (bf16[160,512]{1,0:T(8,128)(2,1)}, f32[56,128]{1,0:T(8,128)}, f32[56,128]{1,0:T(8,128)}) custom-call(s32[1]{0:T(128)} %bitcast.refs_0_.refs_2_, f32[512,128]{1,0:T(8,128)} %bitcast.27, s32[4,32,256]{2,1,0:T(8,128)} %refs_1_.5, f32[4,32,256]{2,1,0:T(8,128)} %refs_2_.5, s32[512,256]{1,0:T(8,128)} %bitcast.15, s32[512,256]{1,0:T(8,128)} %bitcast.19), custom_call_target="tpu_custom_call" | custom-call | tf_op jit(solution)/shard_map/table/pallas_call | solution.py:597
  40.9 1.3 %collective-permute-start.2 = (f32[56,128]{1,0:T(8,128)}, f32[56,128]{1,0:T(8,128)S(1)}, u32[]{:S(2)}, u32[]{:S(2)}) collective-permute-start(f32[56,128]{1,0:T(8,128)} %get-tuple-element.65), channel_id=1, source_target_pairs={{2,0},{4,2},{6,4},{8,6},{10,8},{12,10},{14,12},{3,1},{5,3},{7,5},{... | collective-permute-start | bytes 86024 | tf_op jit(solution)/shard_map/ppermute | solution.py:540
  42.2 4.0 %collective-permute-start.3 = (f32[56,128]{1,0:T(8,128)}, f32[56,128]{1,0:T(8,128)S(1)}, u32[]{:S(2)}, u32[]{:S(2)}) collective-permute-start(f32[56,128]{1,0:T(8,128)} %get-tuple-element.66), channel_id=1, source_target_pairs={{0,2},{2,4},{4,6},{6,8},{8,10},{10,12},{12,14},{1,3},{3,5},{5,7},{... | collective-permute-start | bytes 86024 | tf_op jit(solution)/shard_map/ppermute | solution.py:540
  46.2 0.0 copy-start.2
  46.2 1.0 %copy-done.2 = s32[16,32,256]{2,1,0:T(8,128)S(1)} copy-done((s32[16,32,256]{2,1,0:T(8,128)S(1)}, s32[16,32,256]{2,1,0:T(8,128)}, u32[]{:S(2)}) %copy-start.2) | copy-done | bytes 524312
  47.2 0.9 copy-done.8
  48.1 2.4 %edge.1 = (f32[2,8,40,128]{3,2,1,0:T(8,128)S(1)}, f32[2,4,40,128]{3,2,1,0:T(8,128)S(1)}, f32[248,256]{1,0:T(8,128)S(1)}, f32[248,256]{1,0:T(8,128)S(1)}) custom-call(s32[1]{0:T(128)} %bitcast.refs_0_.refs_2_, bf16[160,512]{1,0:T(8,128)(2,1)S(1)} %copy-done.8, s32[4,32,256]{2,1,0:T(8,128)S(1)} %copy-done.5, f32[4,32,256]{2,1,0:T(8,128)S(1)} %copy-done.6, ...), custom_call_target="tpu_custom_call" | custom-call | flops 3000000000 | bytes 2500000 | tf_op jit(solution)/shard_map/edge/pallas_call | solution.py:597
  50.6 0.0 copy-start.3
  50.6 1.4 %collective-permute-start.4 = (f32[248,256]{1,0:T(8,128)S(1)}, f32[248,256]{1,0:T(8,128)S(1)}, u32[]{:S(2)}, u32[]{:S(2)}) collective-permute-start(f32[248,256]{1,0:T(8,128)S(1)} %get-tuple-element.69), channel_id=1, source_target_pairs={{16,0},{32,16},{48,32},{64,48},{80,64},{96,80},{112,96},{128,112},... | collective-permute-start | bytes 761864 | tf_op jit(solution)/shard_map/ppermute | solution.py:540
  52.1 4.2 %collective-permute-start.5 = (f32[248,256]{1,0:T(8,128)S(1)}, f32[248,256]{1,0:T(8,128)S(1)}, u32[]{:S(2)}, u32[]{:S(2)}) collective-permute-start(f32[248,256]{1,0:T(8,128)S(1)} %get-tuple-element.70), channel_id=1, source_target_pairs={{0,16},{16,32},{32,48},{48,64},{64,80},{80,96},{96,112},{112,128},... | collective-permute-start | bytes 761864 | tf_op jit(solution)/shard_map/ppermute | solution.py:540
  56.3 3.6 %middle.1.refs_5_ = f32[2,20,40,128]{3,2,1,0:T(8,128)S(1)} custom-call(bf16[160,512]{1,0:T(8,128)(2,1)S(1)} %copy-done.9, s32[4,32,256]{2,1,0:T(8,128)S(1)} %copy-done.5, f32[4,32,256]{2,1,0:T(8,128)S(1)} %copy-done.6), custom_call_target="tpu_custom_call" | custom-call | flops 3000000000 | bytes 1600000 | tf_op jit(solution)/shard_map/middle/pallas_call | solution.py:597
  59.9 4.9 %basis.1 = (f32[3,17,40,384]{3,2,1,0:T(8,128)S(1)}, f32[256,128]{1,0:T(8,128)S(1)}) custom-call(s32[1]{0:T(128)} %bitcast.3.refs_0_, s32[1]{0:T(128)} %bitcast.4.refs_1_, s32[1]{0:T(128)} %bitcast.refs_0_.refs_2_, f32[2,8,40,128]{3,2,1,0:T(8,128)S(1)} %get-tuple-element.62.refs_3_, f32[2,4,40,128]{3,2,1,0:T(8,128)S(1)} %get-tuple-element.63.refs_4_, ...), custom_call_target="tpu_custom_call" | custom-call | tf_op jit(solution)/shard_map/basis/pallas_call | solution.py:597
  64.8 0.0 copy-start.7
  64.8 25.1 %all_to_all.17 = f32[256,1,128]{2,1,0:T(1,128)S(1)} all-to-all(f32[256,1,128]{2,1,0:T(1,128)S(1)} %bitcast.26), channel_id=1, replica_groups=mesh['gx'=16,'gy'=8,'gz'=2] {'gx','gy','gz'}, dimensions={0} | all-to-all | bytes 262144 | tf_op jit(solution)/shard_map/all_to_all | solution.py:704
  89.9 2.3 %wind.1 = (f32[16,32,256]{2,1,0:T(8,128)}, f32[3,16,32,256]{3,2,1,0:T(8,128)}, f32[32,256]{1,0:T(8,128)S(1)}, f32[32,256]{1,0:T(8,128)S(1)}) custom-call(s32[1]{0:T(128)} %bitcast.refs_0_.refs_2_, f32[256,128]{1,0:T(8,128)S(1)} %bitcast.25, f32[3,17,40,384]{3,2,1,0:T(8,128)S(1)} %get-tuple-element.72.refs_2_, f32[2,320,128]{2,1,0:T(8,128)S(1)} %bitcast.22, ...), custom_call_target="tpu_custom_call" | custom-call | tf_op jit(solution)/shard_map/wind/pallas_call | solution.py:597
  92.2 0.9 collective-permute-start.6
  93.1 0.9 collective-permute-done.6.refs_1_
  93.9 0.7 fuel.1
  (18 shorter events, 0.1 us)
Async XLA Ops:
  0.6 45.5 %copy-start = (s32[16,32,256]{2,1,0:T(8,128)S(1)}, s32[16,32,256]{2,1,0:T(8,128)}, u32[]{:S(2)}) copy-start(s32[16,32,256]{2,1,0:T(8,128)} %refs_6_.1) | copy-start | bytes 1572868
  0.6 45.5 %copy-start.6 = (f32[4,32,256]{2,1,0:T(8,128)S(1)}, f32[4,32,256]{2,1,0:T(8,128)}, u32[]{:S(2)}) copy-start(f32[4,32,256]{2,1,0:T(8,128)} %refs_2_.5) | copy-start | bytes 393220
  0.7 45.5 %copy-start.5 = (s32[4,32,256]{2,1,0:T(8,128)S(1)}, s32[4,32,256]{2,1,0:T(8,128)}, u32[]{:S(2)}) copy-start(s32[4,32,256]{2,1,0:T(8,128)} %refs_1_.5) | copy-start | bytes 393220
  0.7 9.0 %collective-permute-start.1 = (s32[16,32,256]{2,1,0:T(8,128)}, s32[16,32,256]{2,1,0:T(8,128)S(1)}, u32[]{:S(2)}, u32[]{:S(2)}) collective-permute-start(s32[16,32,256]{2,1,0:T(8,128)} %refs_6_.1), channel_id=1, source_target_pairs={{0,1},{1,0},{2,3},{3,2},{4,5},{5,4},{6,7},{7,6},{8,9},{9,8},{10,11... | collective-permute-start | bytes 1572872 | tf_op jit(solution)/shard_map/ppermute | solution.py:545
  6.1 1.9 %collective-permute-start = (f32[8,1024]{1,0:T(8,128)}, f32[8,1024]{1,0:T(8,128)S(1)}, u32[]{:S(2)}, u32[]{:S(2)}) collective-permute-start(f32[8,1024]{1,0:T(8,128)} %get-tuple-element.52), channel_id=1, source_target_pairs={{0,1},{1,0},{2,3},{3,2},{4,5},{5,4},{6,7},{7,6},{8,9},{9,8},{10,11... | collective-permute-start | bytes 98312 | tf_op jit(solution)/shard_map/ppermute | solution.py:545
  6.8 0.7 copy-start.10
  8.0 0.9 copy-start.4
  9.7 27.7 %copy-start.1 = (s32[16,32,256]{2,1,0:T(8,128)}, s32[16,32,256]{2,1,0:T(8,128)S(1)}, u32[]{:S(2)}) copy-start(s32[16,32,256]{2,1,0:T(8,128)S(1)} %collective-permute-done.1) | copy-start | bytes 1572868
  40.9 9.7 %collective-permute-start.2 = (f32[56,128]{1,0:T(8,128)}, f32[56,128]{1,0:T(8,128)S(1)}, u32[]{:S(2)}, u32[]{:S(2)}) collective-permute-start(f32[56,128]{1,0:T(8,128)} %get-tuple-element.65), channel_id=1, source_target_pairs={{2,0},{4,2},{6,4},{8,6},{10,8},{12,10},{14,12},{3,1},{5,3},{7,5},{... | collective-permute-start | bytes 86024 | tf_op jit(solution)/shard_map/ppermute | solution.py:540
  42.2 8.4 %collective-permute-start.3 = (f32[56,128]{1,0:T(8,128)}, f32[56,128]{1,0:T(8,128)S(1)}, u32[]{:S(2)}, u32[]{:S(2)}) collective-permute-start(f32[56,128]{1,0:T(8,128)} %get-tuple-element.66), channel_id=1, source_target_pairs={{0,2},{2,4},{4,6},{6,8},{8,10},{10,12},{12,14},{1,3},{3,5},{5,7},{... | collective-permute-start | bytes 86024 | tf_op jit(solution)/shard_map/ppermute | solution.py:540
  46.2 1.0 %copy-start.2 = (s32[16,32,256]{2,1,0:T(8,128)S(1)}, s32[16,32,256]{2,1,0:T(8,128)}, u32[]{:S(2)}) copy-start(s32[16,32,256]{2,1,0:T(8,128)} %copy-done.1) | copy-start | bytes 1572868
  47.2 0.9 copy-start.8
  48.1 8.1 %copy-start.9 = (bf16[160,512]{1,0:T(8,128)(2,1)S(1)}, bf16[160,512]{1,0:T(8,128)(2,1)}, u32[]{:S(2)}) copy-start(bf16[160,512]{1,0:T(8,128)(2,1)} %get-tuple-element.68.refs_1_.refs_0_) | copy-start | bytes 491524
  50.6 9.3 %copy-start.3 = (s32[16,32,256]{2,1,0:T(8,128)S(1)}, s32[16,32,256]{2,1,0:T(8,128)}, u32[]{:S(2)}) copy-start(s32[16,32,256]{2,1,0:T(8,128)} %copy-done.1) | copy-start | bytes 1572868
  50.6 9.2 %collective-permute-start.4 = (f32[248,256]{1,0:T(8,128)S(1)}, f32[248,256]{1,0:T(8,128)S(1)}, u32[]{:S(2)}, u32[]{:S(2)}) collective-permute-start(f32[248,256]{1,0:T(8,128)S(1)} %get-tuple-element.69), channel_id=1, source_target_pairs={{16,0},{32,16},{48,32},{64,48},{80,64},{96,80},{112,96},{128,112},... | collective-permute-start | bytes 761864 | tf_op jit(solution)/shard_map/ppermute | solution.py:540
  52.1 7.8 %collective-permute-start.5 = (f32[248,256]{1,0:T(8,128)S(1)}, f32[248,256]{1,0:T(8,128)S(1)}, u32[]{:S(2)}, u32[]{:S(2)}) collective-permute-start(f32[248,256]{1,0:T(8,128)S(1)} %get-tuple-element.70), channel_id=1, source_target_pairs={{0,16},{16,32},{32,48},{48,64},{64,80},{80,96},{96,112},{112,128},... | collective-permute-start | bytes 761864 | tf_op jit(solution)/shard_map/ppermute | solution.py:540
  64.8 29.1 %copy-start.7 = (f32[3,32,256]{2,1,0:T(8,128)S(1)}, f32[3,32,256]{2,1,0:T(8,128)}, u32[]{:S(2)}) copy-start(f32[3,32,256]{2,1,0:T(8,128)} %refs_3_.5) | copy-start | bytes 294916
  92.2 1.7 %collective-permute-start.6 = (f32[32,256]{1,0:T(8,128)S(1)}, f32[32,256]{1,0:T(8,128)S(1)}, u32[]{:S(2)}, u32[]{:S(2)}) collective-permute-start(f32[32,256]{1,0:T(8,128)S(1)} %get-tuple-element.75.refs_0_), channel_id=1, source_target_pairs={{0,1},{1,0},{2,3},{3,2},{4,5},{5,4},{6,7},{7,6},{8,9},{9,8},{10,11... | collective-permute-start | bytes 98312 | tf_op jit(solution)/shard_map/ppermute | solution.py:545

commit v8 on v5

--- a/solution.py
+++ b/solution.py
@@ -22,7 +22,8 @@
 YR = 384
 
 
-GY = ("zh", "zl")
+SPLIT = 8
+GY = ("gy",)
 
 
 def split(value):
@@ -238,7 +239,7 @@
                 else:
                     out[NS * 3 : NS * 3 + 16, at] = edge_ref[h, kept, 0:16]
                     out[NS * 3 + 16 : NS * 3 + 24, at] = edge_ref[h, kept, 32:40]
-    pick_rows(table_ref, index_ref, weight_ref, list(range(4, 12)), middle_ref, capacity)
+    pick_rows(table_ref, index_ref, weight_ref, list(range(4, SPLIT)), middle_ref, capacity)
 
 
 def middle_kernel(table_ref, index_ref, weight_ref, middle_ref, *, first, capacity):
@@ -251,7 +252,7 @@
         return edge_ref, x
     if x >= rows - 4:
         return edge_ref, x - rows + 8
-    return (middle_refs[0], x - 4) if x < 12 else (middle_refs[1], x - 12)
+    return (middle_refs[0], x - 4) if x < SPLIT else (middle_refs[1], x - SPLIT)
 
 
 def ring_smooth(plane):
@@ -453,7 +454,7 @@
 
 
 def wind_kernel(
-    gz_ref, moments_ref, other_moments_ref, basis_ref, edge_ref, middle_0_ref, middle_1_ref, mask_ref,
+    gz_ref, moments_ref, basis_ref, edge_ref, middle_0_ref, middle_1_ref, mask_ref,
     potential_ref, wind_ref, speed_ref, balance_ref, p_ref, grid_ref
 ):
     gz = gz_ref[0]
@@ -461,10 +462,10 @@
     near = 4 * NF
     for h in range(cols // 128):
         grid_ref[h, 0:near] = edge_ref[h, 0:near]
-        grid_ref[h, near : near + 8 * NF] = middle_0_ref[h]
-        grid_ref[h, near + 8 * NF : (rows - 4) * NF] = middle_1_ref[h]
+        grid_ref[h, near : SPLIT * NF] = middle_0_ref[h]
+        grid_ref[h, SPLIT * NF : (rows - 4) * NF] = middle_1_ref[h]
         grid_ref[h, (rows - 4) * NF :] = edge_ref[h, near:]
-    totals = moments_ref[...] + other_moments_ref[...]
+    totals = jnp.sum(moments_ref[...], axis=0, keepdims=True)
     factors = iterate([totals[:, k : k + 1] for k in range(6)])
     factors = [jnp.broadcast_to(c, (8, 128)) for c in factors]
     factors = [jnp.tile(c, (XR // 8, YR // 128)) for c in factors]
@@ -641,7 +642,7 @@
         "edge",
         [
             ((halves, 8, NF, 128), F32),
-            ((halves, 8, NF, 128), F32),
+            ((halves, SPLIT - 4, NF, 128), F32),
             ((STRIP + NS, cols), F32),
             ((STRIP + NS, cols), F32),
         ],
@@ -658,21 +659,21 @@
     above = shifted(low_x, "gx", -1)
     below = shifted(high_x, "gx", 1)
     (middle_1,) = kernel(
-        functools.partial(middle_kernel, first=12, capacity=capacity),
+        functools.partial(middle_kernel, first=SPLIT, capacity=capacity),
         "middle",
-        [((halves, rows - 16, NF, 128), F32)],
+        [((halves, rows - 4 - SPLIT, NF, 128), F32)],
         [table, stencil_index, stencil_weight],
         cost=pl.CostEstimate(flops=3_000_000_000, bytes_accessed=1_600_000, transcendentals=0),
     )
     middles = (middle_0, middle_1)
 
-    near_group = lax.axis_size(("gx", "zl"))
+    devices = tiles * lax.axis_size("gz")
     basis, moments = kernel(
         functools.partial(
             basis_kernel, last_gx=lax.axis_size("gx") - 1, last_gy=lax.axis_size(GY) - 1
         ),
         "basis",
-        [((3, LZ + 1, XR, YR), F32), ((near_group, 128), F32)],
+        [((3, LZ + 1, XR, YR), F32), ((devices, 128), F32)],
         [gx, gy, gz, edge, *middles, near_mask, far_mask, right, left, above, below],
         scratch=[
             ((YR // 128, XR * NS, 128), F32),
@@ -685,14 +686,8 @@
         tail=7,
     )
     moments = lax.all_to_all(
-        moments, ("gx", "zl"), split_axis=0, concat_axis=0, tiled=True
-    )
-    moments = jnp.sum(moments, axis=0, keepdims=True)
-    bit = 1
-    while bit < lax.axis_size("zh"):
-        moments = moments + swapped(moments, "zh", bit)
-        bit *= 2
-    other_moments = swapped(moments, "gz", 1)
+        moments, ("gx", *GY, "gz"), split_axis=0, concat_axis=0, tiled=True
+    )
     potential, wind_field, speed, balance = kernel(
         wind_kernel,
         "wind",
@@ -705,7 +700,6 @@
         [
             gz,
             moments,
-            other_moments,
             basis,
             *(piece.reshape(halves, -1, 128) for piece in (edge, *middles)),
             terrain_mask,
@@ -724,11 +718,6 @@
 
 
 def solution(mesh):
-    count_gx, count_gy, count_gz = mesh.devices.shape
-    near = math.gcd(count_gy, 4)
-    finer = jax.sharding.Mesh(
-        mesh.devices.reshape(count_gx, count_gy // near, near, count_gz), ("gx", *GY, "gz")
-    )
     placed = (
         P(("gx", *GY), None, "gz"),
         P(("gx", *GY), None),
@@ -741,7 +730,7 @@
     )
     return jax.shard_map(
         shards,
-        mesh=finer,
+        mesh=mesh,
         in_specs=placed,
         out_specs=(P("gz", "gx", GY), P(None, "gz", "gx", GY), P(None, "gx", GY)),
         check_vma=False,

time: 101 us -> 92.3 us (0.914)
  waiting for transfers between devices: 9.92 us -> 2.41 us
  blocking collectives: 46 us -> 53.3 us
  starting transfers between devices: 21.1 us -> 16.6 us
  local copies, waits for them, and re-layouts: 3.56 us -> 0.04 us
    all_to_all x1, blocking collectives: 17.8 us -> 25.1 us  [shards(): lax.all_to_all(moments, ('gx', *GY, 'gz'), split_axis=0, concat_axis=0, t...]
    ppermute x5 -> x3, waiting for transfers between devices: 8.93 us -> 2.02 us  [swapped(): return lax.ppermute(block, axis, [(i, i ^ bit) for i in range(count)])]
    ppermute x5 -> x3, starting transfers between devices: 10.3 us -> 5.82 us  [swapped(): return lax.ppermute(block, axis, [(i, i ^ bit) for i in range(count)])]
    unnamed x13 -> x9, local copies, waits for them, and re-layouts: 3.55 us -> 0.02 us
  transfers between devices with their start and end apart: 9 -> 7, of which waited for: 6 -> 3; matrix products, arithmetic and copies ran while one was open for 0% -> 0% of each run, Pallas kernels for 9% -> 10%
where the time goes in v8:
time: 92.3 us; the launch traced here: 91.9 us
  blocking collectives  53.3 us (58%)
  Pallas kernels  18 us (20%)
  starting transfers between devices  16.6 us (18%)
  waiting for transfers between devices  2.41 us (3%)
  between operations  1.59 us (2%)
    all_to_all x1, blocking collectives, shards(): lax.all_to_all(outgoing.reshape(tiles, capacity // 2, 128), ('gx', *GY),...  28.2 us
    all_to_all x1, blocking collectives, shards(): lax.all_to_all(moments, ('gx', *GY, 'gz'), split_axis=0, concat_axis=0, t...  25.1 us
    pallas_call x7, Pallas kernels, kernel(): pl.pallas_call(whole, out_shape=tuple((jax.ShapeDtypeStruct(shape, dtype)...  18 us
    ppermute x4, starting transfers between devices, shifted(): return lax.ppermute(block, axis, pairs)  10.8 us
    ppermute x3, starting transfers between devices, swapped(): return lax.ppermute(block, axis, [(i, i ^ bit) for i in range(count)])  5.82 us
    ppermute x3, waiting for transfers between devices, swapped(): return lax.ppermute(block, axis, [(i, i ^ bit) for i in range(count)])  2.02 us
  transfers between devices with their start and end apart: 7, of which 3 were waited for; matrix products, arithmetic and copies ran while one was open for 0% of the time, Pallas kernels for 10%

profile of v8, /device:TPU:1, one launch (start us, length us, event | category | flops | bytes accessed | tf_op | source)
XLA Modules:
  0.0 91.9 jit_solution(3102433913101123245)
XLA Ops:
  0.6 0.0 copy-start
  0.6 0.0 copy-start.2
  0.7 0.0 copy-start.1
  0.7 3.3 %collective-permute-start = (s32[16,32,256]{2,1,0:T(8,128)}, s32[16,32,256]{2,1,0:T(8,128)S(1)}, u32[]{:S(2)}, u32[]{:S(2)}) collective-permute-start(s32[16,32,256]{2,1,0:T(8,128)} %refs_6_.1), channel_id=1, source_target_pairs={{0,1},{1,0},{2,3},{3,2},{4,5},{5,4},{6,7},{7,6},{8,9},{9,8},{10,11... | collective-permute-start | bytes 1572872 | tf_op jit(solution)/shard_map/ppermute | solution.py:543
  4.6 3.2 %route.1 = f32[512,128]{1,0:T(8,128)} custom-call(s32[1]{0:T(128)} %bitcast.refs_0_.refs_2_, s32[1]{0:T(128)S(6)} %copy.15.refs_1_, f32[16,32]{1,0:T(8,128)} %refs_2_.3, f32[1024,128]{1,0:T(8,128)} %bitcast.29, s32[1,1024]{1,0:T(1,128)} %refs_4_.2), custom_call_target="tpu_custom_call" | custom-call | flops 1000000000 | bytes 1000000 | tf_op jit(solution)/shard_map/route/pallas_call | solution.py:595
  7.9 0.0 collective-permute-done
  7.9 28.2 %all_to_all.16 = f32[128,4,128]{2,1,0:T(4,128)S(1)} all-to-all(f32[128,4,128]{2,1,0:T(4,128)} %bitcast.28), channel_id=1, replica_groups=mesh['gx'=16,'gy'=8,'gz'=2] {'gx','gy'}, dimensions={0} | all-to-all | bytes 524288 | tf_op jit(solution)/shard_map/all_to_all | solution.py:619
  36.1 1.6 %collective-permute-start.1 = (f32[512,128]{1,0:T(8,128)S(1)}, f32[512,128]{1,0:T(8,128)S(1)}, u32[]{:S(2)}, u32[]{:S(2)}) collective-permute-start(f32[512,128]{1,0:T(8,128)S(1)} %bitcast.23), channel_id=1, source_target_pairs={{0,1},{1,0},{2,3},{3,2},{4,5},{5,4},{6,7},{7,6},{8,9},{9,8},{10,11... | collective-permute-start | bytes 786440 | tf_op jit(solution)/shard_map/ppermute | solution.py:543
  37.7 1.2 %collective-permute-done.1.refs_2_ = f32[512,128]{1,0:T(8,128)S(1)} collective-permute-done((f32[512,128]{1,0:T(8,128)S(1)}, f32[512,128]{1,0:T(8,128)S(1)}, u32[]{:S(2)}, u32[]{:S(2)}) %collective-permute-start.1) | collective-permute-done | bytes 262176 | tf_op jit(solution)/shard_map/ppermute | solution.py:543
  38.8 0.0 copy-done
  38.8 0.0 copy-done.2
  38.8 0.0 copy-done.1
  38.9 0.9 table.1
  39.8 1.3 %collective-permute-start.2 = (f32[56,128]{1,0:T(8,128)S(1)}, f32[56,128]{1,0:T(8,128)S(1)}, u32[]{:S(2)}, u32[]{:S(2)}) collective-permute-start(f32[56,128]{1,0:T(8,128)S(1)} %get-tuple-element.57), channel_id=1, source_target_pairs={{2,0},{4,2},{6,4},{8,6},{10,8},{12,10},{14,12},{3,1},{5,3},{7,5},{... | collective-permute-start | bytes 86024 | tf_op jit(solution)/shard_map/ppermute | solution.py:538
  41.1 4.0 %collective-permute-start.3 = (f32[56,128]{1,0:T(8,128)S(1)}, f32[56,128]{1,0:T(8,128)S(1)}, u32[]{:S(2)}, u32[]{:S(2)}) collective-permute-start(f32[56,128]{1,0:T(8,128)S(1)} %get-tuple-element.58), channel_id=1, source_target_pairs={{0,2},{2,4},{4,6},{6,8},{8,10},{10,12},{12,14},{1,3},{3,5},{5,7},{... | collective-permute-start | bytes 86024 | tf_op jit(solution)/shard_map/ppermute | solution.py:538
  45.1 2.4 %edge.1 = (f32[2,8,40,128]{3,2,1,0:T(8,128)S(1)}, f32[2,4,40,128]{3,2,1,0:T(8,128)S(1)}, f32[248,256]{1,0:T(8,128)S(1)}, f32[248,256]{1,0:T(8,128)S(1)}) custom-call(s32[1]{0:T(128)} %bitcast.refs_0_.refs_2_, bf16[160,512]{1,0:T(8,128)(2,1)S(1)} %get-tuple-element.60.refs_1_.refs_0_, s32[4,32,256]{2,1,0:T(8,128)S(1)} %copy-done.1, ...), custom_call_target="tpu_custom_call" | custom-call | flops 3000000000 | bytes 2500000 | tf_op jit(solution)/shard_map/edge/pallas_call | solution.py:595
  47.5 0.0 collective-permute-done.2.refs_8_
  47.5 0.0 collective-permute-done.3.refs_9_
  47.6 1.3 %collective-permute-start.4 = (f32[248,256]{1,0:T(8,128)S(1)}, f32[248,256]{1,0:T(8,128)S(1)}, u32[]{:S(2)}, u32[]{:S(2)}) collective-permute-start(f32[248,256]{1,0:T(8,128)S(1)} %get-tuple-element.61), channel_id=1, source_target_pairs={{16,0},{32,16},{48,32},{64,48},{80,64},{96,80},{112,96},{128,112},... | collective-permute-start | bytes 761864 | tf_op jit(solution)/shard_map/ppermute | solution.py:538
  48.9 4.2 %collective-permute-start.5 = (f32[248,256]{1,0:T(8,128)S(1)}, f32[248,256]{1,0:T(8,128)S(1)}, u32[]{:S(2)}, u32[]{:S(2)}) collective-permute-start(f32[248,256]{1,0:T(8,128)S(1)} %get-tuple-element.62), channel_id=1, source_target_pairs={{0,16},{16,32},{32,48},{48,64},{64,80},{80,96},{96,112},{112,128},... | collective-permute-start | bytes 761864 | tf_op jit(solution)/shard_map/ppermute | solution.py:538
  53.1 3.6 %middle.1.refs_5_ = f32[2,20,40,128]{3,2,1,0:T(8,128)S(1)} custom-call(bf16[160,512]{1,0:T(8,128)(2,1)S(1)} %get-tuple-element.60.refs_1_.refs_0_, s32[4,32,256]{2,1,0:T(8,128)S(1)} %copy-done.1, f32[4,32,256]{2,1,0:T(8,128)S(1)} %copy-done.2), custom_call_target="tpu_custom_call" | custom-call | flops 3000000000 | bytes 1600000 | tf_op jit(solution)/shard_map/middle/pallas_call | solution.py:595
  56.7 0.0 collective-permute-done.4.refs_10_
  56.7 0.4 collective-permute-done.5.refs_11_
  57.0 4.8 %basis.1 = (f32[3,17,40,384]{3,2,1,0:T(8,128)S(1)}, f32[256,128]{1,0:T(8,128)S(1)}) custom-call(s32[1]{0:T(128)} %bitcast.3.refs_0_, s32[1]{0:T(128)} %bitcast.4.refs_1_, s32[1]{0:T(128)} %bitcast.refs_0_.refs_2_, f32[2,8,40,128]{3,2,1,0:T(8,128)S(1)} %get-tuple-element.54.refs_3_, f32[2,4,40,128]{3,2,1,0:T(8,128)S(1)} %get-tuple-element.55.refs_4_, ...), custom_call_target="tpu_custom_call" | custom-call | tf_op jit(solution)/shard_map/basis/pallas_call | solution.py:595
  61.9 0.0 copy-start.3
  61.9 25.1 %all_to_all.17 = f32[256,1,128]{2,1,0:T(1,128)S(1)} all-to-all(f32[256,1,128]{2,1,0:T(1,128)S(1)} %bitcast.27), channel_id=1, replica_groups=mesh['gx'=16,'gy'=8,'gz'=2] {'gx','gy','gz'}, dimensions={0} | all-to-all | bytes 262144 | tf_op jit(solution)/shard_map/all_to_all | solution.py:688
  87.0 2.3 %wind.1 = (f32[16,32,256]{2,1,0:T(8,128)}, f32[3,16,32,256]{3,2,1,0:T(8,128)}, f32[32,256]{1,0:T(8,128)S(1)}, f32[32,256]{1,0:T(8,128)S(1)}) custom-call(s32[1]{0:T(128)} %bitcast.refs_0_.refs_2_, f32[256,128]{1,0:T(8,128)S(1)} %bitcast.26, f32[3,17,40,384]{3,2,1,0:T(8,128)S(1)} %get-tuple-element.64.refs_2_, f32[2,320,128]{2,1,0:T(8,128)S(1)} %bitcast.22, ...), custom_call_target="tpu_custom_call" | custom-call | tf_op jit(solution)/shard_map/wind/pallas_call | solution.py:595
  89.3 0.9 collective-permute-start.6
  90.2 0.9 collective-permute-done.6.refs_1_
  91.0 0.0 copy-done.3
  91.0 0.7 fuel.1
  (3 shorter events, 0.0 us)
Async XLA Ops:
  0.6 38.2 %copy-start = (s32[16,32,256]{2,1,0:T(8,128)S(1)}, s32[16,32,256]{2,1,0:T(8,128)}, u32[]{:S(2)}) copy-start(s32[16,32,256]{2,1,0:T(8,128)} %refs_6_.1) | copy-start | bytes 1572868
  0.6 38.2 %copy-start.2 = (f32[4,32,256]{2,1,0:T(8,128)S(1)}, f32[4,32,256]{2,1,0:T(8,128)}, u32[]{:S(2)}) copy-start(f32[4,32,256]{2,1,0:T(8,128)} %refs_2_.5) | copy-start | bytes 393220
  0.7 38.2 %copy-start.1 = (s32[4,32,256]{2,1,0:T(8,128)S(1)}, s32[4,32,256]{2,1,0:T(8,128)}, u32[]{:S(2)}) copy-start(s32[4,32,256]{2,1,0:T(8,128)} %refs_1_.2) | copy-start | bytes 393220
  0.7 7.2 %collective-permute-start = (s32[16,32,256]{2,1,0:T(8,128)}, s32[16,32,256]{2,1,0:T(8,128)S(1)}, u32[]{:S(2)}, u32[]{:S(2)}) collective-permute-start(s32[16,32,256]{2,1,0:T(8,128)} %refs_6_.1), channel_id=1, source_target_pairs={{0,1},{1,0},{2,3},{3,2},{4,5},{5,4},{6,7},{7,6},{8,9},{9,8},{10,11... | collective-permute-start | bytes 1572872 | tf_op jit(solution)/shard_map/ppermute | solution.py:543
  36.1 2.8 %collective-permute-start.1 = (f32[512,128]{1,0:T(8,128)S(1)}, f32[512,128]{1,0:T(8,128)S(1)}, u32[]{:S(2)}, u32[]{:S(2)}) collective-permute-start(f32[512,128]{1,0:T(8,128)S(1)} %bitcast.23), channel_id=1, source_target_pairs={{0,1},{1,0},{2,3},{3,2},{4,5},{5,4},{6,7},{7,6},{8,9},{9,8},{10,11... | collective-permute-start | bytes 786440 | tf_op jit(solution)/shard_map/ppermute | solution.py:543
  39.8 7.8 %collective-permute-start.2 = (f32[56,128]{1,0:T(8,128)S(1)}, f32[56,128]{1,0:T(8,128)S(1)}, u32[]{:S(2)}, u32[]{:S(2)}) collective-permute-start(f32[56,128]{1,0:T(8,128)S(1)} %get-tuple-element.57), channel_id=1, source_target_pairs={{2,0},{4,2},{6,4},{8,6},{10,8},{12,10},{14,12},{3,1},{5,3},{7,5},{... | collective-permute-start | bytes 86024 | tf_op jit(solution)/shard_map/ppermute | solution.py:538
  41.1 6.5 %collective-permute-start.3 = (f32[56,128]{1,0:T(8,128)S(1)}, f32[56,128]{1,0:T(8,128)S(1)}, u32[]{:S(2)}, u32[]{:S(2)}) collective-permute-start(f32[56,128]{1,0:T(8,128)S(1)} %get-tuple-element.58), channel_id=1, source_target_pairs={{0,2},{2,4},{4,6},{6,8},{8,10},{10,12},{12,14},{1,3},{3,5},{5,7},{... | collective-permute-start | bytes 86024 | tf_op jit(solution)/shard_map/ppermute | solution.py:538
  47.6 9.1 %collective-permute-start.4 = (f32[248,256]{1,0:T(8,128)S(1)}, f32[248,256]{1,0:T(8,128)S(1)}, u32[]{:S(2)}, u32[]{:S(2)}) collective-permute-start(f32[248,256]{1,0:T(8,128)S(1)} %get-tuple-element.61), channel_id=1, source_target_pairs={{16,0},{32,16},{48,32},{64,48},{80,64},{96,80},{112,96},{128,112},... | collective-permute-start | bytes 761864 | tf_op jit(solution)/shard_map/ppermute | solution.py:538
  48.9 8.2 %collective-permute-start.5 = (f32[248,256]{1,0:T(8,128)S(1)}, f32[248,256]{1,0:T(8,128)S(1)}, u32[]{:S(2)}, u32[]{:S(2)}) collective-permute-start(f32[248,256]{1,0:T(8,128)S(1)} %get-tuple-element.62), channel_id=1, source_target_pairs={{0,16},{16,32},{32,48},{48,64},{64,80},{80,96},{96,112},{112,128},... | collective-permute-start | bytes 761864 | tf_op jit(solution)/shard_map/ppermute | solution.py:538
  61.9 29.1 %copy-start.3 = (f32[3,32,256]{2,1,0:T(8,128)S(1)}, f32[3,32,256]{2,1,0:T(8,128)}, u32[]{:S(2)}) copy-start(f32[3,32,256]{2,1,0:T(8,128)} %refs_3_.5) | copy-start | bytes 294916
  89.3 1.7 %collective-permute-start.6 = (f32[32,256]{1,0:T(8,128)S(1)}, f32[32,256]{1,0:T(8,128)S(1)}, u32[]{:S(2)}, u32[]{:S(2)}) collective-permute-start(f32[32,256]{1,0:T(8,128)S(1)} %get-tuple-element.67.refs_0_), channel_id=1, source_target_pairs={{0,1},{1,0},{2,3},{3,2},{4,5},{5,4},{6,7},{7,6},{8,9},{9,8},{10,11... | collective-permute-start | bytes 98312 | tf_op jit(solution)/shard_map/ppermute | solution.py:543

commit v9 on v8

--- a/solution.py
+++ b/solution.py
@@ -22,7 +22,7 @@
 YR = 384
 
 
-SPLIT = 8
+SPLIT = 5
 GY = ("gy",)
 
 

time: 92.3 us -> 92 us (level)
  transfers between devices with their start and end apart: 7 -> 7, of which waited for: 3 -> 2; matrix products, arithmetic and copies ran while one was open for 0% -> 0% of each run, Pallas kernels for 10% -> 10%
where the time goes in v9:
time: 92 us; the launch traced here: 91.7 us
  blocking collectives  53.6 us (58%)
  Pallas kernels  17.9 us (19%)
  starting transfers between devices  16.6 us (18%)
  waiting for transfers between devices  2.04 us (2%)
  between operations  1.6 us (2%)
    all_to_all x1, blocking collectives, shards(): lax.all_to_all(outgoing.reshape(tiles, capacity // 2, 128), ('gx', *GY),...  28.2 us
    all_to_all x1, blocking collectives, shards(): lax.all_to_all(moments, ('gx', *GY, 'gz'), split_axis=0, concat_axis=0, t...  25.4 us
    pallas_call x7, Pallas kernels, kernel(): pl.pallas_call(whole, out_shape=tuple((jax.ShapeDtypeStruct(shape, dtype)...  17.9 us
    ppermute x4, starting transfers between devices, shifted(): return lax.ppermute(block, axis, pairs)  10.8 us
    ppermute x3, starting transfers between devices, swapped(): return lax.ppermute(block, axis, [(i, i ^ bit) for i in range(count)])  5.82 us
    ppermute x3, waiting for transfers between devices, swapped(): return lax.ppermute(block, axis, [(i, i ^ bit) for i in range(count)])  2.02 us
  transfers between devices with their start and end apart: 7, of which 2 were waited for; matrix products, arithmetic and copies ran while one was open for 0% of the time, Pallas kernels for 10%

profile of v9, /device:TPU:1, one launch (start us, length us, event | category | flops | bytes accessed | tf_op | source)
XLA Modules:
  0.0 91.7 jit_solution(1749004270908538876)
XLA Ops:
  0.6 0.0 copy-start
  0.6 0.0 copy-start.2
  0.7 0.0 copy-start.1
  0.7 3.3 %collective-permute-start = (s32[16,32,256]{2,1,0:T(8,128)}, s32[16,32,256]{2,1,0:T(8,128)S(1)}, u32[]{:S(2)}, u32[]{:S(2)}) collective-permute-start(s32[16,32,256]{2,1,0:T(8,128)} %refs_6_.1), channel_id=1, source_target_pairs={{0,1},{1,0},{2,3},{3,2},{4,5},{5,4},{6,7},{7,6},{8,9},{9,8},{10,11... | collective-permute-start | bytes 1572872 | tf_op jit(solution)/shard_map/ppermute | solution.py:543
  4.6 3.2 %route.1 = f32[512,128]{1,0:T(8,128)} custom-call(s32[1]{0:T(128)} %bitcast.refs_0_.refs_2_, s32[1]{0:T(128)S(6)} %copy.15.refs_1_, f32[16,32]{1,0:T(8,128)} %refs_2_.3, f32[1024,128]{1,0:T(8,128)} %bitcast.29, s32[1,1024]{1,0:T(1,128)} %refs_4_.2), custom_call_target="tpu_custom_call" | custom-call | flops 1000000000 | bytes 1000000 | tf_op jit(solution)/shard_map/route/pallas_call | solution.py:595
  7.9 0.0 collective-permute-done
  7.9 28.2 %all_to_all.16 = f32[128,4,128]{2,1,0:T(4,128)S(1)} all-to-all(f32[128,4,128]{2,1,0:T(4,128)} %bitcast.28), channel_id=1, replica_groups=mesh['gx'=16,'gy'=8,'gz'=2] {'gx','gy'}, dimensions={0} | all-to-all | bytes 524288 | tf_op jit(solution)/shard_map/all_to_all | solution.py:619
  36.1 1.6 %collective-permute-start.1 = (f32[512,128]{1,0:T(8,128)S(1)}, f32[512,128]{1,0:T(8,128)S(1)}, u32[]{:S(2)}, u32[]{:S(2)}) collective-permute-start(f32[512,128]{1,0:T(8,128)S(1)} %bitcast.23), channel_id=1, source_target_pairs={{0,1},{1,0},{2,3},{3,2},{4,5},{5,4},{6,7},{7,6},{8,9},{9,8},{10,11... | collective-permute-start | bytes 786440 | tf_op jit(solution)/shard_map/ppermute | solution.py:543
  37.7 1.2 %collective-permute-done.1.refs_2_ = f32[512,128]{1,0:T(8,128)S(1)} collective-permute-done((f32[512,128]{1,0:T(8,128)S(1)}, f32[512,128]{1,0:T(8,128)S(1)}, u32[]{:S(2)}, u32[]{:S(2)}) %collective-permute-start.1) | collective-permute-done | bytes 262176 | tf_op jit(solution)/shard_map/ppermute | solution.py:543
  38.8 0.0 copy-done
  38.8 0.0 copy-done.2
  38.8 0.0 copy-done.1
  38.9 0.9 table.1
  39.8 1.3 %collective-permute-start.2 = (f32[56,128]{1,0:T(8,128)S(1)}, f32[56,128]{1,0:T(8,128)S(1)}, u32[]{:S(2)}, u32[]{:S(2)}) collective-permute-start(f32[56,128]{1,0:T(8,128)S(1)} %get-tuple-element.57), channel_id=1, source_target_pairs={{2,0},{4,2},{6,4},{8,6},{10,8},{12,10},{14,12},{3,1},{5,3},{7,5},{... | collective-permute-start | bytes 86024 | tf_op jit(solution)/shard_map/ppermute | solution.py:538
  41.1 4.0 %collective-permute-start.3 = (f32[56,128]{1,0:T(8,128)S(1)}, f32[56,128]{1,0:T(8,128)S(1)}, u32[]{:S(2)}, u32[]{:S(2)}) collective-permute-start(f32[56,128]{1,0:T(8,128)S(1)} %get-tuple-element.58), channel_id=1, source_target_pairs={{0,2},{2,4},{4,6},{6,8},{8,10},{10,12},{12,14},{1,3},{3,5},{5,7},{... | collective-permute-start | bytes 86024 | tf_op jit(solution)/shard_map/ppermute | solution.py:538
  45.1 1.9 %edge.1 = (f32[2,8,40,128]{3,2,1,0:T(8,128)S(1)}, f32[2,1,40,128]{3,2,1,0:T(8,128)S(1)}, f32[248,256]{1,0:T(8,128)S(1)}, f32[248,256]{1,0:T(8,128)S(1)}) custom-call(s32[1]{0:T(128)} %bitcast.refs_0_.refs_2_, bf16[160,512]{1,0:T(8,128)(2,1)S(1)} %get-tuple-element.60.refs_1_.refs_0_, s32[4,32,256]{2,1,0:T(8,128)S(1)} %copy-done.1, ...), custom_call_target="tpu_custom_call" | custom-call | flops 3000000000 | bytes 2500000 | tf_op jit(solution)/shard_map/edge/pallas_call | solution.py:595
  47.0 0.0 collective-permute-done.2.refs_8_
  47.0 0.0 collective-permute-done.3.refs_9_
  47.1 1.3 %collective-permute-start.4 = (f32[248,256]{1,0:T(8,128)S(1)}, f32[248,256]{1,0:T(8,128)S(1)}, u32[]{:S(2)}, u32[]{:S(2)}) collective-permute-start(f32[248,256]{1,0:T(8,128)S(1)} %get-tuple-element.61), channel_id=1, source_target_pairs={{16,0},{32,16},{48,32},{64,48},{80,64},{96,80},{112,96},{128,112},... | collective-permute-start | bytes 761864 | tf_op jit(solution)/shard_map/ppermute | solution.py:538
  48.4 4.2 %collective-permute-start.5 = (f32[248,256]{1,0:T(8,128)S(1)}, f32[248,256]{1,0:T(8,128)S(1)}, u32[]{:S(2)}, u32[]{:S(2)}) collective-permute-start(f32[248,256]{1,0:T(8,128)S(1)} %get-tuple-element.62), channel_id=1, source_target_pairs={{0,16},{16,32},{32,48},{48,64},{64,80},{80,96},{96,112},{112,128},... | collective-permute-start | bytes 761864 | tf_op jit(solution)/shard_map/ppermute | solution.py:538
  52.6 4.1 %middle.1.refs_5_ = f32[2,23,40,128]{3,2,1,0:T(8,128)S(1)} custom-call(bf16[160,512]{1,0:T(8,128)(2,1)S(1)} %get-tuple-element.60.refs_1_.refs_0_, s32[4,32,256]{2,1,0:T(8,128)S(1)} %copy-done.1, f32[4,32,256]{2,1,0:T(8,128)S(1)} %copy-done.2), custom_call_target="tpu_custom_call" | custom-call | flops 3000000000 | bytes 1600000 | tf_op jit(solution)/shard_map/middle/pallas_call | solution.py:595
  56.7 0.0 collective-permute-done.4.refs_10_
  56.7 0.0 collective-permute-done.5.refs_11_
  56.7 4.7 %basis.1 = (f32[3,17,40,384]{3,2,1,0:T(8,128)S(1)}, f32[256,128]{1,0:T(8,128)S(1)}) custom-call(s32[1]{0:T(128)} %bitcast.3.refs_0_, s32[1]{0:T(128)} %bitcast.4.refs_1_, s32[1]{0:T(128)} %bitcast.refs_0_.refs_2_, f32[2,8,40,128]{3,2,1,0:T(8,128)S(1)} %get-tuple-element.54.refs_3_, f32[2,1,40,128]{3,2,1,0:T(8,128)S(1)} %get-tuple-element.55.refs_4_, ...), custom_call_target="tpu_custom_call" | custom-call | tf_op jit(solution)/shard_map/basis/pallas_call | solution.py:595
  61.4 0.0 copy-start.3
  61.4 25.4 %all_to_all.17 = f32[256,1,128]{2,1,0:T(1,128)S(1)} all-to-all(f32[256,1,128]{2,1,0:T(1,128)S(1)} %bitcast.27), channel_id=1, replica_groups=mesh['gx'=16,'gy'=8,'gz'=2] {'gx','gy','gz'}, dimensions={0} | all-to-all | bytes 262144 | tf_op jit(solution)/shard_map/all_to_all | solution.py:688
  86.8 2.3 %wind.1 = (f32[16,32,256]{2,1,0:T(8,128)}, f32[3,16,32,256]{3,2,1,0:T(8,128)}, f32[32,256]{1,0:T(8,128)S(1)}, f32[32,256]{1,0:T(8,128)S(1)}) custom-call(s32[1]{0:T(128)} %bitcast.refs_0_.refs_2_, f32[256,128]{1,0:T(8,128)S(1)} %bitcast.25, f32[3,17,40,384]{3,2,1,0:T(8,128)S(1)} %get-tuple-element.64.refs_2_, f32[2,320,128]{2,1,0:T(8,128)S(1)} %bitcast.22, ...), custom_call_target="tpu_custom_call" | custom-call | tf_op jit(solution)/shard_map/wind/pallas_call | solution.py:595
  89.1 0.9 collective-permute-start.6
  89.9 0.9 collective-permute-done.6.refs_1_
  90.8 0.0 copy-done.3
  90.8 0.7 fuel.1
  (3 shorter events, 0.0 us)
Async XLA Ops:
  0.6 38.2 %copy-start = (s32[16,32,256]{2,1,0:T(8,128)S(1)}, s32[16,32,256]{2,1,0:T(8,128)}, u32[]{:S(2)}) copy-start(s32[16,32,256]{2,1,0:T(8,128)} %refs_6_.1) | copy-start | bytes 1572868
  0.6 38.2 %copy-start.2 = (f32[4,32,256]{2,1,0:T(8,128)S(1)}, f32[4,32,256]{2,1,0:T(8,128)}, u32[]{:S(2)}) copy-start(f32[4,32,256]{2,1,0:T(8,128)} %refs_2_.5) | copy-start | bytes 393220
  0.7 38.2 %copy-start.1 = (s32[4,32,256]{2,1,0:T(8,128)S(1)}, s32[4,32,256]{2,1,0:T(8,128)}, u32[]{:S(2)}) copy-start(s32[4,32,256]{2,1,0:T(8,128)} %refs_1_.2) | copy-start | bytes 393220
  0.7 7.2 %collective-permute-start = (s32[16,32,256]{2,1,0:T(8,128)}, s32[16,32,256]{2,1,0:T(8,128)S(1)}, u32[]{:S(2)}, u32[]{:S(2)}) collective-permute-start(s32[16,32,256]{2,1,0:T(8,128)} %refs_6_.1), channel_id=1, source_target_pairs={{0,1},{1,0},{2,3},{3,2},{4,5},{5,4},{6,7},{7,6},{8,9},{9,8},{10,11... | collective-permute-start | bytes 1572872 | tf_op jit(solution)/shard_map/ppermute | solution.py:543
  36.1 2.8 %collective-permute-start.1 = (f32[512,128]{1,0:T(8,128)S(1)}, f32[512,128]{1,0:T(8,128)S(1)}, u32[]{:S(2)}, u32[]{:S(2)}) collective-permute-start(f32[512,128]{1,0:T(8,128)S(1)} %bitcast.23), channel_id=1, source_target_pairs={{0,1},{1,0},{2,3},{3,2},{4,5},{5,4},{6,7},{7,6},{8,9},{9,8},{10,11... | collective-permute-start | bytes 786440 | tf_op jit(solution)/shard_map/ppermute | solution.py:543
  39.8 7.2 %collective-permute-start.2 = (f32[56,128]{1,0:T(8,128)S(1)}, f32[56,128]{1,0:T(8,128)S(1)}, u32[]{:S(2)}, u32[]{:S(2)}) collective-permute-start(f32[56,128]{1,0:T(8,128)S(1)} %get-tuple-element.57), channel_id=1, source_target_pairs={{2,0},{4,2},{6,4},{8,6},{10,8},{12,10},{14,12},{3,1},{5,3},{7,5},{... | collective-permute-start | bytes 86024 | tf_op jit(solution)/shard_map/ppermute | solution.py:538
  41.1 6.0 %collective-permute-start.3 = (f32[56,128]{1,0:T(8,128)S(1)}, f32[56,128]{1,0:T(8,128)S(1)}, u32[]{:S(2)}, u32[]{:S(2)}) collective-permute-start(f32[56,128]{1,0:T(8,128)S(1)} %get-tuple-element.58), channel_id=1, source_target_pairs={{0,2},{2,4},{4,6},{6,8},{8,10},{10,12},{12,14},{1,3},{3,5},{5,7},{... | collective-permute-start | bytes 86024 | tf_op jit(solution)/shard_map/ppermute | solution.py:538
  47.1 9.6 %collective-permute-start.4 = (f32[248,256]{1,0:T(8,128)S(1)}, f32[248,256]{1,0:T(8,128)S(1)}, u32[]{:S(2)}, u32[]{:S(2)}) collective-permute-start(f32[248,256]{1,0:T(8,128)S(1)} %get-tuple-element.61), channel_id=1, source_target_pairs={{16,0},{32,16},{48,32},{64,48},{80,64},{96,80},{112,96},{128,112},... | collective-permute-start | bytes 761864 | tf_op jit(solution)/shard_map/ppermute | solution.py:538
  48.4 8.3 %collective-permute-start.5 = (f32[248,256]{1,0:T(8,128)S(1)}, f32[248,256]{1,0:T(8,128)S(1)}, u32[]{:S(2)}, u32[]{:S(2)}) collective-permute-start(f32[248,256]{1,0:T(8,128)S(1)} %get-tuple-element.62), channel_id=1, source_target_pairs={{0,16},{16,32},{32,48},{48,64},{64,80},{80,96},{96,112},{112,128},... | collective-permute-start | bytes 761864 | tf_op jit(solution)/shard_map/ppermute | solution.py:538
  61.4 29.4 %copy-start.3 = (f32[3,32,256]{2,1,0:T(8,128)S(1)}, f32[3,32,256]{2,1,0:T(8,128)}, u32[]{:S(2)}) copy-start(f32[3,32,256]{2,1,0:T(8,128)} %refs_3_.5) | copy-start | bytes 294916
  89.1 1.7 %collective-permute-start.6 = (f32[32,256]{1,0:T(8,128)S(1)}, f32[32,256]{1,0:T(8,128)S(1)}, u32[]{:S(2)}, u32[]{:S(2)}) collective-permute-start(f32[32,256]{1,0:T(8,128)S(1)} %get-tuple-element.67.refs_0_), channel_id=1, source_target_pairs={{0,1},{1,0},{2,3},{3,2},{4,5},{5,4},{6,7},{7,6},{8,9},{9,8},{10,11... | collective-permute-start | bytes 98312 | tf_op jit(solution)/shard_map/ppermute | solution.py:543
